TPU v7x, 128 devices: a whole 4x4x4 slice. The times are simulated.
128 devices in a mesh: hi: 4 (over z_hi, core), lo: 32 (over y, z_lo, x).
Axes of the slice: x: 4, y: 4, z: 4 (z_hi: 2, z_lo: 2; z = z_hi * 2 + z_lo), core: 2. Of those that a mesh axis runs over, the one named last changes fastest.
Arguments:
- sources: bfloat16 [2, 256, 1048576], P(None, None, ('hi', 'lo')), may hold values from -6 to 6
- source_map: bfloat16 [64, 256], replicated, may hold values from -0.375 to 0.375
- translation: bfloat16 [15, 2, 64, 128], replicated, may hold values from -0.5 to 0.5
- box_gain: float32 [15, 1048576], P(None, ('hi', 'lo')), may hold values from 0.5 to 1.5
- target_order: int32 [128, 8192], P(('hi', 'lo')), may hold values from 0 to 8191, each once within a row
- target_map: bfloat16 [256, 64], replicated, may hold values from -0.75 to 0.75
Outputs:
- field: bfloat16 [2, 256, 1048576], P(None, None, ('hi', 'lo'))
Inputs may be any that keep to these rules, and one draw needn't show every extreme that they name: Each row of target_order holds every number of 0 to 8191 once.
All inputs are finite; a program needn't handle non-finite values.
Results may differ from a plain program's by a relative error of at most 0.03.
Values may be sent and summed in bfloat16 or wider, within the bound.
No kernel may reach another device: no remote copies, remote signals or barrier semaphores. Data moves between devices by JAX's collectives and lax.ppermute only.
A program may use at most 128 MiB of HBM per device.

v0:
```python
import functools

import jax
import jax.numpy as jnp
from jax import lax
from jax.experimental import pallas as pl
from jax.experimental.pallas import tpu as pltpu
from jax.sharding import PartitionSpec as P

LOCAL_LEVELS = 8
F32 = jnp.float32
BF16 = jnp.bfloat16
VMEM_LIMIT = 48 * 2**20


def dot(a, b):
    return jnp.dot(a, b, preferred_element_type=F32)


def pick(own, kept, received):
    first = own == 0
    return jnp.where(first, kept, received), jnp.where(first, received, kept)


def pair(matrix, low, high, gains):
    ranks = low.shape[0]
    product = dot(matrix, jnp.concatenate([low, high], axis=0))
    return (
        (product[:ranks] * gains[0]).astype(BF16),
        (product[ranks:] * gains[1]).astype(BF16),
    )


def front_kernel(levels, own_ref, low_ref, high_ref, map_ref, tr_ref, gl_ref, gh_ref, kept_ref, sent_ref):
    own = own_ref[0]
    images = low_ref.shape[0]
    source_map = map_ref[...]
    for c in range(images):
        low = dot(source_map, low_ref[c]).astype(BF16)
        high = dot(source_map, high_ref[c]).astype(BF16)
        for level in range(levels):
            gains = gl_ref[level : level + 1, :], gh_ref[level : level + 1, :]
            low, high = pair(tr_ref[level], low, high, gains)
        kept_ref[c], sent_ref[c] = pick(own, low, high)


def front(own, sources, source_map, matrices, box_gain, cols):
    images, points, boxes = sources.shape
    ranks = source_map.shape[0]
    half = boxes // 2
    steps = half // cols
    levels = matrices.shape[0]
    grid_spec = pltpu.PrefetchScalarGridSpec(
        num_scalar_prefetch=1,
        grid=(steps,),
        in_specs=[
            pl.BlockSpec((images, points, cols), lambda i, s: (0, 0, i)),
            pl.BlockSpec((images, points, cols), lambda i, s: (0, 0, i + steps)),
            pl.BlockSpec((ranks, points), lambda i, s: (0, 0)),
            pl.BlockSpec(matrices.shape, lambda i, s: (0, 0, 0)),
            pl.BlockSpec((box_gain.shape[0], cols), lambda i, s: (0, i)),
            pl.BlockSpec((box_gain.shape[0], cols), lambda i, s: (0, i + steps)),
        ],
        out_specs=[pl.BlockSpec((images, ranks, cols), lambda i, s: (0, 0, i))] * 2,
    )
    return pl.pallas_call(
        functools.partial(front_kernel, LOCAL_LEVELS),
        grid_spec=grid_spec,
        out_shape=[jax.ShapeDtypeStruct((images, ranks, half), BF16)] * 2,
        compiler_params=pltpu.CompilerParams(vmem_limit_bytes=VMEM_LIMIT),
        name="source_map_and_local_levels",
    )(own, sources, sources, source_map, matrices, box_gain, box_gain)


def swap_kernel(level, own_ref, kept_in, recv_in, tr_ref, gl_ref, gh_ref, kept_ref, sent_ref):
    images = kept_in.shape[0]
    gains = gl_ref[level : level + 1, :], gh_ref[level : level + 1, :]
    for c in range(images):
        low, high = pick(own_ref[0], kept_in[c], recv_in[c])
        low, high = pair(tr_ref[level], low, high, gains)
        kept_ref[c], sent_ref[c] = pick(own_ref[1], low, high)


def swap_level(level, owns, kept, received, matrices, box_gain, cols):
    images, ranks, half = kept.shape
    steps = half // cols
    block = pl.BlockSpec((images, ranks, cols), lambda i, s: (0, 0, i))
    grid_spec = pltpu.PrefetchScalarGridSpec(
        num_scalar_prefetch=1,
        grid=(steps,),
        in_specs=[
            block,
            block,
            pl.BlockSpec(matrices.shape, lambda i, s: (0, 0, 0)),
            pl.BlockSpec((box_gain.shape[0], cols), lambda i, s: (0, i)),
            pl.BlockSpec((box_gain.shape[0], cols), lambda i, s: (0, i + steps)),
        ],
        out_specs=[block] * 2,
    )
    return pl.pallas_call(
        functools.partial(swap_kernel, level),
        grid_spec=grid_spec,
        out_shape=[jax.ShapeDtypeStruct(kept.shape, BF16)] * 2,
        compiler_params=pltpu.CompilerParams(vmem_limit_bytes=VMEM_LIMIT),
        name="upper_level",
    )(owns, kept, received, matrices, box_gain, box_gain)


def rows_kernel(level, own_ref, kept_in, recv_in, tr_ref, gl_ref, gh_ref, out_ref):
    images = kept_in.shape[0]
    gains = gl_ref[level : level + 1, :], gh_ref[level : level + 1, :]
    lows, highs = [], []
    for c in range(images):
        low, high = pick(own_ref[0], kept_in[c], recv_in[c])
        low, high = pair(tr_ref[level], low, high, gains)
        lows.append(low)
        highs.append(high)
    piece = out_ref.shape[2]
    for n, parts in enumerate((lows, highs)):
        stacked = jnp.concatenate(parts, axis=0).astype(F32)
        for k in range(out_ref.shape[1]):
            out_ref[n, k] = stacked[:, k * piece : (k + 1) * piece].T.astype(BF16)


def rows_level(level, owns, kept, received, matrices, box_gain, cols, pieces):
    images, ranks, half = kept.shape
    steps = half // cols
    piece = 2 * half // pieces
    block = pl.BlockSpec((images, ranks, cols), lambda i, s: (0, 0, i))
    grid_spec = pltpu.PrefetchScalarGridSpec(
        num_scalar_prefetch=1,
        grid=(steps,),
        in_specs=[
            block,
            block,
            pl.BlockSpec(matrices.shape, lambda i, s: (0, 0, 0)),
            pl.BlockSpec((box_gain.shape[0], cols), lambda i, s: (0, i)),
            pl.BlockSpec((box_gain.shape[0], cols), lambda i, s: (0, i + steps)),
        ],
        out_specs=pl.BlockSpec((2, cols // piece, piece, images * ranks), lambda i, s: (0, i, 0, 0)),
    )
    out = pl.pallas_call(
        functools.partial(rows_kernel, level),
        grid_spec=grid_spec,
        out_shape=jax.ShapeDtypeStruct((2, pieces // 2, piece, images * ranks), BF16),
        compiler_params=pltpu.CompilerParams(vmem_limit_bytes=VMEM_LIMIT),
        name="upper_level_to_rows",
    )(owns, kept, received, matrices, box_gain, box_gain)
    return out.reshape(pieces, piece, images * ranks)


UNROLL = 32


def gather_kernel(order_ref, rows_ref, out_ref, table, picked):
    boxes = table.shape[0]
    chunk = 256

    def widen(i, carry):
        at = pl.ds(pl.multiple_of(i * chunk, chunk), chunk)
        table[at, :] = rows_ref[at, :].astype(F32)
        return carry

    lax.fori_loop(0, boxes // chunk, widen, 0)

    def move(i, carry):
        base = pl.multiple_of(i * UNROLL, UNROLL)
        for k in range(UNROLL):
            picked[pl.ds(base + k, 1), :] = table[pl.ds(order_ref[0, base + k], 1), :]
        return carry

    lax.fori_loop(0, boxes // UNROLL, move, 0)

    def narrow(i, carry):
        at = pl.ds(pl.multiple_of(i * chunk, chunk), chunk)
        out_ref[at, :] = picked[at, :].astype(BF16)
        return carry

    lax.fori_loop(0, boxes // chunk, narrow, 0)


def gather_rows(order, rows):
    boxes, width = rows.shape
    return pl.pallas_call(
        gather_kernel,
        in_specs=[
            pl.BlockSpec(memory_space=pltpu.SMEM),
            pl.BlockSpec(memory_space=pltpu.VMEM),
        ],
        out_specs=pl.BlockSpec(memory_space=pltpu.VMEM),
        out_shape=jax.ShapeDtypeStruct((boxes, width), BF16),
        scratch_shapes=[pltpu.VMEM((boxes, width), F32), pltpu.VMEM((boxes, width), F32)],
        compiler_params=pltpu.CompilerParams(vmem_limit_bytes=VMEM_LIMIT),
        name="box_order",
    )(order, rows)


def lower_kernel(levels, first, x_ref, tr_ref, gain_ref, out_ref, held):
    devices, cols, _ = x_ref.shape
    images, ranks = out_ref.shape[1], out_ref.shape[2]
    for i in range(levels):
        bit = levels - 1 - i
        matrix = tr_ref[first + i]
        if i == 0:
            blank = jnp.zeros((2 * ranks, ranks), BF16)
            sides = []
            for side in range(2):
                part = matrix[:, side * ranks : (side + 1) * ranks]
                bands = [
                    jnp.concatenate([part if c == b else blank for b in range(images)], axis=1)
                    for c in range(images)
                ]
                sides.append(jnp.concatenate(bands, axis=0))
            both = jnp.concatenate(sides, axis=1)
        target = out_ref if i == levels - 1 else held

        def group(g, carry):
            low_at = ((g >> bit) << (bit + 1)) | (g & ((1 << bit) - 1))
            high_at = low_at + (1 << bit)
            gains = gain_ref[g, 2 * i : 2 * i + 1, :], gain_ref[g, 2 * i + 1 : 2 * i + 2, :]
            if i == 0:
                stacked = jnp.concatenate([x_ref[low_at], x_ref[high_at]], axis=1)
                product = lax.dot_general(
                    both, stacked, (((1,), (1,)), ((), ())), preferred_element_type=F32
                )
            for c in range(images):
                if i == 0:
                    own = product[c * 2 * ranks : (c + 1) * 2 * ranks]
                else:
                    own = dot(matrix, jnp.concatenate([held[low_at, c], held[high_at, c]], axis=0))
                target[low_at, c] = (own[:ranks] * gains[0].astype(F32)).astype(BF16)
                target[high_at, c] = (own[ranks:] * gains[1].astype(F32)).astype(BF16)
            return carry

        lax.fori_loop(0, devices // 2, group, 0, unroll=2)


def lower_levels(x, matrices, gains, images, first):
    devices, cols, width = x.shape
    ranks = width // images
    levels = devices.bit_length() - 1
    shape = (devices, images, ranks, cols)
    return pl.pallas_call(
        functools.partial(lower_kernel, levels, first),
        in_specs=[pl.BlockSpec(memory_space=pltpu.VMEM)] * 3,
        out_specs=pl.BlockSpec(memory_space=pltpu.VMEM),
        out_shape=jax.ShapeDtypeStruct(shape, BF16),
        scratch_shapes=[pltpu.VMEM(shape, BF16)],
        compiler_params=pltpu.CompilerParams(vmem_limit_bytes=VMEM_LIMIT),
        name="lower_levels",
    )(x, matrices, gains)


def target_kernel(x_ref, map_ref, out_ref):
    pieces, _, images, ranks, cols = x_ref.shape
    target_map = map_ref[...]
    for k in range(pieces):
        for c in range(images):
            out_ref[c, :, k * cols : (k + 1) * cols] = dot(target_map, x_ref[k, 0, c]).astype(BF16)


def to_targets(x, target_map, pieces):
    t_pieces, two, images, ranks, cols = x.shape
    points = target_map.shape[0]
    per_half = t_pieces // pieces
    return pl.pallas_call(
        target_kernel,
        grid=(two, per_half),
        in_specs=[
            pl.BlockSpec((pieces, 1, images, ranks, cols), lambda n, i: (i, n, 0, 0, 0)),
            pl.BlockSpec((points, ranks), lambda n, i: (0, 0)),
        ],
        out_specs=pl.BlockSpec((images, points, pieces * cols), lambda n, i: (0, 0, n * per_half + i)),
        out_shape=jax.ShapeDtypeStruct((images, points, two * t_pieces * cols), BF16),
        compiler_params=pltpu.CompilerParams(vmem_limit_bytes=VMEM_LIMIT),
        name="target_map",
    )(x, target_map)


def body(sources, source_map, translation, box_gain, target_order, target_map):
    images, _, boxes = sources.shape
    ranks = source_map.shape[0]
    n_lower = lax.axis_size("lo")
    matrices = translation.reshape(translation.shape[0], 2 * ranks, 2 * ranks)
    upper = lax.axis_index("hi")
    owns = jnp.stack([upper >> 1 & 1, upper & 1]).astype(jnp.int32)
    first_lower = LOCAL_LEVELS + 2
    levels_lo = n_lower.bit_length() - 1
    piece = boxes // n_lower
    halves = n_lower // 2

    gains = box_gain[first_lower:].astype(BF16).reshape(levels_lo, 2, halves, piece)
    gains = gains.transpose(2, 0, 1, 3).reshape(halves, 2 * levels_lo, piece)
    groups = [list(range(halves)), list(range(halves, n_lower))]
    gains = lax.all_to_all(gains, "lo", 0, 0, axis_index_groups=groups)

    kept, sent = front(owns[:1], sources, source_map, matrices, box_gain, 512)
    received = lax.ppermute(sent, "hi", [(i, i ^ 2) for i in range(4)])
    kept, sent = swap_level(LOCAL_LEVELS, owns, kept, received, matrices, box_gain, 2048)
    received = lax.ppermute(sent, "hi", [(i, i ^ 1) for i in range(4)])
    rows = rows_level(LOCAL_LEVELS + 1, owns[1:], kept, received, matrices, box_gain, 1024, n_lower)
    rows = lax.all_to_all(rows, "lo", 0, 0)
    rows = gather_rows(target_order, rows.reshape(boxes, images * ranks))
    rows = lax.all_to_all(rows.reshape(n_lower, piece, images * ranks), "lo", 0, 0)
    blocks = lower_levels(rows, matrices, gains, images, first_lower)
    blocks = blocks.reshape(halves, 2, images, ranks, piece)
    blocks = lax.all_to_all(blocks, "lo", 0, 0, axis_index_groups=groups)
    return to_targets(blocks, target_map, 4)


def solution(mesh):
    return jax.shard_map(
        body,
        mesh=mesh,
        in_specs=(
            P(None, None, ("hi", "lo")),
            P(),
            P(),
            P(None, ("hi", "lo")),
            P(("hi", "lo"), None),
            P(),
        ),
        out_specs=P(None, None, ("hi", "lo")),
        check_vma=False,
    )
```

profile of v0, /device:TPU:1, one launch (start us, length us, event | category | flops | bytes accessed | tf_op | source)
XLA Modules:
  0.0 197.6 jit_solution(18032166029756675994)
XLA Ops:
  0.0 0.0 copy-start
  0.0 1.0 copy-done
  1.0 1.0 copy-done.4
  2.1 0.8 copy-done.6
  2.8 24.8 %source_map_and_local_levels.1 = (bf16[2,64,4096]{2,1,0:T(8,128)(2,1)S(1)}, bf16[2,64,4096]{2,1,0:T(8,128)(2,1)}) custom-call(s32[1]{0:T(128)} %bitcast.1.own_ref, bf16[2,256,8192]{2,1,0:T(8,128)(2,1)} %high_ref.1, bf16[2,256,8192]{2,1,0:T(8,128)(2,1)} %high_ref.1, bf16[64,256]{1,0:T(8,128)(2,1)S(1)} %copy-done.6, bf16[15,128,128]{2,1,0:T(8,128)(2,1)S(1)} %bitcast.17, ...), custom_call_target="tpu_custom_call" | custom-call | tf_op jit(solution)/shard_map/source_map_and_local_levels/pallas_call | solution.py:66
  27.6 4.4 %collective-permute-start = (bf16[2,64,4096]{2,1,0:T(8,128)(2,1)}, bf16[2,64,4096]{2,1,0:T(8,128)(2,1)S(1)}, u32[]{:S(2)}, u32[]{:S(2)}) collective-permute-start(bf16[2,64,4096]{2,1,0:T(8,128)(2,1)} %get-tuple-element.10), channel_id=1, source_target_pairs={{0,64},{32,96},{64,0},{96,32},{1,65},{33,97},{65,1},{97,33},{2,66}... | collective-permute-start | bytes 3145736 | tf_op jit(solution)/shard_map/ppermute | solution.py:298
  32.1 0.1 pad_add_fusion.own_ref
  32.1 23.0 %collective-permute-done.recv_in = bf16[2,64,4096]{2,1,0:T(8,128)(2,1)S(1)} collective-permute-done((bf16[2,64,4096]{2,1,0:T(8,128)(2,1)}, bf16[2,64,4096]{2,1,0:T(8,128)(2,1)S(1)}, u32[]{:S(2)}, u32[]{:S(2)}) %collective-permute-start) | collective-permute-done | bytes 1048608 | tf_op jit(solution)/shard_map/ppermute | solution.py:298
  55.1 0.0 copy-done.1
  55.1 0.0 copy-done.5
  55.2 1.8 upper_level.1
  57.0 1.3 collective-permute-start.1
  58.3 2.3 %collective-permute-done.1.recv_in = bf16[2,64,4096]{2,1,0:T(8,128)(2,1)S(1)} collective-permute-done((bf16[2,64,4096]{2,1,0:T(8,128)(2,1)S(1)}, bf16[2,64,4096]{2,1,0:T(8,128)(2,1)S(1)}, u32[]{:S(2)}, u32[]{:S(2)}) %collective-permute-start.1) | collective-permute-done | bytes 1048608 | tf_op jit(solution)/shard_map/ppermute | solution.py:300
  60.6 3.0 %upper_level_to_rows.1 = bf16[2,16,256,128]{3,2,1,0:T(8,128)(2,1)} custom-call(s32[1]{0:T(128)} %bitcast.own_ref, bf16[2,64,4096]{2,1,0:T(8,128)(2,1)S(1)} %get-tuple-element.11.kept_in, bf16[2,64,4096]{2,1,0:T(8,128)(2,1)S(1)} %collective-permute-done.1.recv_in, bf16[15,128,128]{2,1,0:T(8,128)(2,1)S(1)} %bitcast.19, f32[15,8192]{1,0:T(8,128)S(1)} %copy-done.1, ...), custom_call_target="tpu_custom_call" | custom-call | tf_op jit(solution)/shard_map/upper_level_to_rows/pallas_call | solution.py:142
  63.6 7.9 %all-to-all-start = ((bf16[32,256,128]{2,1,0:T(8,128)(2,1)}), bf16[32,256,128]{2,1,0:T(8,128)(2,1)S(1)}, u32[]{:S(2)}, u32[]{:S(2)}) async-start(bf16[32,256,128]{2,1,0:T(8,128)(2,1)} %bitcast.3), calls=%async_computation | async-start | bytes 4194304 | tf_op jit(solution)/shard_map/all_to_all | solution.py:302
  71.6 0.7 copy.9
  72.3 26.2 %all-to-all-done = bf16[32,256,128]{2,1,0:T(8,128)(2,1)S(1)} async-done(((bf16[32,256,128]{2,1,0:T(8,128)(2,1)}), bf16[32,256,128]{2,1,0:T(8,128)(2,1)S(1)}, u32[]{:S(2)}, u32[]{:S(2)}) %all-to-all-start) | async-done | bytes 2097184 | tf_op jit(solution)/shard_map/all_to_all | solution.py:302
  98.5 5.5 %all-to-all-start.2 = ((bf16[16,10,256]{2,1,0:T(8,128)(2,1)}), bf16[16,10,256]{2,1,0:T(8,128)(2,1)S(1)}, u32[]{:S(2)}, u32[]{:S(2)}) async-start(bf16[16,10,256]{2,1,0:T(8,128)(2,1)} %copy.9), calls=%async_computation.2 | async-start | bytes 262144 | tf_op jit(solution)/shard_map/all_to_all | solution.py:295
  104.0 0.0 copy-done.7
  104.0 9.5 %box_order.1 = bf16[8192,128]{1,0:T(8,128)(2,1)S(1)} custom-call(s32[1,8192]{1,0:T(1,128)S(1)} %copy-done.7, bf16[8192,128]{1,0:T(8,128)(2,1)S(1)} %bitcast.15), custom_call_target="tpu_custom_call" | custom-call | tf_op jit(solution)/shard_map/box_order/pallas_call | solution.py:184
  113.5 0.0 copy-start.3
  113.5 1.3 copy-done.3
  114.8 0.0 all-to-all-done.2.gain_ref
  114.8 33.2 %all_to_all.20.x_ref = bf16[32,256,128]{2,1,0:T(8,128)(2,1)S(1)} all-to-all(bf16[32,256,128]{2,1,0:T(8,128)(2,1)} %bitcast.16), channel_id=1, replica_groups=mesh['hi'=4,'lo'=32] {'lo'}, dimensions={0} | all-to-all | bytes 4194304 | tf_op jit(solution)/shard_map/all_to_all | solution.py:304
  148.0 12.5 %lower_levels.1 = bf16[32,2,64,256]{3,2,1,0:T(8,128)(2,1)S(1)} custom-call(bf16[32,256,128]{2,1,0:T(8,128)(2,1)S(1)} %all_to_all.20.x_ref, bf16[15,128,128]{2,1,0:T(8,128)(2,1)S(1)} %bitcast.20, bf16[16,10,256]{2,1,0:T(8,128)(2,1)S(1)} %all-to-all-done.2.gain_ref), custom_call_target="tpu_custom_call" | custom-call | tf_op jit(solution)/shard_map/lower_levels/pallas_call | solution.py:243
  160.6 0.0 copy-start.2
  160.6 1.3 copy-done.2
  161.9 4.4 %all-to-all-start.3 = ((bf16[16,2,2,64,256]{4,3,2,1,0:T(8,128)(2,1)}), bf16[16,2,2,64,256]{4,3,2,1,0:T(8,128)(2,1)S(1)}, u32[]{:S(2)}, u32[]{:S(2)}) async-start(bf16[16,2,2,64,256]{4,3,2,1,0:T(8,128)(2,1)} %bitcast.14), calls=%async_computation.3 | async-start | bytes 4194304 | tf_op jit(solution)/shard_map/all_to_all | solution.py:307
  166.3 0.0 copy-done.8
  166.3 0.1 copy.10.map_ref
  166.4 25.1 %all-to-all-done.3.x_ref = bf16[16,2,2,64,256]{4,3,2,1,0:T(8,128)(2,1)S(1)} async-done(((bf16[16,2,2,64,256]{4,3,2,1,0:T(8,128)(2,1)}), bf16[16,2,2,64,256]{4,3,2,1,0:T(8,128)(2,1)S(1)}, u32[]{:S(2)}, u32[]{:S(2)}) %all-to-all-start.3) | async-done | bytes 2097184 | tf_op jit(solution)/shard_map/all_to_all | solution.py:307
  191.5 6.1 %target_map.1 = bf16[2,256,8192]{2,1,0:T(8,128)(2,1)} custom-call(bf16[16,2,2,64,256]{4,3,2,1,0:T(8,128)(2,1)S(1)} %all-to-all-done.3.x_ref, bf16[256,64]{1,0:T(8,128)(2,1)S(1)} %copy.10.map_ref), custom_call_target="tpu_custom_call" | custom-call | tf_op jit(solution)/shard_map/target_map/pallas_call | solution.py:266
  (8 shorter events, 0.1 us)
Async XLA Ops:
  0.0 1.0 copy-start
  1.0 1.0 copy-start.4
  2.1 0.8 copy-start.6
  2.8 52.3 %copy-start.1 = (f32[15,8192]{1,0:T(8,128)S(1)}, f32[15,8192]{1,0:T(8,128)}, u32[]{:S(2)}) copy-start(f32[15,8192]{1,0:T(8,128)} %gh_ref.5) | copy-start | bytes 1474564
  2.8 52.3 %copy-start.5 = (bf16[15,2,64,128]{3,2,1,0:T(8,128)(2,1)S(1)}, bf16[15,2,64,128]{3,2,1,0:T(8,128)(2,1)}, u32[]{:S(2)}) copy-start(bf16[15,2,64,128]{3,2,1,0:T(8,128)(2,1)} %param.8) | copy-start | bytes 1474564
  27.6 27.5 %collective-permute-start = (bf16[2,64,4096]{2,1,0:T(8,128)(2,1)}, bf16[2,64,4096]{2,1,0:T(8,128)(2,1)S(1)}, u32[]{:S(2)}, u32[]{:S(2)}) collective-permute-start(bf16[2,64,4096]{2,1,0:T(8,128)(2,1)} %get-tuple-element.10), channel_id=1, source_target_pairs={{0,64},{32,96},{64,0},{96,32},{1,65},{33,97},{65,1},{97,33},{2,66}... | collective-permute-start | bytes 3145736 | tf_op jit(solution)/shard_map/ppermute | solution.py:298
  57.0 3.6 %collective-permute-start.1 = (bf16[2,64,4096]{2,1,0:T(8,128)(2,1)S(1)}, bf16[2,64,4096]{2,1,0:T(8,128)(2,1)S(1)}, u32[]{:S(2)}, u32[]{:S(2)}) collective-permute-start(bf16[2,64,4096]{2,1,0:T(8,128)(2,1)S(1)} %get-tuple-element.12), channel_id=1, source_target_pairs={{0,32},{32,0},{64,96},{96,64},{1,33},{33,1},{65,97},{97,65},{2,34}... | collective-permute-start | bytes 3145736 | tf_op jit(solution)/shard_map/ppermute | solution.py:300
  63.6 40.4 %copy-start.7 = (s32[1,8192]{1,0:T(1,128)S(1)}, s32[1,8192]{1,0:T(1,128)}, u32[]{:S(2)}) copy-start(s32[1,8192]{1,0:T(1,128)} %order_ref.1) | copy-start | bytes 98308
  63.6 34.9 %all-to-all-start = ((bf16[32,256,128]{2,1,0:T(8,128)(2,1)}), bf16[32,256,128]{2,1,0:T(8,128)(2,1)S(1)}, u32[]{:S(2)}, u32[]{:S(2)}) async-start(bf16[32,256,128]{2,1,0:T(8,128)(2,1)} %bitcast.3), calls=%async_computation | async-start | bytes 4194304 | tf_op jit(solution)/shard_map/all_to_all | solution.py:302
  98.5 16.3 %all-to-all-start.2 = ((bf16[16,10,256]{2,1,0:T(8,128)(2,1)}), bf16[16,10,256]{2,1,0:T(8,128)(2,1)S(1)}, u32[]{:S(2)}, u32[]{:S(2)}) async-start(bf16[16,10,256]{2,1,0:T(8,128)(2,1)} %copy.9), calls=%async_computation.2 | async-start | bytes 262144 | tf_op jit(solution)/shard_map/all_to_all | solution.py:295
  113.5 1.3 copy-start.3
  160.6 1.3 copy-start.2
  161.9 4.4 %copy-start.8 = (bf16[256,64]{0,1:T(8,128)(2,1)S(1)}, bf16[256,64]{0,1:T(8,128)(2,1)}, u32[]{:S(2)}) copy-start(bf16[256,64]{0,1:T(8,128)(2,1)} %param.11) | copy-start | bytes 98308
  161.9 29.6 %all-to-all-start.3 = ((bf16[16,2,2,64,256]{4,3,2,1,0:T(8,128)(2,1)}), bf16[16,2,2,64,256]{4,3,2,1,0:T(8,128)(2,1)S(1)}, u32[]{:S(2)}, u32[]{:S(2)}) async-start(bf16[16,2,2,64,256]{4,3,2,1,0:T(8,128)(2,1)} %bitcast.14), calls=%async_computation.3 | async-start | bytes 4194304 | tf_op jit(solution)/shard_map/all_to_all | solution.py:307
where the time goes:
time: 201 us; the launch traced here: 198 us
  waiting for transfers between devices  76.7 us (38%)
  Pallas kernels  57.7 us (29%)
  blocking collectives  33.2 us (17%)
  starting transfers between devices  23.5 us (12%)
  local copies, waits for them, and re-layouts  6.33 us (3%)
    all_to_all x1, blocking collectives, body(): lax.all_to_all(rows.reshape(n_lower, piece, images * ranks), 'lo', 0, 0)  33.2 us
    all_to_all x1, waiting for transfers between devices, body(): rows = lax.all_to_all(rows, 'lo', 0, 0)  26.2 us
    all_to_all x1, waiting for transfers between devices, body(): blocks = lax.all_to_all(blocks, 'lo', 0, 0, axis_index_groups=groups)  25.1 us
    pallas_call x1, Pallas kernels, front(): pl.pallas_call(functools.partial(front_kernel, LOCAL_LEVELS), grid_spec=g...  24.8 us
    ppermute x1, waiting for transfers between devices, body(): received = lax.ppermute(sent, 'hi', [(i, i ^ 2) for i in range(4)])  23 us
    pallas_call x1, Pallas kernels, lower_levels(): pl.pallas_call(functools.partial(lower_kernel, levels, first), in_specs=[...  12.5 us
    pallas_call x1, Pallas kernels, gather_rows(): pl.pallas_call(gather_kernel, in_specs=[pl.BlockSpec(memory_space=pltpu.S...  9.48 us
    all_to_all x1, starting transfers between devices, body(): rows = lax.all_to_all(rows, 'lo', 0, 0)  7.9 us
  transfers between devices with their start and end apart: 5, of which 4 were waited for; matrix products, arithmetic and copies ran while one was open for 0% of the time, Pallas kernels for 5%

commit v1 on v0

v1 whole, which is shorter than its diff:
```python
import functools

import jax
import jax.numpy as jnp
from jax import lax
from jax.experimental import pallas as pl
from jax.experimental.pallas import tpu as pltpu
from jax.sharding import PartitionSpec as P

LOCAL_LEVELS = 8
F32 = jnp.float32
BF16 = jnp.bfloat16
VMEM_LIMIT = 40 * 2**20


def dot(a, b):
    return jnp.dot(a, b, preferred_element_type=F32)


def params(limit=VMEM_LIMIT):
    return pltpu.CompilerParams(vmem_limit_bytes=limit)


def cost(macs, moved):
    return pl.CostEstimate(flops=2 * macs, bytes_accessed=moved, transcendentals=0)


def pick(own, kept, received):
    first = own == 0
    return jnp.where(first, kept, received), jnp.where(first, received, kept)


def pair(matrix, low, high, gains):
    ranks = low.shape[0]
    product = dot(matrix, jnp.concatenate([low, high], axis=0))
    return (
        (product[:ranks] * gains[0]).astype(BF16),
        (product[ranks:] * gains[1]).astype(BF16),
    )


def front_kernel(levels, own_ref, low_ref, high_ref, map_ref, tr_ref, gl_ref, gh_ref, kept_ref, sent_ref):
    source_map = map_ref[...]
    low = dot(source_map, low_ref[0]).astype(BF16)
    high = dot(source_map, high_ref[0]).astype(BF16)
    for level in range(levels):
        gains = gl_ref[level : level + 1, :], gh_ref[level : level + 1, :]
        low, high = pair(tr_ref[level], low, high, gains)
    kept_ref[...], sent_ref[...] = pick(own_ref[0], low, high)


def front(image, own, sources, source_map, matrices, box_gain, cols):
    _, points, boxes = sources.shape
    ranks = source_map.shape[0]
    half = boxes // 2
    steps = half // cols
    grid_spec = pltpu.PrefetchScalarGridSpec(
        num_scalar_prefetch=1,
        grid=(steps,),
        in_specs=[
            pl.BlockSpec((1, points, cols), lambda i, s: (image, 0, i)),
            pl.BlockSpec((1, points, cols), lambda i, s: (image, 0, i + steps)),
            pl.BlockSpec((ranks, points), lambda i, s: (0, 0)),
            pl.BlockSpec(matrices.shape, lambda i, s: (0, 0, 0)),
            pl.BlockSpec((box_gain.shape[0], cols), lambda i, s: (0, i)),
            pl.BlockSpec((box_gain.shape[0], cols), lambda i, s: (0, i + steps)),
        ],
        out_specs=[pl.BlockSpec((ranks, cols), lambda i, s: (0, i))] * 2,
    )
    return pl.pallas_call(
        functools.partial(front_kernel, LOCAL_LEVELS),
        grid_spec=grid_spec,
        out_shape=[jax.ShapeDtypeStruct((ranks, half), BF16)] * 2,
        compiler_params=params(56 * 2**20),
        cost_estimate=cost(boxes * ranks * (points + LOCAL_LEVELS * 2 * ranks) * 8, boxes * points * 2),
        name="source_map_and_local_levels",
    )(own, sources, sources, source_map, matrices, box_gain, box_gain)


def swap_kernel(level, own_ref, kept_in, recv_in, tr_ref, gl_ref, gh_ref, kept_ref, sent_ref):
    gains = gl_ref[level : level + 1, :], gh_ref[level : level + 1, :]
    low, high = pick(own_ref[0], kept_in[...], recv_in[...])
    low, high = pair(tr_ref[level], low, high, gains)
    kept_ref[...], sent_ref[...] = pick(own_ref[1], low, high)


def pieces_kernel(level, own_ref, kept_in, recv_in, tr_ref, gl_ref, gh_ref, out_ref):
    gains = gl_ref[level : level + 1, :], gh_ref[level : level + 1, :]
    low, high = pick(own_ref[0], kept_in[...], recv_in[...])
    both = pair(tr_ref[level], low, high, gains)
    ranks = low.shape[0]
    piece = out_ref.shape[3]
    extra = out_ref.shape[2] - ranks
    if extra:
        later = [ref[i : i + 1, :] for i in range(level + 1, gl_ref.shape[0]) for ref in (gl_ref, gh_ref)]
        later += [jnp.zeros_like(later[0])] * (extra - len(later))
        later = jnp.concatenate(later, axis=0).astype(BF16)
    for n in range(2):
        for k in range(out_ref.shape[1]):
            at = slice(k * piece, (k + 1) * piece)
            out_ref[n, k, :ranks, :] = both[n][:, at]
            if extra:
                out_ref[n, k, ranks:, :] = later[:, at]


def upper_level(level, owns, kept, received, matrices, box_gain, cols, pieces=None, extra=0):
    ranks, half = kept.shape
    steps = half // cols
    block = pl.BlockSpec((ranks, cols), lambda i, s: (0, i))
    if pieces is None:
        kernel, out_specs = swap_kernel, [block] * 2
        out_shape = [jax.ShapeDtypeStruct(kept.shape, BF16)] * 2
    else:
        piece = 2 * half // pieces
        kernel = pieces_kernel
        out_specs = pl.BlockSpec((2, cols // piece, ranks + extra, piece), lambda i, s: (0, i, 0, 0))
        out_shape = jax.ShapeDtypeStruct((2, pieces // 2, ranks + extra, piece), BF16)
    grid_spec = pltpu.PrefetchScalarGridSpec(
        num_scalar_prefetch=1,
        grid=(steps,),
        in_specs=[
            block,
            block,
            pl.BlockSpec(matrices.shape, lambda i, s: (0, 0, 0)),
            pl.BlockSpec((box_gain.shape[0], cols), lambda i, s: (0, i)),
            pl.BlockSpec((box_gain.shape[0], cols), lambda i, s: (0, i + steps)),
        ],
        out_specs=out_specs,
    )
    return pl.pallas_call(
        functools.partial(kernel, level),
        grid_spec=grid_spec,
        out_shape=out_shape,
        compiler_params=params(),
        cost_estimate=cost(half * 4 * ranks * ranks * 8, half * ranks * 8),
        name="upper_level",
    )(owns, kept, received, matrices, box_gain, box_gain)


UNROLL = 32


def gather_kernel(order_ref, in_ref, out_ref, table, picked):
    pieces, _, piece = in_ref.shape

    def widen(i, carry):
        at = pl.ds(pl.multiple_of(i * piece, piece), piece)
        table[at, :] = in_ref[i, : table.shape[1], :].astype(F32).T
        return carry

    lax.fori_loop(0, pieces, widen, 0, unroll=2)

    def move(i, carry):
        base = pl.multiple_of(i * UNROLL, UNROLL)
        for k in range(UNROLL):
            picked[pl.ds(base + k, 1), :] = table[pl.ds(order_ref[0, base + k], 1), :]
        return carry

    lax.fori_loop(0, pieces * piece // UNROLL, move, 0)

    def narrow(i, carry):
        at = pl.ds(pl.multiple_of(i * piece, piece), piece)
        out_ref[i] = picked[at, :].T.astype(BF16)
        return carry

    lax.fori_loop(0, pieces, narrow, 0, unroll=2)


def gather(order, x, ranks):
    pieces, _, piece = x.shape
    return pl.pallas_call(
        gather_kernel,
        in_specs=[
            pl.BlockSpec(memory_space=pltpu.SMEM),
            pl.BlockSpec(memory_space=pltpu.VMEM),
        ],
        out_specs=pl.BlockSpec(memory_space=pltpu.VMEM),
        out_shape=jax.ShapeDtypeStruct((pieces, ranks, piece), BF16),
        scratch_shapes=[pltpu.VMEM((pieces * piece, ranks), F32)] * 2,
        compiler_params=params(),
        cost_estimate=cost(0, 30 * 2**20),
        name="box_order",
    )(order, x)


def lower_kernel(levels, first, own_ref, x_ref, tr_ref, gain_ref, out_ref, held):
    devices, ranks, _ = x_ref.shape
    half_at = own_ref[0] * (devices // 2)
    for i in range(levels):
        bit = levels - 1 - i
        matrix = tr_ref[first + i]
        origin = x_ref if i == 0 else held
        target = out_ref if i == levels - 1 else held
        for g in range(devices // 2):
            low_at = ((g >> bit) << (bit + 1)) | (g & ((1 << bit) - 1))
            high_at = low_at + (1 << bit)
            rows = gain_ref[half_at + g, 2 * i : 2 * i + 2, :].astype(F32)
            gains = [rows[n : n + 1] for n in range(2)]
            target[low_at], target[high_at] = pair(matrix, origin[low_at], origin[high_at], gains)


def lower_levels(own, x, matrices, gains, first):
    devices, ranks, cols = x.shape
    levels = devices.bit_length() - 1
    return pl.pallas_call(
        functools.partial(lower_kernel, levels, first),
        in_specs=[pl.BlockSpec(memory_space=pltpu.SMEM)] + [pl.BlockSpec(memory_space=pltpu.VMEM)] * 3,
        out_specs=pl.BlockSpec(memory_space=pltpu.VMEM),
        out_shape=jax.ShapeDtypeStruct(x.shape, BF16),
        scratch_shapes=[pltpu.VMEM(x.shape, BF16)],
        compiler_params=params(),
        cost_estimate=cost(levels * devices * cols * 2 * ranks * ranks * 8, devices * ranks * cols * 4),
        name="lower_levels",
    )(own, x, matrices, gains)


def target_kernel(x_ref, map_ref, *refs):
    out_ref = refs[-1]
    pieces, _, _, cols = x_ref.shape
    target_map = map_ref[...]
    for k in range(pieces):
        out_ref[0, :, k * cols : (k + 1) * cols] = dot(target_map, x_ref[k, 0]).astype(BF16)


def to_targets(image, images, x, target_map, pieces, field):
    t_pieces, two, ranks, cols = x.shape
    points = target_map.shape[0]
    per_half = t_pieces // pieces
    operands = [x, target_map] + ([] if field is None else [field])
    return pl.pallas_call(
        target_kernel,
        grid=(two, per_half),
        in_specs=[
            pl.BlockSpec((pieces, 1, ranks, cols), lambda n, i: (i, n, 0, 0)),
            pl.BlockSpec((points, ranks), lambda n, i: (0, 0)),
        ]
        + ([] if field is None else [pl.BlockSpec(memory_space=pl.ANY)]),
        out_specs=pl.BlockSpec((1, points, pieces * cols), lambda n, i: (image, 0, n * per_half + i)),
        out_shape=jax.ShapeDtypeStruct((images, points, two * t_pieces * cols), BF16),
        input_output_aliases={} if field is None else {2: 0},
        compiler_params=params(),
        cost_estimate=cost(points * ranks * two * t_pieces * cols * 4, points * two * t_pieces * cols * 2),
        name="target_map",
    )(*operands)


def body(sources, source_map, translation, box_gain, target_order, target_map):
    images, _, boxes = sources.shape
    ranks = source_map.shape[0]
    n_lower = lax.axis_size("lo")
    matrices = translation.reshape(translation.shape[0], 2 * ranks, 2 * ranks)
    upper = lax.axis_index("hi")
    owns = jnp.stack([upper >> 1 & 1, upper & 1]).astype(jnp.int32)
    first_lower = LOCAL_LEVELS + 2
    levels_lo = n_lower.bit_length() - 1
    piece = boxes // n_lower
    halves = n_lower // 2

    groups = [list(range(halves)), list(range(halves, n_lower))]
    own_half = (lax.axis_index("lo") // halves).astype(jnp.int32).reshape(1)
    gain_rows = -(-2 * levels_lo // 16) * 16

    fronts = [front(c, owns[:1], sources, source_map, matrices, box_gain, 2048) for c in range(images)]
    arrived = []
    for kept, sent in fronts:
        arrived.append(lax.ppermute(sent, "hi", [(i, i ^ 2) for i in range(4)]))
    owns, _ = lax.optimization_barrier((owns, fronts[-1][0]))
    field = None
    for c in range(images):
        kept = fronts[c][0]
        kept, sent = upper_level(LOCAL_LEVELS, owns, kept, arrived[c], matrices, box_gain, 2048)
        received = lax.ppermute(sent, "hi", [(i, i ^ 1) for i in range(4)])
        if c == 0:
            received, arrived[1] = lax.optimization_barrier((received, arrived[1]))
        extra = gain_rows if c == 0 else 0
        x = upper_level(
            LOCAL_LEVELS + 1, owns[1:], kept, received, matrices, box_gain, 2048, n_lower, extra
        )
        x = lax.all_to_all(x.reshape(n_lower, ranks + extra, piece), "lo", 0, 0)
        if c == 0:
            gains = x[:, ranks:, :]
        x = gather(target_order, x, ranks)
        x = lax.all_to_all(x, "lo", 0, 0)
        x = lower_levels(own_half, x, matrices, gains, first_lower)
        x = x.reshape(halves, 2, ranks, piece)
        x = lax.all_to_all(x, "lo", 0, 0, axis_index_groups=groups)
        field = to_targets(c, images, x, target_map, 8, field)
    return field


def solution(mesh):
    return jax.shard_map(
        body,
        mesh=mesh,
        in_specs=(
            P(None, None, ("hi", "lo")),
            P(),
            P(),
            P(None, ("hi", "lo")),
            P(("hi", "lo"), None),
            P(),
        ),
        out_specs=P(None, None, ("hi", "lo")),
        check_vma=False,
    )
```

time: 201 us -> 164 us (0.82)
  the two profiles are of different devices: /device:TPU:1 before, /device:TPU:0 now
where the time goes in v1:
time: 164 us; the launch traced here: 163 us
  waiting for transfers between devices  62.3 us (38%)
  Pallas kernels  56.7 us (35%)
  starting transfers between devices  37.7 us (23%)
  local copies, waits for them, and re-layouts  6.45 us (4%)
    pallas_call x2, Pallas kernels, gather(): pl.pallas_call(gather_kernel, in_specs=[pl.BlockSpec(memory_space=pltpu.S...  25.6 us
    all_to_all x2, waiting for transfers between devices, body(): x = lax.all_to_all(x, 'lo', 0, 0, axis_index_groups=groups)  21.2 us
    ppermute x2, waiting for transfers between devices, body(): arrived.append(lax.ppermute(sent, 'hi', [(i, i ^ 2) for i in range(4)]))  14.2 us
    all_to_all x2, waiting for transfers between devices, body(): x = lax.all_to_all(x.reshape(n_lower, ranks + extra, piece), 'lo', 0, 0)  14.1 us
    pallas_call x2, Pallas kernels, front(): pl.pallas_call(functools.partial(front_kernel, LOCAL_LEVELS), grid_spec=g...  13.4 us
    all_to_all x2, starting transfers between devices, body(): x = lax.all_to_all(x, 'lo', 0, 0)  13.1 us
    all_to_all x2, starting transfers between devices, body(): x = lax.all_to_all(x.reshape(n_lower, ranks + extra, piece), 'lo', 0, 0)  12.8 us
    all_to_all x2, waiting for transfers between devices, body(): x = lax.all_to_all(x, 'lo', 0, 0)  10.9 us
  transfers between devices with their start and end apart: 10, of which 9 were waited for; matrix products, arithmetic and copies ran while one was open for 0% of the time, Pallas kernels for 27%

profile of v1, /device:TPU:0, one launch (start us, length us, event | category | flops | bytes accessed | tf_op | source)
XLA Modules:
  0.0 163.5 jit_solution(3208434380125323271)
XLA Ops:
  0.0 6.7 %source_map_and_local_levels.3 = (bf16[64,4096]{1,0:T(8,128)(2,1)}, bf16[64,4096]{1,0:T(8,128)(2,1)}) custom-call(s32[1]{0:T(128)} %bitcast.1.own_ref, bf16[2,256,8192]{2,1,0:T(8,128)(2,1)} %high_ref.3, bf16[2,256,8192]{2,1,0:T(8,128)(2,1)} %high_ref.3, bf16[64,256]{1,0:T(8,128)(2,1)} %map_ref.5, bf16[15,128,128]{2,1,0:T(8,128)(2,1)} %bitcast.9, ...), custom_call_target="tpu_custom_call" | custom-call | flops 10737418240 | bytes 4194304 | tf_op jit(solution)/shard_map/source_map_and_local_levels/pallas_call | solution.py:70
  6.7 4.0 %collective-permute-start = (bf16[64,4096]{1,0:T(8,128)(2,1)}, bf16[64,4096]{1,0:T(8,128)(2,1)S(1)}, u32[]{:S(2)}, u32[]{:S(2)}) collective-permute-start(bf16[64,4096]{1,0:T(8,128)(2,1)} %get-tuple-element.19), channel_id=1, source_target_pairs={{0,64},{32,96},{64,0},{96,32},{1,65},{33,97},{65,1},{97,33},{2,66}... | collective-permute-start | bytes 1572872 | tf_op jit(solution)/shard_map/ppermute | solution.py:266
  10.8 6.7 %source_map_and_local_levels.2 = (bf16[64,4096]{1,0:T(8,128)(2,1)}, bf16[64,4096]{1,0:T(8,128)(2,1)}) custom-call(s32[1]{0:T(128)} %bitcast.1.own_ref, bf16[2,256,8192]{2,1,0:T(8,128)(2,1)} %high_ref.3, bf16[2,256,8192]{2,1,0:T(8,128)(2,1)} %high_ref.3, bf16[64,256]{1,0:T(8,128)(2,1)} %map_ref.5, bf16[15,128,128]{2,1,0:T(8,128)(2,1)} %bitcast.10, ...), custom_call_target="tpu_custom_call" | custom-call | flops 10737418240 | bytes 4194304 | tf_op jit(solution)/shard_map/source_map_and_local_levels/pallas_call | solution.py:70
  17.8 5.9 %collective-permute-done.recv_in = bf16[64,4096]{1,0:T(8,128)(2,1)S(1)} collective-permute-done((bf16[64,4096]{1,0:T(8,128)(2,1)}, bf16[64,4096]{1,0:T(8,128)(2,1)S(1)}, u32[]{:S(2)}, u32[]{:S(2)}) %collective-permute-start) | collective-permute-done | bytes 524320 | tf_op jit(solution)/shard_map/ppermute | solution.py:266
  23.8 1.4 upper_level.4
  25.8 8.3 %collective-permute-done.2.recv_in = bf16[64,4096]{1,0:T(8,128)(2,1)S(1)} collective-permute-done((bf16[64,4096]{1,0:T(8,128)(2,1)}, bf16[64,4096]{1,0:T(8,128)(2,1)S(1)}, u32[]{:S(2)}, u32[]{:S(2)}) %collective-permute-start.2) | collective-permute-done | bytes 524320 | tf_op jit(solution)/shard_map/ppermute | solution.py:266
  34.2 2.2 %upper_level.7 = bf16[2,16,80,256]{3,2,1,0:T(8,128)(2,1)} custom-call(s32[1]{0:T(128)} %slice.7.own_ref, bf16[64,4096]{1,0:T(8,128)(2,1)S(1)} %get-tuple-element.25.kept_in, bf16[64,4096]{1,0:T(8,128)(2,1)S(1)} %collective-permute-done.1.recv_in, bf16[15,128,128]{2,1,0:T(8,128)(2,1)S(1)} %bitcast.12, f32[15,8192]{1,0:T(8,128)S(1)} %copy-done.4, ...), custom_call_target="tpu_custom_call" | custom-call | flops 1073741824 | bytes 2097152 | tf_op jit(solution)/shard_map/upper_level/pallas_call | solution.py:130
  36.4 8.0 %all-to-all-start.2 = ((bf16[32,80,256]{2,1,0:T(8,128)(2,1)}), bf16[32,80,256]{2,1,0:T(8,128)(2,1)S(1)}, u32[]{:S(2)}, u32[]{:S(2)}) async-start(bf16[32,80,256]{2,1,0:T(8,128)(2,1)} %bitcast.5), calls=%async_computation.2 | async-start | bytes 2621440 | tf_op jit(solution)/shard_map/all_to_all | solution.py:279
  44.5 1.0 copy-done.8
  45.5 1.4 upper_level.5
  47.0 1.9 %collective-permute-done.3.recv_in = bf16[64,4096]{1,0:T(8,128)(2,1)S(1)} collective-permute-done((bf16[64,4096]{1,0:T(8,128)(2,1)S(1)}, bf16[64,4096]{1,0:T(8,128)(2,1)S(1)}, u32[]{:S(2)}, u32[]{:S(2)}) %collective-permute-start.3) | collective-permute-done | bytes 524320 | tf_op jit(solution)/shard_map/ppermute | solution.py:272
  48.9 2.1 %upper_level.6 = bf16[2,16,64,256]{3,2,1,0:T(8,128)(2,1)} custom-call(s32[1]{0:T(128)} %slice.7.own_ref, bf16[64,4096]{1,0:T(8,128)(2,1)S(1)} %get-tuple-element.23.kept_in, bf16[64,4096]{1,0:T(8,128)(2,1)S(1)} %collective-permute-done.3.recv_in, bf16[15,128,128]{2,1,0:T(8,128)(2,1)S(1)} %bitcast.14, f32[15,8192]{1,0:T(8,128)S(1)} %copy-done.4, ...), custom_call_target="tpu_custom_call" | custom-call | flops 1073741824 | bytes 2097152 | tf_op jit(solution)/shard_map/upper_level/pallas_call | solution.py:130
  51.0 12.0 %all-to-all-done.2.in_ref = bf16[32,80,256]{2,1,0:T(8,128)(2,1)S(1)} async-done(((bf16[32,80,256]{2,1,0:T(8,128)(2,1)}), bf16[32,80,256]{2,1,0:T(8,128)(2,1)S(1)}, u32[]{:S(2)}, u32[]{:S(2)}) %all-to-all-start.2) | async-done | bytes 1310752 | tf_op jit(solution)/shard_map/all_to_all | solution.py:279
  63.0 4.8 %all-to-all-start = ((bf16[32,64,256]{2,1,0:T(8,128)(2,1)}), bf16[32,64,256]{2,1,0:T(8,128)(2,1)S(1)}, u32[]{:S(2)}, u32[]{:S(2)}) async-start(bf16[32,64,256]{2,1,0:T(8,128)(2,1)} %bitcast.4), calls=%async_computation | async-start | bytes 2097152 | tf_op jit(solution)/shard_map/all_to_all | solution.py:279
  67.8 12.8 %box_order.3 = bf16[32,64,256]{2,1,0:T(8,128)(2,1)} custom-call(s32[1,8192]{1,0:T(1,128)S(1)} %copy-done.3, bf16[32,80,256]{2,1,0:T(8,128)(2,1)S(1)} %all-to-all-done.2.in_ref), custom_call_target="tpu_custom_call" | custom-call | bytes 31457280 | tf_op jit(solution)/shard_map/box_order/pallas_call | solution.py:171
  80.6 2.0 %all-to-all-done.in_ref = bf16[32,64,256]{2,1,0:T(8,128)(2,1)S(1)} async-done(((bf16[32,64,256]{2,1,0:T(8,128)(2,1)}), bf16[32,64,256]{2,1,0:T(8,128)(2,1)S(1)}, u32[]{:S(2)}, u32[]{:S(2)}) %all-to-all-start) | async-done | bytes 1048608 | tf_op jit(solution)/shard_map/all_to_all | solution.py:279
  82.6 6.3 %all-to-all-start.4 = ((bf16[32,64,256]{2,1,0:T(8,128)(2,1)}), bf16[32,64,256]{2,1,0:T(8,128)(2,1)S(1)}, u32[]{:S(2)}, u32[]{:S(2)}) async-start(bf16[32,64,256]{2,1,0:T(8,128)(2,1)} %box_order.3), calls=%async_computation.4 | async-start | bytes 2097152 | tf_op jit(solution)/shard_map/all_to_all | solution.py:283
  88.9 12.8 %box_order.2 = bf16[32,64,256]{2,1,0:T(8,128)(2,1)} custom-call(s32[1,8192]{1,0:T(1,128)S(1)} %copy-done.3, bf16[32,64,256]{2,1,0:T(8,128)(2,1)S(1)} %all-to-all-done.in_ref), custom_call_target="tpu_custom_call" | custom-call | bytes 31457280 | tf_op jit(solution)/shard_map/box_order/pallas_call | solution.py:171
  101.7 1.5 all-to-all-done.4.x_ref
  103.2 6.8 %all-to-all-start.1 = ((bf16[32,64,256]{2,1,0:T(8,128)(2,1)}), bf16[32,64,256]{2,1,0:T(8,128)(2,1)S(1)}, u32[]{:S(2)}, u32[]{:S(2)}) async-start(bf16[32,64,256]{2,1,0:T(8,128)(2,1)} %box_order.2), calls=%async_computation.1 | async-start | bytes 2097152 | tf_op jit(solution)/shard_map/all_to_all | solution.py:283
  110.1 1.0 copy-done.6
  111.1 1.5 lower_levels.3
  112.6 1.0 copy-done
  114.3 9.4 %all-to-all-done.1.x_ref = bf16[32,64,256]{2,1,0:T(8,128)(2,1)S(1)} async-done(((bf16[32,64,256]{2,1,0:T(8,128)(2,1)}), bf16[32,64,256]{2,1,0:T(8,128)(2,1)S(1)}, u32[]{:S(2)}, u32[]{:S(2)}) %all-to-all-start.1) | async-done | bytes 1048608 | tf_op jit(solution)/shard_map/all_to_all | solution.py:283
  123.7 3.7 %all-to-all-start.5 = ((bf16[16,2,64,256]{3,2,1,0:T(8,128)(2,1)}), bf16[16,2,64,256]{3,2,1,0:T(8,128)(2,1)S(1)}, u32[]{:S(2)}, u32[]{:S(2)}) async-start(bf16[16,2,64,256]{3,2,1,0:T(8,128)(2,1)} %bitcast.8), calls=%async_computation.5 | async-start | bytes 2097152 | tf_op jit(solution)/shard_map/all_to_all | solution.py:286
  128.4 1.0 copy-done.7
  129.4 2.5 %lower_levels.2 = bf16[32,64,256]{2,1,0:T(8,128)(2,1)} custom-call(s32[1]{0:T(128)} %bitcast.own_ref, bf16[32,64,256]{2,1,0:T(8,128)(2,1)S(1)} %all-to-all-done.1.x_ref, bf16[15,128,128]{2,1,0:T(8,128)(2,1)S(1)} %bitcast.16, bf16[32,16,256]{2,1,0:T(8,128)(2,1)S(1)} %copy-done.2), custom_call_target="tpu_custom_call" | custom-call | flops 5368709120 | bytes 2097152 | tf_op jit(solution)/shard_map/lower_levels/pallas_call | solution.py:205
  131.9 10.3 %all-to-all-done.5.x_ref = bf16[16,2,64,256]{3,2,1,0:T(8,128)(2,1)S(1)} async-done(((bf16[16,2,64,256]{3,2,1,0:T(8,128)(2,1)}), bf16[16,2,64,256]{3,2,1,0:T(8,128)(2,1)S(1)}, u32[]{:S(2)}, u32[]{:S(2)}) %all-to-all-start.5) | async-done | bytes 1048608 | tf_op jit(solution)/shard_map/all_to_all | solution.py:286
  142.2 3.7 %all-to-all-start.3 = ((bf16[16,2,64,256]{3,2,1,0:T(8,128)(2,1)}), bf16[16,2,64,256]{3,2,1,0:T(8,128)(2,1)S(1)}, u32[]{:S(2)}, u32[]{:S(2)}) async-start(bf16[16,2,64,256]{3,2,1,0:T(8,128)(2,1)} %bitcast.6), calls=%async_computation.3 | async-start | bytes 2097152 | tf_op jit(solution)/shard_map/all_to_all | solution.py:286
  146.0 3.3 %target_map.2.refs_0_ = bf16[2,256,8192]{2,1,0:T(8,128)(2,1)} custom-call(bf16[16,2,64,256]{3,2,1,0:T(8,128)(2,1)S(1)} %all-to-all-done.5.x_ref, bf16[256,64]{1,0:T(8,128)(2,1)S(1)} %copy.9.map_ref), custom_call_target="tpu_custom_call" | custom-call | flops 1073741824 | bytes 4194304 | tf_op jit(solution)/shard_map/target_map/pallas_call | solution.py:230
  149.3 11.0 %all-to-all-done.3.x_ref = bf16[16,2,64,256]{3,2,1,0:T(8,128)(2,1)S(1)} async-done(((bf16[16,2,64,256]{3,2,1,0:T(8,128)(2,1)}), bf16[16,2,64,256]{3,2,1,0:T(8,128)(2,1)S(1)}, u32[]{:S(2)}, u32[]{:S(2)}) %all-to-all-start.3) | async-done | bytes 1048608 | tf_op jit(solution)/shard_map/all_to_all | solution.py:286
  160.2 3.3 %target_map.3 = bf16[2,256,8192]{2,1,0:T(8,128)(2,1)} custom-call(bf16[16,2,64,256]{3,2,1,0:T(8,128)(2,1)S(1)} %all-to-all-done.3.x_ref, bf16[256,64]{1,0:T(8,128)(2,1)S(1)} %copy.9.map_ref, bf16[2,256,8192]{2,1,0:T(8,128)(2,1)} %target_map.2.refs_0_), custom_call_target="tpu_custom_call", output_to_operand_aliasing={{}: (2, {})} | custom-call | flops 1073741824 | bytes 4194304 | tf_op jit(solution)/shard_map/target_map/pallas_call | solution.py:230
  (26 shorter events, 2.9 us)
Async XLA Ops:
  6.7 17.0 %copy-start.4 = (f32[15,8192]{1,0:T(8,128)S(1)}, f32[15,8192]{1,0:T(8,128)}, u32[]{:S(2)}) copy-start(f32[15,8192]{1,0:T(8,128)} %gh_ref.11) | copy-start | bytes 1474564
  6.7 17.0 %copy-start.5 = (bf16[15,2,64,128]{3,2,1,0:T(8,128)(2,1)S(1)}, bf16[15,2,64,128]{3,2,1,0:T(8,128)(2,1)}, u32[]{:S(2)}) copy-start(bf16[15,2,64,128]{3,2,1,0:T(8,128)(2,1)} %param.8) | copy-start | bytes 1474564
  6.7 17.0 %copy-start.9 = (bf16[64,4096]{1,0:T(8,128)(2,1)S(1)}, bf16[64,4096]{1,0:T(8,128)(2,1)}, u32[]{:S(2)}) copy-start(bf16[64,4096]{1,0:T(8,128)(2,1)} %get-tuple-element.18.kept_in) | copy-start | bytes 1572868
  6.7 17.0 %collective-permute-start = (bf16[64,4096]{1,0:T(8,128)(2,1)}, bf16[64,4096]{1,0:T(8,128)(2,1)S(1)}, u32[]{:S(2)}, u32[]{:S(2)}) collective-permute-start(bf16[64,4096]{1,0:T(8,128)(2,1)} %get-tuple-element.19), channel_id=1, source_target_pairs={{0,64},{32,96},{64,0},{96,32},{1,65},{33,97},{65,1},{97,33},{2,66}... | collective-permute-start | bytes 1572872 | tf_op jit(solution)/shard_map/ppermute | solution.py:266
  17.5 16.7 %collective-permute-start.2 = (bf16[64,4096]{1,0:T(8,128)(2,1)}, bf16[64,4096]{1,0:T(8,128)(2,1)S(1)}, u32[]{:S(2)}, u32[]{:S(2)}) collective-permute-start(bf16[64,4096]{1,0:T(8,128)(2,1)} %get-tuple-element.21), channel_id=1, source_target_pairs={{0,64},{32,96},{64,0},{96,32},{1,65},{33,97},{65,1},{97,33},{2,66}... | collective-permute-start | bytes 1572872 | tf_op jit(solution)/shard_map/ppermute | solution.py:266
  25.2 42.7 %copy-start.3 = (s32[1,8192]{1,0:T(1,128)S(1)}, s32[1,8192]{1,0:T(1,128)}, u32[]{:S(2)}) copy-start(s32[1,8192]{1,0:T(1,128)} %order_ref.3) | copy-start | bytes 98308
  25.2 9.0 %collective-permute-start.1 = (bf16[64,4096]{1,0:T(8,128)(2,1)S(1)}, bf16[64,4096]{1,0:T(8,128)(2,1)S(1)}, u32[]{:S(2)}, u32[]{:S(2)}) collective-permute-start(bf16[64,4096]{1,0:T(8,128)(2,1)S(1)} %get-tuple-element.20), channel_id=1, source_target_pairs={{0,32},{32,0},{64,96},{96,64},{1,33},{33,1},{65,97},{97,65},{2,34}... | collective-permute-start | bytes 1572872 | tf_op jit(solution)/shard_map/ppermute | solution.py:272
  36.4 26.7 %all-to-all-start.2 = ((bf16[32,80,256]{2,1,0:T(8,128)(2,1)}), bf16[32,80,256]{2,1,0:T(8,128)(2,1)S(1)}, u32[]{:S(2)}, u32[]{:S(2)}) async-start(bf16[32,80,256]{2,1,0:T(8,128)(2,1)} %bitcast.5), calls=%async_computation.2 | async-start | bytes 2621440 | tf_op jit(solution)/shard_map/all_to_all | solution.py:279
  44.4 1.0 copy-start.8
  46.9 2.0 %collective-permute-start.3 = (bf16[64,4096]{1,0:T(8,128)(2,1)S(1)}, bf16[64,4096]{1,0:T(8,128)(2,1)S(1)}, u32[]{:S(2)}, u32[]{:S(2)}) collective-permute-start(bf16[64,4096]{1,0:T(8,128)(2,1)S(1)} %get-tuple-element.24), channel_id=1, source_target_pairs={{0,32},{32,0},{64,96},{96,64},{1,33},{33,1},{65,97},{97,65},{2,34}... | collective-permute-start | bytes 1572872 | tf_op jit(solution)/shard_map/ppermute | solution.py:272
  63.0 19.6 %all-to-all-start = ((bf16[32,64,256]{2,1,0:T(8,128)(2,1)}), bf16[32,64,256]{2,1,0:T(8,128)(2,1)S(1)}, u32[]{:S(2)}, u32[]{:S(2)}) async-start(bf16[32,64,256]{2,1,0:T(8,128)(2,1)} %bitcast.4), calls=%async_computation | async-start | bytes 2097152 | tf_op jit(solution)/shard_map/all_to_all | solution.py:279
  82.6 20.5 %all-to-all-start.4 = ((bf16[32,64,256]{2,1,0:T(8,128)(2,1)}), bf16[32,64,256]{2,1,0:T(8,128)(2,1)S(1)}, u32[]{:S(2)}, u32[]{:S(2)}) async-start(bf16[32,64,256]{2,1,0:T(8,128)(2,1)} %box_order.3), calls=%async_computation.4 | async-start | bytes 2097152 | tf_op jit(solution)/shard_map/all_to_all | solution.py:283
  103.2 20.5 %all-to-all-start.1 = ((bf16[32,64,256]{2,1,0:T(8,128)(2,1)}), bf16[32,64,256]{2,1,0:T(8,128)(2,1)S(1)}, u32[]{:S(2)}, u32[]{:S(2)}) async-start(bf16[32,64,256]{2,1,0:T(8,128)(2,1)} %box_order.2), calls=%async_computation.1 | async-start | bytes 2097152 | tf_op jit(solution)/shard_map/all_to_all | solution.py:283
  110.1 1.0 copy-start.6
  112.6 1.0 copy-start
  113.6 0.7 copy-start.1
  123.7 18.5 %all-to-all-start.5 = ((bf16[16,2,64,256]{3,2,1,0:T(8,128)(2,1)}), bf16[16,2,64,256]{3,2,1,0:T(8,128)(2,1)S(1)}, u32[]{:S(2)}, u32[]{:S(2)}) async-start(bf16[16,2,64,256]{3,2,1,0:T(8,128)(2,1)} %bitcast.8), calls=%async_computation.5 | async-start | bytes 2097152 | tf_op jit(solution)/shard_map/all_to_all | solution.py:286
  127.4 1.0 copy-start.2
  128.4 1.0 copy-start.7
  129.4 16.4 %copy-start.10 = (bf16[256,64]{0,1:T(8,128)(2,1)S(1)}, bf16[256,64]{0,1:T(8,128)(2,1)}, u32[]{:S(2)}) copy-start(bf16[256,64]{0,1:T(8,128)(2,1)} %param.11) | copy-start | bytes 98308
  142.2 18.0 %all-to-all-start.3 = ((bf16[16,2,64,256]{3,2,1,0:T(8,128)(2,1)}), bf16[16,2,64,256]{3,2,1,0:T(8,128)(2,1)S(1)}, u32[]{:S(2)}, u32[]{:S(2)}) async-start(bf16[16,2,64,256]{3,2,1,0:T(8,128)(2,1)} %bitcast.6), calls=%async_computation.3 | async-start | bytes 2097152 | tf_op jit(solution)/shard_map/all_to_all | solution.py:286

commit v2 on v0

v2 whole, which is shorter than its diff:
```python
import functools

import jax
import jax.numpy as jnp
from jax import lax
from jax.experimental import pallas as pl
from jax.experimental.pallas import tpu as pltpu
from jax.sharding import PartitionSpec as P

LOCAL_LEVELS = 8
F32 = jnp.float32
BF16 = jnp.bfloat16
VMEM_LIMIT = 40 * 2**20
FRONT_LIMIT = 56 * 2**20
PARTS = 2


def dot(a, b):
    return jnp.dot(a, b, preferred_element_type=F32)


def params(limit=VMEM_LIMIT):
    return pltpu.CompilerParams(vmem_limit_bytes=limit)


def cost(macs, moved):
    return pl.CostEstimate(flops=2 * macs, bytes_accessed=moved, transcendentals=0)


def pick(own, kept, received):
    first = own == 0
    return jnp.where(first, kept, received), jnp.where(first, received, kept)


def pair(matrix, low, high, gains):
    ranks = low.shape[0]
    product = dot(matrix, jnp.concatenate([low, high], axis=0))
    return (
        (product[:ranks] * gains[0]).astype(BF16),
        (product[ranks:] * gains[1]).astype(BF16),
    )


def front_kernel(levels, own_ref, low_ref, high_ref, map_ref, tr_ref, gl_ref, gh_ref, kept_ref, sent_ref):
    source_map = map_ref[...]
    low = dot(source_map, low_ref[0]).astype(BF16)
    high = dot(source_map, high_ref[0]).astype(BF16)
    for level in range(levels):
        gains = gl_ref[level : level + 1, :], gh_ref[level : level + 1, :]
        low, high = pair(tr_ref[level], low, high, gains)
    kept_ref[...], sent_ref[...] = pick(own_ref[0], low, high)


def front(image, part, parts, own, sources, source_map, matrices, box_gain):
    _, points, boxes = sources.shape
    ranks = source_map.shape[0]
    cols = boxes // 2 // parts
    grid_spec = pltpu.PrefetchScalarGridSpec(
        num_scalar_prefetch=1,
        grid=(1,),
        in_specs=[
            pl.BlockSpec((1, points, cols), lambda i, s: (image, 0, part)),
            pl.BlockSpec((1, points, cols), lambda i, s: (image, 0, parts + part)),
            pl.BlockSpec((ranks, points), lambda i, s: (0, 0)),
            pl.BlockSpec((LOCAL_LEVELS,) + matrices.shape[1:], lambda i, s: (0, 0, 0)),
            pl.BlockSpec((LOCAL_LEVELS, cols), lambda i, s: (0, part)),
            pl.BlockSpec((LOCAL_LEVELS, cols), lambda i, s: (0, parts + part)),
        ],
        out_specs=[pl.BlockSpec((ranks, cols), lambda i, s: (0, 0))] * 2,
    )
    return pl.pallas_call(
        functools.partial(front_kernel, LOCAL_LEVELS),
        grid_spec=grid_spec,
        out_shape=[jax.ShapeDtypeStruct((ranks, cols), BF16)] * 2,
        compiler_params=params(FRONT_LIMIT),
        cost_estimate=cost(2 * cols * ranks * (points + LOCAL_LEVELS * 2 * ranks) * 8, 2 * cols * points * 2),
        name="source_map_and_local_levels",
    )(own, sources, sources, source_map, matrices, box_gain, box_gain)


def swap_kernel(level, own_ref, kept_in, recv_in, tr_ref, gl_ref, gh_ref, kept_ref, sent_ref):
    gains = gl_ref[level : level + 1, :], gh_ref[level : level + 1, :]
    low, high = pick(own_ref[0], kept_in[...], recv_in[...])
    low, high = pair(tr_ref[level], low, high, gains)
    kept_ref[...], sent_ref[...] = pick(own_ref[1], low, high)


def upper_level(level, part, parts, owns, kept, received, matrices, box_gain):
    ranks, cols = kept.shape
    block = pl.BlockSpec((ranks, cols), lambda i, s: (0, 0))
    grid_spec = pltpu.PrefetchScalarGridSpec(
        num_scalar_prefetch=1,
        grid=(1,),
        in_specs=[
            block,
            block,
            pl.BlockSpec(matrices.shape, lambda i, s: (0, 0, 0)),
            pl.BlockSpec((box_gain.shape[0], cols), lambda i, s: (0, part)),
            pl.BlockSpec((box_gain.shape[0], cols), lambda i, s: (0, parts + part)),
        ],
        out_specs=[block] * 2,
    )
    return pl.pallas_call(
        functools.partial(swap_kernel, level),
        grid_spec=grid_spec,
        out_shape=[jax.ShapeDtypeStruct(kept.shape, BF16)] * 2,
        compiler_params=params(),
        cost_estimate=cost(cols * 4 * ranks * ranks * 8, cols * ranks * 8),
        name="upper_level",
    )(owns, kept, received, matrices, box_gain, box_gain)


def rows_kernel(level, images, own_ref, *refs):
    parts, (tr_ref, gl_ref, gh_ref), out_ref = refs[: 2 * images], refs[2 * images : 2 * images + 3], refs[-1]
    gains = gl_ref[level : level + 1, :], gh_ref[level : level + 1, :]
    lows, highs = [], []
    for c in range(images):
        low, high = pick(own_ref[0], parts[c][...], parts[images + c][...])
        low, high = pair(tr_ref[level], low, high, gains)
        lows.append(low)
        highs.append(high)
    piece = gl_ref.shape[1] // out_ref.shape[1]
    width = out_ref.shape[3]
    later = [ref[i : i + 1, :] for i in range(level + 1, gl_ref.shape[0] - 1) for ref in (gl_ref, gh_ref)]
    blank = jnp.zeros((1, width), F32)
    for k in range(out_ref.shape[1]):
        rows = [row[:, at : at + width] for at in range(k * piece, (k + 1) * piece, width) for row in later]
        rows += [blank] * (out_ref.shape[2] - piece - len(rows))
        rows = jnp.concatenate(rows, axis=0).astype(BF16)
        for n in range(2):
            out_ref[n, k, piece:, :] = rows
    for n, blocks in enumerate((lows, highs)):
        stacked = jnp.concatenate(blocks, axis=0).astype(F32)
        for k in range(out_ref.shape[1]):
            out_ref[n, k, :piece, :] = stacked[:, k * piece : (k + 1) * piece].T.astype(BF16)


def rows_level(level, part, parts, owns, kept, received, matrices, box_gain, pieces, extra, before):
    images = len(kept)
    ranks, cols = kept[0].shape
    piece = 2 * parts * cols // pieces
    block = pl.BlockSpec((ranks, cols), lambda i, s: (0, 0))
    more = [] if before is None else [before]
    grid_spec = pltpu.PrefetchScalarGridSpec(
        num_scalar_prefetch=1,
        grid=(1,),
        in_specs=[block] * (2 * images)
        + [
            pl.BlockSpec(matrices.shape, lambda i, s: (0, 0, 0)),
            pl.BlockSpec((box_gain.shape[0], cols), lambda i, s: (0, part)),
            pl.BlockSpec((box_gain.shape[0], cols), lambda i, s: (0, parts + part)),
        ]
        + [pl.BlockSpec(memory_space=pl.ANY)] * len(more),
        out_specs=pl.BlockSpec(
            (2, cols // piece, piece + extra, images * ranks), lambda i, s: (0, part, 0, 0)
        ),
    )
    return pl.pallas_call(
        functools.partial(rows_kernel, level, images),
        grid_spec=grid_spec,
        out_shape=jax.ShapeDtypeStruct((2, pieces // 2, piece + extra, images * ranks), BF16),
        input_output_aliases={2 * images + 4: 0} if more else {},
        compiler_params=params(),
        cost_estimate=cost(images * cols * 4 * ranks * ranks * 8, images * cols * ranks * 8),
        name="upper_level_to_rows",
    )(owns, *kept, *received, matrices, box_gain, box_gain, *more)


UNROLL = 32


def gather_kernel(order_ref, rows_ref, out_ref, table, picked):
    boxes = table.shape[0]
    pieces = rows_ref.shape[0]
    chunk = boxes // pieces

    def widen(i, carry):
        table[pl.ds(pl.multiple_of(i * chunk, chunk), chunk), :] = rows_ref[i, :chunk, :].astype(F32)
        return carry

    lax.fori_loop(0, pieces, widen, 0)

    def move(i, carry):
        base = pl.multiple_of(i * UNROLL, UNROLL)
        for k in range(UNROLL):
            picked[pl.ds(base + k, 1), :] = table[pl.ds(order_ref[0, base + k], 1), :]
        return carry

    lax.fori_loop(0, boxes // UNROLL, move, 0)

    def narrow(i, carry):
        at = pl.ds(pl.multiple_of(i * chunk, chunk), chunk)
        out_ref[at, :] = picked[at, :].astype(BF16)
        return carry

    lax.fori_loop(0, boxes // chunk, narrow, 0)


def gather_rows(order, rows):
    boxes, width = order.shape[1], rows.shape[2]
    return pl.pallas_call(
        gather_kernel,
        in_specs=[
            pl.BlockSpec(memory_space=pltpu.SMEM),
            pl.BlockSpec(memory_space=pltpu.VMEM),
        ],
        out_specs=pl.BlockSpec(memory_space=pltpu.VMEM),
        out_shape=jax.ShapeDtypeStruct((boxes, width), BF16),
        scratch_shapes=[pltpu.VMEM((boxes, width), F32), pltpu.VMEM((boxes, width), F32)],
        compiler_params=params(),
        cost_estimate=cost(0, 30 * 2**20),
        name="box_order",
    )(order, rows)


def lower_kernel(levels, first, own_ref, x_ref, tr_ref, gain_ref, out_ref, held, scales):
    devices, cols, width = x_ref.shape
    images, ranks = out_ref.shape[1], out_ref.shape[2]
    half_at = own_ref[0] * (devices // 2)
    for g in range(devices // 2):
        scales[g] = gain_ref[half_at + g, cols:, :].astype(F32)
    for i in range(levels):
        bit = levels - 1 - i
        matrix = tr_ref[first + i]
        if i == 0:
            blank = jnp.zeros((2 * ranks, ranks), BF16)
            sides = []
            for side in range(2):
                part = matrix[:, side * ranks : (side + 1) * ranks]
                bands = [
                    jnp.concatenate([part if c == b else blank for b in range(images)], axis=1)
                    for c in range(images)
                ]
                sides.append(jnp.concatenate(bands, axis=0))
            both = jnp.concatenate(sides, axis=1)
        target = out_ref if i == levels - 1 else held
        for g in range(devices // 2):
            low_at = ((g >> bit) << (bit + 1)) | (g & ((1 << bit) - 1))
            high_at = low_at + (1 << bit)
            if i < levels - 1:
                gains = []
                for n in range(2):
                    at = [2 * (levels - 1) * k + 2 * i + n for k in range(cols // width)]
                    gains.append(jnp.concatenate([scales[g, r : r + 1, :] for r in at], axis=1))
            if i == 0:
                stacked = jnp.concatenate([x_ref[low_at], x_ref[high_at]], axis=1)
                product = lax.dot_general(
                    both, stacked, (((1,), (1,)), ((), ())), preferred_element_type=F32
                )
            for c in range(images):
                if i == 0:
                    own = product[c * 2 * ranks : (c + 1) * 2 * ranks]
                else:
                    own = dot(matrix, jnp.concatenate([held[low_at, c], held[high_at, c]], axis=0))
                low, high = own[:ranks], own[ranks:]
                if i < levels - 1:
                    low, high = low * gains[0], high * gains[1]
                target[low_at, c] = low.astype(BF16)
                target[high_at, c] = high.astype(BF16)


def lower_levels(own, x, matrices, gains, images, first):
    devices, cols, width = x.shape
    ranks = width // images
    levels = devices.bit_length() - 1
    shape = (devices, images, ranks, cols)
    return pl.pallas_call(
        functools.partial(lower_kernel, levels, first),
        in_specs=[pl.BlockSpec(memory_space=pltpu.SMEM)] + [pl.BlockSpec(memory_space=pltpu.VMEM)] * 3,
        out_specs=pl.BlockSpec(memory_space=pltpu.VMEM),
        out_shape=jax.ShapeDtypeStruct(shape, BF16),
        scratch_shapes=[
            pltpu.VMEM(shape, BF16),
            pltpu.VMEM((devices // 2, gains.shape[1] - cols, width), F32),
        ],
        compiler_params=params(),
        cost_estimate=cost(levels * devices * cols * 2 * width * ranks * 8, devices * width * cols * 4),
        name="lower_levels",
    )(own, x, matrices, gains)


def target_kernel(level, x_ref, map_ref, gain_ref, out_ref):
    pieces, _, images, ranks, cols = x_ref.shape
    target_map = map_ref[...].astype(F32).T.astype(BF16)
    for k in range(pieces):
        at = slice(k * cols, (k + 1) * cols)
        gains = gain_ref[level : level + 1, at]
        for c in range(images):
            scaled = (x_ref[k, 0, c].astype(F32) * gains).astype(BF16)
            out_ref[c, :, at] = dot(target_map, scaled).astype(BF16)


def to_targets(x, target_map, box_gain, pieces):
    t_pieces, two, images, ranks, cols = x.shape
    points = target_map.shape[1]
    per_half = t_pieces // pieces
    return pl.pallas_call(
        functools.partial(target_kernel, box_gain.shape[0] - 1),
        grid=(two, per_half),
        in_specs=[
            pl.BlockSpec((pieces, 1, images, ranks, cols), lambda n, i: (i, n, 0, 0, 0)),
            pl.BlockSpec((ranks, points), lambda n, i: (0, 0)),
            pl.BlockSpec((box_gain.shape[0], pieces * cols), lambda n, i: (0, n * per_half + i)),
        ],
        out_specs=pl.BlockSpec((images, points, pieces * cols), lambda n, i: (0, 0, n * per_half + i)),
        out_shape=jax.ShapeDtypeStruct((images, points, two * t_pieces * cols), BF16),
        compiler_params=params(),
        cost_estimate=cost(images * points * ranks * two * t_pieces * cols * 4, images * points * two * t_pieces * cols * 2),
        name="target_map",
    )(x, target_map, box_gain)


def body(sources, source_map, translation, box_gain, target_order, target_map):
    images, _, boxes = sources.shape
    ranks = source_map.shape[0]
    n_lower = lax.axis_size("lo")
    matrices = translation.reshape(translation.shape[0], 2 * ranks, 2 * ranks)
    upper = lax.axis_index("hi")
    owns = jnp.stack([upper >> 1 & 1, upper & 1]).astype(jnp.int32)
    first_lower = LOCAL_LEVELS + 2
    levels_lo = n_lower.bit_length() - 1
    piece = boxes // n_lower
    halves = n_lower // 2
    groups = [list(range(halves)), list(range(halves, n_lower))]

    own_half = (lax.axis_index("lo") >> levels_lo - 1).astype(jnp.int32).reshape(1)
    extra = -(-2 * (levels_lo - 1) * piece // (images * ranks) // 16) * 16

    kept, received = {}, {}
    for part in range(PARTS):
        for c in range(images):
            at = part, c
            kept[at], sent = front(c, part, PARTS, owns[:1], sources, source_map, matrices, box_gain)
            received[at] = lax.ppermute(sent, "hi", [(i, i ^ 2) for i in range(4)])
    rows = None
    for part in range(PARTS):
        for c in range(images):
            at = part, c
            kept[at], sent = upper_level(
                LOCAL_LEVELS, part, PARTS, owns, kept[at], received[at], matrices, box_gain
            )
            received[at] = lax.ppermute(sent, "hi", [(i, i ^ 1) for i in range(4)])
        rows = rows_level(
            LOCAL_LEVELS + 1,
            part,
            PARTS,
            owns[1:],
            [kept[part, c] for c in range(images)],
            [received[part, c] for c in range(images)],
            matrices,
            box_gain,
            n_lower,
            extra,
            rows,
        )
    own_half, rows = lax.optimization_barrier((own_half, rows))
    moved = lax.all_to_all(rows.reshape(n_lower, piece + extra, images * ranks), "lo", 0, 0)
    rows = gather_rows(target_order, moved)
    rows = lax.all_to_all(rows.reshape(n_lower, piece, images * ranks), "lo", 0, 0)
    blocks = lower_levels(own_half, rows, matrices, moved, images, first_lower)
    blocks = blocks.reshape(halves, 2, images, ranks, piece)
    blocks = lax.all_to_all(blocks, "lo", 0, 0, axis_index_groups=groups)
    return to_targets(blocks, target_map.T, box_gain, 8)


def solution(mesh):
    return jax.shard_map(
        body,
        mesh=mesh,
        in_specs=(
            P(None, None, ("hi", "lo")),
            P(),
            P(),
            P(None, ("hi", "lo")),
            P(("hi", "lo"), None),
            P(),
        ),
        out_specs=P(None, None, ("hi", "lo")),
        check_vma=False,
    )
```

time: 201 us -> 155 us (0.77)
  waiting for transfers between devices: 76.7 us -> 1.76 us
  blocking collectives: 33.2 us -> 96.1 us
  Pallas kernels: 57.7 us -> 42.5 us
  starting transfers between devices: 23.5 us -> 12 us
  local copies, waits for them, and re-layouts: 6.33 us -> 0.04 us
    all_to_all x0 -> x2, blocking collectives: none -> 67 us  [the longest x1 36.7 us: body(): lax.all_to_all(rows.reshape(n_lower, piece + extra, images * ranks), 'lo'...]
    all_to_all x3 -> x0, waiting for transfers between devices: 51.4 us -> none  [the longest x1 26.2 us: body(): rows = lax.all_to_all(rows, 'lo', 0, 0)]
    ppermute x2 -> x8, waiting for transfers between devices: 25.3 us -> 1.76 us  [the longest x4 1.21 us: body(): received[at] = lax.ppermute(sent, 'hi', [(i, i ^ 2) for i in range(4)])]
    all_to_all x3 -> x0, starting transfers between devices: 17.8 us -> none  [the longest x1 7.9 us: body(): rows = lax.all_to_all(rows, 'lo', 0, 0)]
    pallas_call x1, Pallas kernels: 12.5 us -> 2.98 us  [lower_levels(): pl.pallas_call(functools.partial(lower_kernel, levels, first), in_specs=[...]
    pallas_call x1 -> x4, Pallas kernels: 24.8 us -> 17.2 us  [front(): pl.pallas_call(functools.partial(front_kernel, LOCAL_LEVELS), grid_spec=g...]
    ppermute x2 -> x8, starting transfers between devices: 5.74 us -> 12 us  [the longest x4 7.64 us: body(): received[at] = lax.ppermute(sent, 'hi', [(i, i ^ 2) for i in range(4)])]
    unnamed x20 -> x16, local copies, waits for them, and re-layouts: 5.6 us -> 0.04 us
  transfers between devices with their start and end apart: 5 -> 8, of which waited for: 4 -> 2; matrix products, arithmetic and copies ran while one was open for 0% -> 0% of each run, Pallas kernels for 5% -> 13%
where the time goes in v2:
time: 155 us; the launch traced here: 153 us
  blocking collectives  96.1 us (62%)
  Pallas kernels  42.5 us (27%)
  starting transfers between devices  12 us (8%)
  waiting for transfers between devices  1.76 us (1%)
    all_to_all x1, blocking collectives, body(): lax.all_to_all(rows.reshape(n_lower, piece + extra, images * ranks), 'lo'...  36.7 us
    all_to_all x1, blocking collectives, body(): blocks = lax.all_to_all(blocks, 'lo', 0, 0, axis_index_groups=groups)  30.3 us
    all_to_all x1, blocking collectives, body(): lax.all_to_all(rows.reshape(n_lower, piece, images * ranks), 'lo', 0, 0)  29.1 us
    pallas_call x4, Pallas kernels, front(): pl.pallas_call(functools.partial(front_kernel, LOCAL_LEVELS), grid_spec=g...  17.2 us
    pallas_call x1, Pallas kernels, gather_rows(): pl.pallas_call(gather_kernel, in_specs=[pl.BlockSpec(memory_space=pltpu.S...  9.46 us
    ppermute x4, starting transfers between devices, body(): received[at] = lax.ppermute(sent, 'hi', [(i, i ^ 2) for i in range(4)])  7.64 us
    pallas_call x4, Pallas kernels, upper_level(): pl.pallas_call(functools.partial(swap_kernel, level), grid_spec=grid_spec...  6.13 us
    pallas_call x1, Pallas kernels, to_targets(): pl.pallas_call(functools.partial(target_kernel, box_gain.shape[0] - 1), g...  5.07 us
  transfers between devices with their start and end apart: 8, of which 2 were waited for; matrix products, arithmetic and copies ran while one was open for 0% of the time, Pallas kernels for 13%

profile of v2, /device:TPU:1, one launch (start us, length us, event | category | flops | bytes accessed | tf_op | source)
XLA Modules:
  0.0 152.6 jit_solution(2012563090051948795)
XLA Ops:
  0.0 4.3 %source_map_and_local_levels.7 = (bf16[64,2048]{1,0:T(8,128)(2,1)}, bf16[64,2048]{1,0:T(8,128)(2,1)}) custom-call(s32[1]{0:T(128)} %bitcast.2.own_ref, bf16[2,256,8192]{2,1,0:T(8,128)(2,1)} %high_ref.7, bf16[2,256,8192]{2,1,0:T(8,128)(2,1)} %high_ref.7, bf16[64,256]{1,0:T(8,128)(2,1)} %map_ref.7, bf16[15,128,128]{2,1,0:T(8,128)(2,1)} %bitcast.9, ...), custom_call_target="tpu_custom_call" | custom-call | flops 5368709120 | bytes 2097152 | tf_op jit(solution)/shard_map/source_map_and_local_levels/pallas_call | solution.py:71
  4.3 4.4 %collective-permute-start.5 = (bf16[64,2048]{1,0:T(8,128)(2,1)}, bf16[64,2048]{1,0:T(8,128)(2,1)S(1)}, u32[]{:S(2)}, u32[]{:S(2)}) collective-permute-start(bf16[64,2048]{1,0:T(8,128)(2,1)} %get-tuple-element.35), channel_id=1, source_target_pairs={{0,64},{32,96},{64,0},{96,32},{1,65},{33,97},{65,1},{97,33},{2,66}... | collective-permute-start | bytes 786440 | tf_op jit(solution)/shard_map/ppermute | solution.py:334
  8.7 4.3 %source_map_and_local_levels.6 = (bf16[64,2048]{1,0:T(8,128)(2,1)}, bf16[64,2048]{1,0:T(8,128)(2,1)}) custom-call(s32[1]{0:T(128)} %bitcast.2.own_ref, bf16[2,256,8192]{2,1,0:T(8,128)(2,1)} %high_ref.7, bf16[2,256,8192]{2,1,0:T(8,128)(2,1)} %high_ref.7, bf16[64,256]{1,0:T(8,128)(2,1)} %map_ref.7, bf16[15,128,128]{2,1,0:T(8,128)(2,1)} %bitcast.10, ...), custom_call_target="tpu_custom_call" | custom-call | flops 5368709120 | bytes 2097152 | tf_op jit(solution)/shard_map/source_map_and_local_levels/pallas_call | solution.py:71
  13.0 0.0 collective-permute-start.4
  13.0 4.3 %source_map_and_local_levels.5 = (bf16[64,2048]{1,0:T(8,128)(2,1)}, bf16[64,2048]{1,0:T(8,128)(2,1)}) custom-call(s32[1]{0:T(128)} %bitcast.2.own_ref, bf16[2,256,8192]{2,1,0:T(8,128)(2,1)} %high_ref.7, bf16[2,256,8192]{2,1,0:T(8,128)(2,1)} %high_ref.7, bf16[64,256]{1,0:T(8,128)(2,1)} %map_ref.7, bf16[15,128,128]{2,1,0:T(8,128)(2,1)} %bitcast.11, ...), custom_call_target="tpu_custom_call" | custom-call | flops 5368709120 | bytes 2097152 | tf_op jit(solution)/shard_map/source_map_and_local_levels/pallas_call | solution.py:71
  17.4 3.0 %collective-permute-start.1 = (bf16[64,2048]{1,0:T(8,128)(2,1)}, bf16[64,2048]{1,0:T(8,128)(2,1)S(1)}, u32[]{:S(2)}, u32[]{:S(2)}) collective-permute-start(bf16[64,2048]{1,0:T(8,128)(2,1)} %get-tuple-element.27), channel_id=1, source_target_pairs={{0,64},{32,96},{64,0},{96,32},{1,65},{33,97},{65,1},{97,33},{2,66}... | collective-permute-start | bytes 786440 | tf_op jit(solution)/shard_map/ppermute | solution.py:334
  20.4 4.3 %source_map_and_local_levels.4 = (bf16[64,2048]{1,0:T(8,128)(2,1)}, bf16[64,2048]{1,0:T(8,128)(2,1)}) custom-call(s32[1]{0:T(128)} %bitcast.2.own_ref, bf16[2,256,8192]{2,1,0:T(8,128)(2,1)} %high_ref.7, bf16[2,256,8192]{2,1,0:T(8,128)(2,1)} %high_ref.7, bf16[64,256]{1,0:T(8,128)(2,1)} %map_ref.7, bf16[15,128,128]{2,1,0:T(8,128)(2,1)} %bitcast.12, ...), custom_call_target="tpu_custom_call" | custom-call | flops 5368709120 | bytes 2097152 | tf_op jit(solution)/shard_map/source_map_and_local_levels/pallas_call | solution.py:71
  24.7 0.2 collective-permute-start
  24.9 0.1 pad_add_fusion.own_ref
  25.0 0.0 collective-permute-done.5.recv_in
  25.0 1.5 %upper_level.7 = (bf16[64,2048]{1,0:T(8,128)(2,1)S(1)}, bf16[64,2048]{1,0:T(8,128)(2,1)}) custom-call(s32[2]{0:T(128)S(1)} %pad_add_fusion.own_ref, bf16[64,2048]{1,0:T(8,128)(2,1)S(1)} %copy-done.5, bf16[64,2048]{1,0:T(8,128)(2,1)S(1)} %collective-permute-done.5.recv_in, bf16[15,128,128]{2,1,0:T(8,128)(2,1)S(1)} %bitcast.13, f32[15,8192]{1,0:T(8,128)S(1)} %copy-done, ...), custom_call_target="tpu_custom_call" | custom-call | flops 536870912 | bytes 1048576 | tf_op jit(solution)/shard_map/upper_level/pallas_call | solution.py:103
  26.5 1.5 collective-permute-start.7
  28.0 0.0 collective-permute-done.4.recv_in
  28.0 1.5 %upper_level.6 = (bf16[64,2048]{1,0:T(8,128)(2,1)S(1)}, bf16[64,2048]{1,0:T(8,128)(2,1)}) custom-call(s32[2]{0:T(128)S(1)} %pad_add_fusion.own_ref, bf16[64,2048]{1,0:T(8,128)(2,1)S(1)} %copy-done.4, bf16[64,2048]{1,0:T(8,128)(2,1)S(1)} %collective-permute-done.4.recv_in, bf16[15,128,128]{2,1,0:T(8,128)(2,1)S(1)} %bitcast.14, f32[15,8192]{1,0:T(8,128)S(1)} %copy-done, ...), custom_call_target="tpu_custom_call" | custom-call | flops 536870912 | bytes 1048576 | tf_op jit(solution)/shard_map/upper_level/pallas_call | solution.py:103
  29.5 0.0 collective-permute-start.6
  29.5 1.5 %upper_level.5 = (bf16[64,2048]{1,0:T(8,128)(2,1)S(1)}, bf16[64,2048]{1,0:T(8,128)(2,1)}) custom-call(s32[2]{0:T(128)S(1)} %pad_add_fusion.own_ref, bf16[64,2048]{1,0:T(8,128)(2,1)S(1)} %copy-done.3, bf16[64,2048]{1,0:T(8,128)(2,1)S(1)} %collective-permute-done.1.recv_in, bf16[15,128,128]{2,1,0:T(8,128)(2,1)S(1)} %bitcast.15, f32[15,8192]{1,0:T(8,128)S(1)} %copy-done, ...), custom_call_target="tpu_custom_call" | custom-call | flops 536870912 | bytes 1048576 | tf_op jit(solution)/shard_map/upper_level/pallas_call | solution.py:103
  31.0 0.5 collective-permute-start.3
  31.5 1.2 collective-permute-done.recv_in
  32.8 1.5 %upper_level.4 = (bf16[64,2048]{1,0:T(8,128)(2,1)S(1)}, bf16[64,2048]{1,0:T(8,128)(2,1)}) custom-call(s32[2]{0:T(128)S(1)} %pad_add_fusion.own_ref, bf16[64,2048]{1,0:T(8,128)(2,1)S(1)} %copy-done.2, bf16[64,2048]{1,0:T(8,128)(2,1)S(1)} %collective-permute-done.recv_in, bf16[15,128,128]{2,1,0:T(8,128)(2,1)S(1)} %bitcast.16, f32[15,8192]{1,0:T(8,128)S(1)} %copy-done, ...), custom_call_target="tpu_custom_call" | custom-call | flops 536870912 | bytes 1048576 | tf_op jit(solution)/shard_map/upper_level/pallas_call | solution.py:103
  34.3 2.4 %collective-permute-start.2 = (bf16[64,2048]{1,0:T(8,128)(2,1)}, bf16[64,2048]{1,0:T(8,128)(2,1)S(1)}, u32[]{:S(2)}, u32[]{:S(2)}) collective-permute-start(bf16[64,2048]{1,0:T(8,128)(2,1)} %get-tuple-element.29), channel_id=1, source_target_pairs={{0,32},{32,0},{64,96},{96,64},{1,33},{33,1},{65,97},{97,65},{2,34}... | collective-permute-start | bytes 786440 | tf_op jit(solution)/shard_map/ppermute | solution.py:342
  36.7 0.0 collective-permute-done.6.refs_2_
  36.7 0.8 upper_level_to_rows.2.refs_7_
  37.5 0.5 collective-permute-done.2.refs_2_
  38.1 0.8 upper_level_to_rows.3
  38.9 0.0 copy-start.6
  38.9 36.7 %all_to_all.15.rows_ref.gain_ref = bf16[32,272,128]{2,1,0:T(8,128)(2,1)S(1)} all-to-all(bf16[32,272,128]{2,1,0:T(8,128)(2,1)S(1)} %bitcast.8), channel_id=1, replica_groups=mesh['hi'=4,'lo'=32] {'lo'}, dimensions={0} | all-to-all | bytes 4456448 | tf_op jit(solution)/shard_map/all_to_all | solution.py:357
  75.6 9.5 %box_order.1 = bf16[8192,128]{1,0:T(8,128)(2,1)S(1)} custom-call(s32[1,8192]{1,0:T(1,128)S(1)} %copy-done.6, bf16[32,272,128]{2,1,0:T(8,128)(2,1)S(1)} %all_to_all.15.rows_ref.gain_ref), custom_call_target="tpu_custom_call" | custom-call | bytes 31457280 | tf_op jit(solution)/shard_map/box_order/pallas_call | solution.py:201
  85.1 29.1 %all_to_all.16.x_ref = bf16[32,256,128]{2,1,0:T(8,128)(2,1)S(1)} all-to-all(bf16[32,256,128]{2,1,0:T(8,128)(2,1)S(1)} %bitcast.20), channel_id=1, replica_groups=mesh['hi'=4,'lo'=32] {'lo'}, dimensions={0} | all-to-all | bytes 4194304 | tf_op jit(solution)/shard_map/all_to_all | solution.py:359
  114.2 3.0 %lower_levels.1 = bf16[32,2,64,256]{3,2,1,0:T(8,128)(2,1)S(1)} custom-call(s32[1]{0:T(128)} %bitcast.own_ref, bf16[32,256,128]{2,1,0:T(8,128)(2,1)S(1)} %all_to_all.16.x_ref, bf16[15,128,128]{2,1,0:T(8,128)(2,1)S(1)} %bitcast.19, bf16[32,272,128]{2,1,0:T(8,128)(2,1)S(1)} %all_to_all.15.rows_ref.gain_ref), custom_call_target="tpu_custom_call" | custom-call | flops 10737418240 | bytes 4194304 | tf_op jit(solution)/shard_map/lower_levels/pallas_call | solution.py:267
  117.2 0.0 copy-start.7
  117.2 30.3 %all_to_all.17.x_ref = bf16[16,2,2,64,256]{4,3,2,1,0:T(8,128)(2,1)S(1)} all-to-all(bf16[16,2,2,64,256]{4,3,2,1,0:T(8,128)(2,1)S(1)} %bitcast.21), channel_id=1, replica_groups={{0,1,2,3,4,5,6,7,8,9,10,11,12,13,14,15},{16,17,18,19,20,21,22,23,24,25,..., dimensions={0} | all-to-all | bytes 4194304 | tf_op jit(solution)/shard_map/all_to_all | solution.py:362
  147.5 5.1 %target_map.1 = bf16[2,256,8192]{2,1,0:T(8,128)(2,1)} custom-call(bf16[16,2,2,64,256]{4,3,2,1,0:T(8,128)(2,1)S(1)} %all_to_all.17.x_ref, bf16[64,256]{1,0:T(8,128)(2,1)S(1)} %bitcast.22, f32[15,8192]{1,0:T(8,128)S(1)} %copy-done), custom_call_target="tpu_custom_call" | custom-call | flops 2147483648 | bytes 8388608 | tf_op jit(solution)/shard_map/target_map/pallas_call | solution.py:297
  (17 shorter events, 0.0 us)
Async XLA Ops:
  4.3 20.7 %collective-permute-start.5 = (bf16[64,2048]{1,0:T(8,128)(2,1)}, bf16[64,2048]{1,0:T(8,128)(2,1)S(1)}, u32[]{:S(2)}, u32[]{:S(2)}) collective-permute-start(bf16[64,2048]{1,0:T(8,128)(2,1)} %get-tuple-element.35), channel_id=1, source_target_pairs={{0,64},{32,96},{64,0},{96,32},{1,65},{33,97},{65,1},{97,33},{2,66}... | collective-permute-start | bytes 786440 | tf_op jit(solution)/shard_map/ppermute | solution.py:334
  13.0 14.9 %collective-permute-start.4 = (bf16[64,2048]{1,0:T(8,128)(2,1)}, bf16[64,2048]{1,0:T(8,128)(2,1)S(1)}, u32[]{:S(2)}, u32[]{:S(2)}) collective-permute-start(bf16[64,2048]{1,0:T(8,128)(2,1)} %get-tuple-element.32), channel_id=1, source_target_pairs={{0,64},{32,96},{64,0},{96,32},{1,65},{33,97},{65,1},{97,33},{2,66}... | collective-permute-start | bytes 786440 | tf_op jit(solution)/shard_map/ppermute | solution.py:334
  17.4 7.6 %copy-start = (f32[15,8192]{1,0:T(8,128)S(1)}, f32[15,8192]{1,0:T(8,128)}, u32[]{:S(2)}) copy-start(f32[15,8192]{1,0:T(8,128)} %gain_ref.1) | copy-start | bytes 1474564
  17.4 7.6 %copy-start.1 = (bf16[15,2,64,128]{3,2,1,0:T(8,128)(2,1)S(1)}, bf16[15,2,64,128]{3,2,1,0:T(8,128)(2,1)}, u32[]{:S(2)}) copy-start(bf16[15,2,64,128]{3,2,1,0:T(8,128)(2,1)} %param.8) | copy-start | bytes 1474564
  17.4 7.6 %copy-start.5 = (bf16[64,2048]{1,0:T(8,128)(2,1)S(1)}, bf16[64,2048]{1,0:T(8,128)(2,1)}, u32[]{:S(2)}) copy-start(bf16[64,2048]{1,0:T(8,128)(2,1)} %get-tuple-element.34.kept_in) | copy-start | bytes 786436
  17.4 10.6 %copy-start.4 = (bf16[64,2048]{1,0:T(8,128)(2,1)S(1)}, bf16[64,2048]{1,0:T(8,128)(2,1)}, u32[]{:S(2)}) copy-start(bf16[64,2048]{1,0:T(8,128)(2,1)} %get-tuple-element.31.kept_in) | copy-start | bytes 786436
  17.4 12.1 %collective-permute-start.1 = (bf16[64,2048]{1,0:T(8,128)(2,1)}, bf16[64,2048]{1,0:T(8,128)(2,1)S(1)}, u32[]{:S(2)}, u32[]{:S(2)}) collective-permute-start(bf16[64,2048]{1,0:T(8,128)(2,1)} %get-tuple-element.27), channel_id=1, source_target_pairs={{0,64},{32,96},{64,0},{96,32},{1,65},{33,97},{65,1},{97,33},{2,66}... | collective-permute-start | bytes 786440 | tf_op jit(solution)/shard_map/ppermute | solution.py:334
  24.7 4.8 %copy-start.3 = (bf16[64,2048]{1,0:T(8,128)(2,1)S(1)}, bf16[64,2048]{1,0:T(8,128)(2,1)}, u32[]{:S(2)}) copy-start(bf16[64,2048]{1,0:T(8,128)(2,1)} %get-tuple-element.26.kept_in) | copy-start | bytes 786436
  24.7 8.0 %collective-permute-start = (bf16[64,2048]{1,0:T(8,128)(2,1)}, bf16[64,2048]{1,0:T(8,128)(2,1)S(1)}, u32[]{:S(2)}, u32[]{:S(2)}) collective-permute-start(bf16[64,2048]{1,0:T(8,128)(2,1)} %get-tuple-element.24), channel_id=1, source_target_pairs={{0,64},{32,96},{64,0},{96,32},{1,65},{33,97},{65,1},{97,33},{2,66}... | collective-permute-start | bytes 786440 | tf_op jit(solution)/shard_map/ppermute | solution.py:334
  26.5 6.3 %copy-start.2 = (bf16[64,2048]{1,0:T(8,128)(2,1)S(1)}, bf16[64,2048]{1,0:T(8,128)(2,1)}, u32[]{:S(2)}) copy-start(bf16[64,2048]{1,0:T(8,128)(2,1)} %get-tuple-element.23.kept_in) | copy-start | bytes 786436
  26.5 10.2 %collective-permute-start.7 = (bf16[64,2048]{1,0:T(8,128)(2,1)}, bf16[64,2048]{1,0:T(8,128)(2,1)S(1)}, u32[]{:S(2)}, u32[]{:S(2)}) collective-permute-start(bf16[64,2048]{1,0:T(8,128)(2,1)} %get-tuple-element.38), channel_id=1, source_target_pairs={{0,32},{32,0},{64,96},{96,64},{1,33},{33,1},{65,97},{97,65},{2,34}... | collective-permute-start | bytes 786440 | tf_op jit(solution)/shard_map/ppermute | solution.py:342
  29.5 7.2 %collective-permute-start.6 = (bf16[64,2048]{1,0:T(8,128)(2,1)}, bf16[64,2048]{1,0:T(8,128)(2,1)S(1)}, u32[]{:S(2)}, u32[]{:S(2)}) collective-permute-start(bf16[64,2048]{1,0:T(8,128)(2,1)} %get-tuple-element.37), channel_id=1, source_target_pairs={{0,32},{32,0},{64,96},{96,64},{1,33},{33,1},{65,97},{97,65},{2,34}... | collective-permute-start | bytes 786440 | tf_op jit(solution)/shard_map/ppermute | solution.py:342
  31.0 6.5 %collective-permute-start.3 = (bf16[64,2048]{1,0:T(8,128)(2,1)}, bf16[64,2048]{1,0:T(8,128)(2,1)S(1)}, u32[]{:S(2)}, u32[]{:S(2)}) collective-permute-start(bf16[64,2048]{1,0:T(8,128)(2,1)} %get-tuple-element.30), channel_id=1, source_target_pairs={{0,32},{32,0},{64,96},{96,64},{1,33},{33,1},{65,97},{97,65},{2,34}... | collective-permute-start | bytes 786440 | tf_op jit(solution)/shard_map/ppermute | solution.py:342
  34.3 3.8 %collective-permute-start.2 = (bf16[64,2048]{1,0:T(8,128)(2,1)}, bf16[64,2048]{1,0:T(8,128)(2,1)S(1)}, u32[]{:S(2)}, u32[]{:S(2)}) collective-permute-start(bf16[64,2048]{1,0:T(8,128)(2,1)} %get-tuple-element.29), channel_id=1, source_target_pairs={{0,32},{32,0},{64,96},{96,64},{1,33},{33,1},{65,97},{97,65},{2,34}... | collective-permute-start | bytes 786440 | tf_op jit(solution)/shard_map/ppermute | solution.py:342
  38.9 36.7 %copy-start.6 = (s32[1,8192]{1,0:T(1,128)S(1)}, s32[1,8192]{1,0:T(1,128)}, u32[]{:S(2)}) copy-start(s32[1,8192]{1,0:T(1,128)} %order_ref.1) | copy-start | bytes 98308
  117.2 30.3 %copy-start.7 = (bf16[256,64]{0,1:T(8,128)(2,1)S(1)}, bf16[256,64]{0,1:T(8,128)(2,1)}, u32[]{:S(2)}) copy-start(bf16[256,64]{0,1:T(8,128)(2,1)} %param.11) | copy-start | bytes 98308

commit v3 on v2

--- a/solution.py
+++ b/solution.py
@@ -13,6 +13,7 @@
 VMEM_LIMIT = 40 * 2**20
 FRONT_LIMIT = 56 * 2**20
 PARTS = 2
+TURN_STEPS = 2
 
 
 def dot(a, b):
@@ -166,7 +167,7 @@
     )(owns, *kept, *received, matrices, box_gain, box_gain, *more)
 
 
-UNROLL = 32
+UNROLL = 128
 
 
 def gather_kernel(order_ref, rows_ref, out_ref, table, picked):
@@ -332,13 +333,14 @@
             at = part, c
             kept[at], sent = front(c, part, PARTS, owns[:1], sources, source_map, matrices, box_gain)
             received[at] = lax.ppermute(sent, "hi", [(i, i ^ 2) for i in range(4)])
-    rows = None
+    rows, turn = None, own_half
     for part in range(PARTS):
         for c in range(images):
             at = part, c
             kept[at], sent = upper_level(
                 LOCAL_LEVELS, part, PARTS, owns, kept[at], received[at], matrices, box_gain
             )
+            turn, sent = lax.optimization_barrier((turn, sent))
             received[at] = lax.ppermute(sent, "hi", [(i, i ^ 1) for i in range(4)])
         rows = rows_level(
             LOCAL_LEVELS + 1,
@@ -353,7 +355,9 @@
             extra,
             rows,
         )
-    own_half, rows = lax.optimization_barrier((own_half, rows))
+    for _ in range(TURN_STEPS):
+        turn = lax.ppermute(turn, "hi", [(1, 3), (3, 1)])
+    own_half, rows = lax.optimization_barrier((jnp.where(owns[1:] == 0, own_half, turn), rows))
     moved = lax.all_to_all(rows.reshape(n_lower, piece + extra, images * ranks), "lo", 0, 0)
     rows = gather_rows(target_order, moved)
     rows = lax.all_to_all(rows.reshape(n_lower, piece, images * ranks), "lo", 0, 0)

time: 155 us -> 149 us (0.961); the launches traced: 153 us -> 148 us
  blocking collectives: 96.1 us -> 81.5 us
  starting transfers between devices: 12 us -> 19.1 us
  waiting for transfers between devices: 1.76 us -> 8.03 us
  Pallas kernels: 42.5 us -> 38.8 us
    ppermute x0 -> x2, starting transfers between devices: none -> 7.1 us  [body(): turn = lax.ppermute(turn, 'hi', [(1, 3), (3, 1)])]
    all_to_all x1, blocking collectives: 36.7 us -> 30 us  [body(): lax.all_to_all(rows.reshape(n_lower, piece + extra, images * ranks), 'lo'...]
    ppermute x0 -> x2, waiting for transfers between devices: none -> 4.56 us  [body(): turn = lax.ppermute(turn, 'hi', [(1, 3), (3, 1)])]
    all_to_all x1, blocking collectives: 29.1 us -> 24.8 us  [body(): lax.all_to_all(rows.reshape(n_lower, piece, images * ranks), 'lo', 0, 0)]
    all_to_all x1, blocking collectives: 30.3 us -> 26.8 us  [body(): blocks = lax.all_to_all(blocks, 'lo', 0, 0, axis_index_groups=groups)]
    pallas_call x4, Pallas kernels: 6.13 us -> 3.35 us  [upper_level(): pl.pallas_call(functools.partial(swap_kernel, level), grid_spec=grid_spec...]
    ppermute x4, waiting for transfers between devices: 1.21 us -> 3.46 us  [body(): received[at] = lax.ppermute(sent, 'hi', [(i, i ^ 2) for i in range(4)])]
  transfers between devices with their start and end apart: 8 -> 10, of which waited for: 2 -> 4; matrix products, arithmetic and copies ran while one was open for 0% -> 0% of each run, Pallas kernels for 13% -> 12%
where the time goes in v3:
time: 149 us; the launch traced here: 148 us
  blocking collectives  81.5 us (55%)
  Pallas kernels  38.8 us (26%)
  starting transfers between devices  19.1 us (13%)
  waiting for transfers between devices  8.03 us (5%)
    all_to_all x1, blocking collectives, body(): lax.all_to_all(rows.reshape(n_lower, piece + extra, images * ranks), 'lo'...  30 us
    all_to_all x1, blocking collectives, body(): blocks = lax.all_to_all(blocks, 'lo', 0, 0, axis_index_groups=groups)  26.8 us
    all_to_all x1, blocking collectives, body(): lax.all_to_all(rows.reshape(n_lower, piece, images * ranks), 'lo', 0, 0)  24.8 us
    pallas_call x4, Pallas kernels, front(): pl.pallas_call(functools.partial(front_kernel, LOCAL_LEVELS), grid_spec=g...  17.2 us
    pallas_call x1, Pallas kernels, gather_rows(): pl.pallas_call(gather_kernel, in_specs=[pl.BlockSpec(memory_space=pltpu.S...  8.55 us
    ppermute x4, starting transfers between devices, body(): received[at] = lax.ppermute(sent, 'hi', [(i, i ^ 2) for i in range(4)])  7.64 us
    ppermute x2, starting transfers between devices, body(): turn = lax.ppermute(turn, 'hi', [(1, 3), (3, 1)])  7.1 us
    pallas_call x1, Pallas kernels, to_targets(): pl.pallas_call(functools.partial(target_kernel, box_gain.shape[0] - 1), g...  5.07 us
  transfers between devices with their start and end apart: 10, of which 4 were waited for; matrix products, arithmetic and copies ran while one was open for 0% of the time, Pallas kernels for 12%

profile of v3, /device:TPU:1, one launch (start us, length us, event | category | flops | bytes accessed | tf_op | source)
XLA Modules:
  0.0 148.3 jit_solution(6330924318622849792)
XLA Ops:
  0.0 4.3 %source_map_and_local_levels.6 = (bf16[64,2048]{1,0:T(8,128)(2,1)}, bf16[64,2048]{1,0:T(8,128)(2,1)}) custom-call(s32[1]{0:T(128)} %bitcast.2.own_ref, bf16[2,256,8192]{2,1,0:T(8,128)(2,1)} %high_ref.7, bf16[2,256,8192]{2,1,0:T(8,128)(2,1)} %high_ref.7, bf16[64,256]{1,0:T(8,128)(2,1)} %map_ref.7, bf16[15,128,128]{2,1,0:T(8,128)(2,1)} %bitcast.9, ...), custom_call_target="tpu_custom_call" | custom-call | flops 5368709120 | bytes 2097152 | tf_op jit(solution)/shard_map/source_map_and_local_levels/pallas_call | solution.py:72
  4.3 4.4 %collective-permute-start.2 = (bf16[64,2048]{1,0:T(8,128)(2,1)}, bf16[64,2048]{1,0:T(8,128)(2,1)S(1)}, u32[]{:S(2)}, u32[]{:S(2)}) collective-permute-start(bf16[64,2048]{1,0:T(8,128)(2,1)} %get-tuple-element.40), channel_id=1, source_target_pairs={{0,64},{32,96},{64,0},{96,32},{1,65},{33,97},{65,1},{97,33},{2,66}... | collective-permute-start | bytes 786440 | tf_op jit(solution)/shard_map/ppermute | solution.py:335
  8.7 4.3 %source_map_and_local_levels.5 = (bf16[64,2048]{1,0:T(8,128)(2,1)}, bf16[64,2048]{1,0:T(8,128)(2,1)}) custom-call(s32[1]{0:T(128)} %bitcast.2.own_ref, bf16[2,256,8192]{2,1,0:T(8,128)(2,1)} %high_ref.7, bf16[2,256,8192]{2,1,0:T(8,128)(2,1)} %high_ref.7, bf16[64,256]{1,0:T(8,128)(2,1)} %map_ref.7, bf16[15,128,128]{2,1,0:T(8,128)(2,1)} %bitcast.10, ...), custom_call_target="tpu_custom_call" | custom-call | flops 5368709120 | bytes 2097152 | tf_op jit(solution)/shard_map/source_map_and_local_levels/pallas_call | solution.py:72
  13.0 4.3 %source_map_and_local_levels.4 = (bf16[64,2048]{1,0:T(8,128)(2,1)}, bf16[64,2048]{1,0:T(8,128)(2,1)}) custom-call(s32[1]{0:T(128)} %bitcast.2.own_ref, bf16[2,256,8192]{2,1,0:T(8,128)(2,1)} %high_ref.7, bf16[2,256,8192]{2,1,0:T(8,128)(2,1)} %high_ref.7, bf16[64,256]{1,0:T(8,128)(2,1)} %map_ref.7, bf16[15,128,128]{2,1,0:T(8,128)(2,1)} %bitcast.11, ...), custom_call_target="tpu_custom_call" | custom-call | flops 5368709120 | bytes 2097152 | tf_op jit(solution)/shard_map/source_map_and_local_levels/pallas_call | solution.py:72
  17.3 3.0 %collective-permute-start = (bf16[64,2048]{1,0:T(8,128)(2,1)}, bf16[64,2048]{1,0:T(8,128)(2,1)S(1)}, u32[]{:S(2)}, u32[]{:S(2)}) collective-permute-start(bf16[64,2048]{1,0:T(8,128)(2,1)} %get-tuple-element.32), channel_id=1, source_target_pairs={{0,64},{32,96},{64,0},{96,32},{1,65},{33,97},{65,1},{97,33},{2,66}... | collective-permute-start | bytes 786440 | tf_op jit(solution)/shard_map/ppermute | solution.py:335
  20.3 4.3 %source_map_and_local_levels.7 = (bf16[64,2048]{1,0:T(8,128)(2,1)}, bf16[64,2048]{1,0:T(8,128)(2,1)}) custom-call(s32[1]{0:T(128)} %bitcast.2.own_ref, bf16[2,256,8192]{2,1,0:T(8,128)(2,1)} %high_ref.7, bf16[2,256,8192]{2,1,0:T(8,128)(2,1)} %high_ref.7, bf16[64,256]{1,0:T(8,128)(2,1)} %map_ref.7, bf16[15,128,128]{2,1,0:T(8,128)(2,1)} %bitcast.12, ...), custom_call_target="tpu_custom_call" | custom-call | flops 5368709120 | bytes 2097152 | tf_op jit(solution)/shard_map/source_map_and_local_levels/pallas_call | solution.py:72
  24.7 0.2 collective-permute-start.3
  24.8 0.1 pad_add_fusion.own_ref
  24.9 2.6 %collective-permute-done.recv_in = bf16[64,2048]{1,0:T(8,128)(2,1)S(1)} collective-permute-done((bf16[64,2048]{1,0:T(8,128)(2,1)}, bf16[64,2048]{1,0:T(8,128)(2,1)S(1)}, u32[]{:S(2)}, u32[]{:S(2)}) %collective-permute-start) | collective-permute-done | bytes 262176 | tf_op jit(solution)/shard_map/ppermute | solution.py:335
  27.5 0.8 upper_level.4
  28.4 0.8 upper_level.5
  29.2 1.6 %collective-permute-start.9 = (bf16[64,2048]{1,0:T(8,128)(2,1)S(1)}, bf16[64,2048]{1,0:T(8,128)(2,1)S(1)}, u32[]{:S(2)}, u32[]{:S(2)}) collective-permute-start(bf16[64,2048]{1,0:T(8,128)(2,1)S(1)} %get-tuple-element.54), channel_id=1, source_target_pairs={{0,32},{32,0},{64,96},{96,64},{1,33},{33,1},{65,97},{97,65},{2,34}... | collective-permute-start | bytes 786440 | tf_op jit(solution)/shard_map/ppermute | solution.py:344
  30.9 0.1 collective-permute-start.8
  31.0 0.8 upper_level.6
  31.8 0.9 collective-permute-done.3.recv_in
  32.7 0.8 upper_level.7
  33.5 2.5 %collective-permute-start.7 = (bf16[64,2048]{1,0:T(8,128)(2,1)S(1)}, bf16[64,2048]{1,0:T(8,128)(2,1)S(1)}, u32[]{:S(2)}, u32[]{:S(2)}) collective-permute-start(bf16[64,2048]{1,0:T(8,128)(2,1)S(1)} %get-tuple-element.50), channel_id=1, source_target_pairs={{0,32},{32,0},{64,96},{96,64},{1,33},{33,1},{65,97},{97,65},{2,34}... | collective-permute-start | bytes 786440 | tf_op jit(solution)/shard_map/ppermute | solution.py:344
  36.0 0.1 collective-permute-start.6
  36.1 3.9 %collective-permute-start.4 = (s32[1]{0:T(128)}, s32[1]{0:T(128)}, u32[]{:S(2)}, u32[]{:S(2)}) collective-permute-start(s32[1]{0:T(128)} %bitcast.1), channel_id=1, source_target_pairs={{32,96},{96,32},{33,97},{97,33},{34,98},{98,34},{35,99},{99,35},{3... | collective-permute-start | bytes 20 | tf_op jit(solution)/shard_map/ppermute | solution.py:359
  40.0 1.8 %collective-permute-done.4 = s32[1]{0:T(128)} collective-permute-done((s32[1]{0:T(128)}, s32[1]{0:T(128)}, u32[]{:S(2)}, u32[]{:S(2)}) %collective-permute-start.4) | collective-permute-done | bytes 36 | tf_op jit(solution)/shard_map/ppermute | solution.py:359
  41.9 3.2 %collective-permute-start.5 = (s32[1]{0:T(128)}, s32[1]{0:T(128)}, u32[]{:S(2)}, u32[]{:S(2)}) collective-permute-start(s32[1]{0:T(128)} %collective-permute-done.4), channel_id=1, source_target_pairs={{32,96},{96,32},{33,97},{97,33},{34,98},{98,34},{35,99},{99,35},{3... | collective-permute-start | bytes 20 | tf_op jit(solution)/shard_map/ppermute | solution.py:359
  45.1 2.7 %collective-permute-done.5 = s32[1]{0:T(128)} collective-permute-done((s32[1]{0:T(128)}, s32[1]{0:T(128)}, u32[]{:S(2)}, u32[]{:S(2)}) %collective-permute-start.5) | collective-permute-done | bytes 36 | tf_op jit(solution)/shard_map/ppermute | solution.py:359
  48.5 0.8 upper_level_to_rows.2.refs_7_
  49.4 0.8 upper_level_to_rows.3
  50.2 0.0 copy-start.6
  50.2 30.0 %all_to_all.15.rows_ref.gain_ref = bf16[32,272,128]{2,1,0:T(8,128)(2,1)S(1)} all-to-all(bf16[32,272,128]{2,1,0:T(8,128)(2,1)S(1)} %bitcast.8), channel_id=1, replica_groups=mesh['hi'=4,'lo'=32] {'lo'}, dimensions={0} | all-to-all | bytes 4456448 | tf_op jit(solution)/shard_map/all_to_all | solution.py:361
  80.2 8.5 %box_order.1 = bf16[8192,128]{1,0:T(8,128)(2,1)S(1)} custom-call(s32[1,8192]{1,0:T(1,128)S(1)} %copy-done.6, bf16[32,272,128]{2,1,0:T(8,128)(2,1)S(1)} %all_to_all.15.rows_ref.gain_ref), custom_call_target="tpu_custom_call" | custom-call | bytes 31457280 | tf_op jit(solution)/shard_map/box_order/pallas_call | solution.py:202
  88.7 24.8 %all_to_all.16.x_ref = bf16[32,256,128]{2,1,0:T(8,128)(2,1)S(1)} all-to-all(bf16[32,256,128]{2,1,0:T(8,128)(2,1)S(1)} %bitcast.20), channel_id=1, replica_groups=mesh['hi'=4,'lo'=32] {'lo'}, dimensions={0} | all-to-all | bytes 4194304 | tf_op jit(solution)/shard_map/all_to_all | solution.py:363
  113.5 3.0 %lower_levels.1 = bf16[32,2,64,256]{3,2,1,0:T(8,128)(2,1)S(1)} custom-call(s32[1]{0:T(128)S(6)} %select_n.4.own_ref, bf16[32,256,128]{2,1,0:T(8,128)(2,1)S(1)} %all_to_all.16.x_ref, bf16[15,128,128]{2,1,0:T(8,128)(2,1)S(1)} %bitcast.19, bf16[32,272,128]{2,1,0:T(8,128)(2,1)S(1)} %all_to_all.15.rows_ref.gain_ref), custom_call_target="tpu_custom_call" | custom-call | flops 10737418240 | bytes 4194304 | tf_op jit(solution)/shard_map/lower_levels/pallas_call | solution.py:268
  116.5 0.0 copy-start.7
  116.5 26.8 %all_to_all.17.x_ref = bf16[16,2,2,64,256]{4,3,2,1,0:T(8,128)(2,1)S(1)} all-to-all(bf16[16,2,2,64,256]{4,3,2,1,0:T(8,128)(2,1)S(1)} %bitcast.21), channel_id=1, replica_groups={{0,1,2,3,4,5,6,7,8,9,10,11,12,13,14,15},{16,17,18,19,20,21,22,23,24,25,..., dimensions={0} | all-to-all | bytes 4194304 | tf_op jit(solution)/shard_map/all_to_all | solution.py:366
  143.3 5.1 %target_map.1 = bf16[2,256,8192]{2,1,0:T(8,128)(2,1)} custom-call(bf16[16,2,2,64,256]{4,3,2,1,0:T(8,128)(2,1)S(1)} %all_to_all.17.x_ref, bf16[64,256]{1,0:T(8,128)(2,1)S(1)} %bitcast.22, f32[15,8192]{1,0:T(8,128)S(1)} %copy-done), custom_call_target="tpu_custom_call" | custom-call | flops 2147483648 | bytes 8388608 | tf_op jit(solution)/shard_map/target_map/pallas_call | solution.py:298
  (21 shorter events, 0.0 us)
Async XLA Ops:
  4.3 26.7 %collective-permute-start.2 = (bf16[64,2048]{1,0:T(8,128)(2,1)}, bf16[64,2048]{1,0:T(8,128)(2,1)S(1)}, u32[]{:S(2)}, u32[]{:S(2)}) collective-permute-start(bf16[64,2048]{1,0:T(8,128)(2,1)} %get-tuple-element.40), channel_id=1, source_target_pairs={{0,64},{32,96},{64,0},{96,32},{1,65},{33,97},{65,1},{97,33},{2,66}... | collective-permute-start | bytes 786440 | tf_op jit(solution)/shard_map/ppermute | solution.py:335
  13.0 15.4 %collective-permute-start.1 = (bf16[64,2048]{1,0:T(8,128)(2,1)}, bf16[64,2048]{1,0:T(8,128)(2,1)S(1)}, u32[]{:S(2)}, u32[]{:S(2)}) collective-permute-start(bf16[64,2048]{1,0:T(8,128)(2,1)} %get-tuple-element.36), channel_id=1, source_target_pairs={{0,64},{32,96},{64,0},{96,32},{1,65},{33,97},{65,1},{97,33},{2,66}... | collective-permute-start | bytes 786440 | tf_op jit(solution)/shard_map/ppermute | solution.py:335
  17.3 10.2 %copy-start = (f32[15,8192]{1,0:T(8,128)S(1)}, f32[15,8192]{1,0:T(8,128)}, u32[]{:S(2)}) copy-start(f32[15,8192]{1,0:T(8,128)} %gain_ref.1) | copy-start | bytes 1474564
  17.3 10.2 %copy-start.1 = (bf16[15,2,64,128]{3,2,1,0:T(8,128)(2,1)S(1)}, bf16[15,2,64,128]{3,2,1,0:T(8,128)(2,1)}, u32[]{:S(2)}) copy-start(bf16[15,2,64,128]{3,2,1,0:T(8,128)(2,1)} %param.8) | copy-start | bytes 1474564
  17.3 10.2 %copy-start.5 = (bf16[64,2048]{1,0:T(8,128)(2,1)S(1)}, bf16[64,2048]{1,0:T(8,128)(2,1)}, u32[]{:S(2)}) copy-start(bf16[64,2048]{1,0:T(8,128)(2,1)} %get-tuple-element.31.kept_in) | copy-start | bytes 786436
  17.3 11.1 %copy-start.4 = (bf16[64,2048]{1,0:T(8,128)(2,1)S(1)}, bf16[64,2048]{1,0:T(8,128)(2,1)}, u32[]{:S(2)}) copy-start(bf16[64,2048]{1,0:T(8,128)(2,1)} %get-tuple-element.35.kept_in) | copy-start | bytes 786436
  17.3 10.2 %collective-permute-start = (bf16[64,2048]{1,0:T(8,128)(2,1)}, bf16[64,2048]{1,0:T(8,128)(2,1)S(1)}, u32[]{:S(2)}, u32[]{:S(2)}) collective-permute-start(bf16[64,2048]{1,0:T(8,128)(2,1)} %get-tuple-element.32), channel_id=1, source_target_pairs={{0,64},{32,96},{64,0},{96,32},{1,65},{33,97},{65,1},{97,33},{2,66}... | collective-permute-start | bytes 786440 | tf_op jit(solution)/shard_map/ppermute | solution.py:335
  24.7 6.3 %copy-start.2 = (bf16[64,2048]{1,0:T(8,128)(2,1)S(1)}, bf16[64,2048]{1,0:T(8,128)(2,1)}, u32[]{:S(2)}) copy-start(bf16[64,2048]{1,0:T(8,128)(2,1)} %get-tuple-element.39.kept_in) | copy-start | bytes 786436
  24.7 8.0 %collective-permute-start.3 = (bf16[64,2048]{1,0:T(8,128)(2,1)}, bf16[64,2048]{1,0:T(8,128)(2,1)S(1)}, u32[]{:S(2)}, u32[]{:S(2)}) collective-permute-start(bf16[64,2048]{1,0:T(8,128)(2,1)} %get-tuple-element.44), channel_id=1, source_target_pairs={{0,64},{32,96},{64,0},{96,32},{1,65},{33,97},{65,1},{97,33},{2,66}... | collective-permute-start | bytes 786440 | tf_op jit(solution)/shard_map/ppermute | solution.py:335
  28.3 4.3 %copy-start.3 = (bf16[64,2048]{1,0:T(8,128)(2,1)S(1)}, bf16[64,2048]{1,0:T(8,128)(2,1)}, u32[]{:S(2)}) copy-start(bf16[64,2048]{1,0:T(8,128)(2,1)} %get-tuple-element.43.kept_in) | copy-start | bytes 786436
  29.2 19.3 %collective-permute-start.9 = (bf16[64,2048]{1,0:T(8,128)(2,1)S(1)}, bf16[64,2048]{1,0:T(8,128)(2,1)S(1)}, u32[]{:S(2)}, u32[]{:S(2)}) collective-permute-start(bf16[64,2048]{1,0:T(8,128)(2,1)S(1)} %get-tuple-element.54), channel_id=1, source_target_pairs={{0,32},{32,0},{64,96},{96,64},{1,33},{33,1},{65,97},{97,65},{2,34}... | collective-permute-start | bytes 786440 | tf_op jit(solution)/shard_map/ppermute | solution.py:344
  30.9 17.7 %collective-permute-start.8 = (bf16[64,2048]{1,0:T(8,128)(2,1)S(1)}, bf16[64,2048]{1,0:T(8,128)(2,1)S(1)}, u32[]{:S(2)}, u32[]{:S(2)}) collective-permute-start(bf16[64,2048]{1,0:T(8,128)(2,1)S(1)} %get-tuple-element.53), channel_id=1, source_target_pairs={{0,32},{32,0},{64,96},{96,64},{1,33},{33,1},{65,97},{97,65},{2,34}... | collective-permute-start | bytes 786440 | tf_op jit(solution)/shard_map/ppermute | solution.py:344
  33.5 15.8 %collective-permute-start.7 = (bf16[64,2048]{1,0:T(8,128)(2,1)S(1)}, bf16[64,2048]{1,0:T(8,128)(2,1)S(1)}, u32[]{:S(2)}, u32[]{:S(2)}) collective-permute-start(bf16[64,2048]{1,0:T(8,128)(2,1)S(1)} %get-tuple-element.50), channel_id=1, source_target_pairs={{0,32},{32,0},{64,96},{96,64},{1,33},{33,1},{65,97},{97,65},{2,34}... | collective-permute-start | bytes 786440 | tf_op jit(solution)/shard_map/ppermute | solution.py:344
  36.0 13.3 %collective-permute-start.6 = (bf16[64,2048]{1,0:T(8,128)(2,1)S(1)}, bf16[64,2048]{1,0:T(8,128)(2,1)S(1)}, u32[]{:S(2)}, u32[]{:S(2)}) collective-permute-start(bf16[64,2048]{1,0:T(8,128)(2,1)S(1)} %get-tuple-element.49), channel_id=1, source_target_pairs={{0,32},{32,0},{64,96},{96,64},{1,33},{33,1},{65,97},{97,65},{2,34}... | collective-permute-start | bytes 786440 | tf_op jit(solution)/shard_map/ppermute | solution.py:344
  36.1 5.7 %collective-permute-start.4 = (s32[1]{0:T(128)}, s32[1]{0:T(128)}, u32[]{:S(2)}, u32[]{:S(2)}) collective-permute-start(s32[1]{0:T(128)} %bitcast.1), channel_id=1, source_target_pairs={{32,96},{96,32},{33,97},{97,33},{34,98},{98,34},{35,99},{99,35},{3... | collective-permute-start | bytes 20 | tf_op jit(solution)/shard_map/ppermute | solution.py:359
  41.9 5.9 %collective-permute-start.5 = (s32[1]{0:T(128)}, s32[1]{0:T(128)}, u32[]{:S(2)}, u32[]{:S(2)}) collective-permute-start(s32[1]{0:T(128)} %collective-permute-done.4), channel_id=1, source_target_pairs={{32,96},{96,32},{33,97},{97,33},{34,98},{98,34},{35,99},{99,35},{3... | collective-permute-start | bytes 20 | tf_op jit(solution)/shard_map/ppermute | solution.py:359
  50.2 30.0 %copy-start.6 = (s32[1,8192]{1,0:T(1,128)S(1)}, s32[1,8192]{1,0:T(1,128)}, u32[]{:S(2)}) copy-start(s32[1,8192]{1,0:T(1,128)} %order_ref.1) | copy-start | bytes 98308
  116.5 26.8 %copy-start.7 = (bf16[256,64]{0,1:T(8,128)(2,1)S(1)}, bf16[256,64]{0,1:T(8,128)(2,1)}, u32[]{:S(2)}) copy-start(bf16[256,64]{0,1:T(8,128)(2,1)} %param.11) | copy-start | bytes 98308

commit v4 on v3

--- a/solution.py
+++ b/solution.py
@@ -12,8 +12,9 @@
 BF16 = jnp.bfloat16
 VMEM_LIMIT = 40 * 2**20
 FRONT_LIMIT = 56 * 2**20
-PARTS = 2
+PARTS = 1
 TURN_STEPS = 2
+PARTNER = 66
 
 
 def dot(a, b):
@@ -355,8 +356,9 @@
             extra,
             rows,
         )
+    over_zx = [(d, d ^ PARTNER) for d in range(4 * n_lower) if d & n_lower]
     for _ in range(TURN_STEPS):
-        turn = lax.ppermute(turn, "hi", [(1, 3), (3, 1)])
+        turn = lax.ppermute(turn, ("hi", "lo"), over_zx)
     own_half, rows = lax.optimization_barrier((jnp.where(owns[1:] == 0, own_half, turn), rows))
     moved = lax.all_to_all(rows.reshape(n_lower, piece + extra, images * ranks), "lo", 0, 0)
     rows = gather_rows(target_order, moved)

time: 149 us -> 142 us (0.953)
  blocking collectives: 81.5 us -> 70.6 us
  waiting for transfers between devices: 8.03 us -> 16.8 us
  Pallas kernels: 38.8 us -> 32.5 us
  starting transfers between devices: 19.1 us -> 21.3 us
    ppermute x4 -> x2, waiting for transfers between devices: 3.46 us -> 15.5 us  [body(): received[at] = lax.ppermute(sent, 'hi', [(i, i ^ 2) for i in range(4)])]
    ppermute x2, starting transfers between devices: 7.1 us -> 15.3 us  [body(): turn = lax.ppermute(turn, ('hi', 'lo'), over_zx)]
    pallas_call x4 -> x2, Pallas kernels: 17.2 us -> 12.7 us  [front(): pl.pallas_call(functools.partial(front_kernel, LOCAL_LEVELS), grid_spec=g...]
    all_to_all x1, blocking collectives: 24.8 us -> 20.4 us  [body(): lax.all_to_all(rows.reshape(n_lower, piece, images * ranks), 'lo', 0, 0)]
    all_to_all x1, blocking collectives: 30 us -> 26.3 us  [body(): lax.all_to_all(rows.reshape(n_lower, piece + extra, images * ranks), 'lo'...]
    ppermute x2, waiting for transfers between devices: 4.56 us -> 1.24 us  [body(): turn = lax.ppermute(turn, ('hi', 'lo'), over_zx)]
    ppermute x4 -> x2, starting transfers between devices: 7.64 us -> 4.63 us  [body(): received[at] = lax.ppermute(sent, 'hi', [(i, i ^ 2) for i in range(4)])]
    ppermute x4 -> x2, starting transfers between devices: 4.34 us -> 1.41 us  [body(): received[at] = lax.ppermute(sent, 'hi', [(i, i ^ 1) for i in range(4)])]
  transfers between devices with their start and end apart: 10 -> 6, of which waited for: 4 -> 4; matrix products, arithmetic and copies ran while one was open for 0% -> 0% of each run, Pallas kernels for 12% -> 5%
where the time goes in v4:
time: 142 us
  blocking collectives  70.6 us (50%)
  Pallas kernels  32.5 us (23%)
  starting transfers between devices  21.3 us (15%)
  waiting for transfers between devices  16.8 us (12%)
    all_to_all x1, blocking collectives, body(): lax.all_to_all(rows.reshape(n_lower, piece + extra, images * ranks), 'lo'...  26.3 us
    all_to_all x1, blocking collectives, body(): blocks = lax.all_to_all(blocks, 'lo', 0, 0, axis_index_groups=groups)  23.9 us
    all_to_all x1, blocking collectives, body(): lax.all_to_all(rows.reshape(n_lower, piece, images * ranks), 'lo', 0, 0)  20.4 us
    ppermute x2, waiting for transfers between devices, body(): received[at] = lax.ppermute(sent, 'hi', [(i, i ^ 2) for i in range(4)])  15.5 us
    ppermute x2, starting transfers between devices, body(): turn = lax.ppermute(turn, ('hi', 'lo'), over_zx)  15.3 us
    pallas_call x2, Pallas kernels, front(): pl.pallas_call(functools.partial(front_kernel, LOCAL_LEVELS), grid_spec=g...  12.7 us
    pallas_call x1, Pallas kernels, gather_rows(): pl.pallas_call(gather_kernel, in_specs=[pl.BlockSpec(memory_space=pltpu.S...  8.55 us
    pallas_call x1, Pallas kernels, to_targets(): pl.pallas_call(functools.partial(target_kernel, box_gain.shape[0] - 1), g...  5.07 us
  transfers between devices with their start and end apart: 6, of which 4 were waited for; matrix products, arithmetic and copies ran while one was open for 0% of the time, Pallas kernels for 5%

profile of v4, /device:TPU:1, one launch (start us, length us, event | category | flops | bytes accessed | tf_op | source)
XLA Modules:
  0.0 142.0 jit_solution(5136883726183978114)
XLA Ops:
  0.0 6.4 %source_map_and_local_levels.2 = (bf16[64,4096]{1,0:T(8,128)(2,1)}, bf16[64,4096]{1,0:T(8,128)(2,1)}) custom-call(s32[1]{0:T(128)} %bitcast.2.own_ref, bf16[2,256,8192]{2,1,0:T(8,128)(2,1)} %high_ref.3, bf16[2,256,8192]{2,1,0:T(8,128)(2,1)} %high_ref.3, bf16[64,256]{1,0:T(8,128)(2,1)} %map_ref.3, bf16[15,128,128]{2,1,0:T(8,128)(2,1)} %bitcast.12, ...), custom_call_target="tpu_custom_call" | custom-call | flops 10737418240 | bytes 4194304 | tf_op jit(solution)/shard_map/source_map_and_local_levels/pallas_call | solution.py:73
  6.4 4.5 %collective-permute-start = (bf16[64,4096]{1,0:T(8,128)(2,1)}, bf16[64,4096]{1,0:T(8,128)(2,1)S(1)}, u32[]{:S(2)}, u32[]{:S(2)}) collective-permute-start(bf16[64,4096]{1,0:T(8,128)(2,1)} %get-tuple-element.20), channel_id=1, source_target_pairs={{0,64},{32,96},{64,0},{96,32},{1,65},{33,97},{65,1},{97,33},{2,66}... | collective-permute-start | bytes 1572872 | tf_op jit(solution)/shard_map/ppermute | solution.py:336
  10.9 6.4 %source_map_and_local_levels.3 = (bf16[64,4096]{1,0:T(8,128)(2,1)}, bf16[64,4096]{1,0:T(8,128)(2,1)}) custom-call(s32[1]{0:T(128)} %bitcast.2.own_ref, bf16[2,256,8192]{2,1,0:T(8,128)(2,1)} %high_ref.3, bf16[2,256,8192]{2,1,0:T(8,128)(2,1)} %high_ref.3, bf16[64,256]{1,0:T(8,128)(2,1)} %map_ref.3, bf16[15,128,128]{2,1,0:T(8,128)(2,1)} %bitcast.13, ...), custom_call_target="tpu_custom_call" | custom-call | flops 10737418240 | bytes 4194304 | tf_op jit(solution)/shard_map/source_map_and_local_levels/pallas_call | solution.py:73
  17.3 0.1 collective-permute-start.1
  17.4 0.1 pad_add_fusion.own_ref
  17.5 5.3 %collective-permute-done.recv_in = bf16[64,4096]{1,0:T(8,128)(2,1)S(1)} collective-permute-done((bf16[64,4096]{1,0:T(8,128)(2,1)}, bf16[64,4096]{1,0:T(8,128)(2,1)S(1)}, u32[]{:S(2)}, u32[]{:S(2)}) %collective-permute-start) | collective-permute-done | bytes 524320 | tf_op jit(solution)/shard_map/ppermute | solution.py:336
  22.7 0.0 copy-done
  22.7 0.0 copy-done.3
  22.7 0.0 copy-done.5
  22.7 1.0 upper_level.2
  23.7 10.2 %collective-permute-done.1.recv_in = bf16[64,4096]{1,0:T(8,128)(2,1)S(1)} collective-permute-done((bf16[64,4096]{1,0:T(8,128)(2,1)}, bf16[64,4096]{1,0:T(8,128)(2,1)S(1)}, u32[]{:S(2)}, u32[]{:S(2)}) %collective-permute-start.1) | collective-permute-done | bytes 524320 | tf_op jit(solution)/shard_map/ppermute | solution.py:336
  34.0 0.0 copy-done.4
  34.0 1.0 upper_level.3
  35.0 1.3 collective-permute-start.5
  36.3 0.1 collective-permute-start.4
  36.4 8.0 %collective-permute-start.2 = (s32[1]{0:T(128)}, s32[1]{0:T(128)}, u32[]{:S(2)}, u32[]{:S(2)}) collective-permute-start(s32[1]{0:T(128)} %bitcast.1), channel_id=1, source_target_pairs={{32,98},{33,99},{34,96},{35,97},{36,102},{37,103},{38,100},{39,101... | collective-permute-start | bytes 20 | tf_op jit(solution)/shard_map/ppermute | solution.py:361
  44.4 0.2 collective-permute-done.2
  44.5 7.3 %collective-permute-start.3 = (s32[1]{0:T(128)}, s32[1]{0:T(128)}, u32[]{:S(2)}, u32[]{:S(2)}) collective-permute-start(s32[1]{0:T(128)} %collective-permute-done.2), channel_id=1, source_target_pairs={{32,98},{33,99},{34,96},{35,97},{36,102},{37,103},{38,100},{39,101... | collective-permute-start | bytes 20 | tf_op jit(solution)/shard_map/ppermute | solution.py:361
  51.8 1.1 collective-permute-done.3
  53.5 0.0 collective-permute-done.5.refs_3_
  53.5 0.0 collective-permute-done.4.refs_2_
  53.5 1.2 upper_level_to_rows.1
  54.8 0.0 copy-start.1
  54.8 26.3 %all_to_all.15.rows_ref.gain_ref = bf16[32,272,128]{2,1,0:T(8,128)(2,1)S(1)} all-to-all(bf16[32,272,128]{2,1,0:T(8,128)(2,1)S(1)} %bitcast.9), channel_id=1, replica_groups=mesh['hi'=4,'lo'=32] {'lo'}, dimensions={0} | all-to-all | bytes 4456448 | tf_op jit(solution)/shard_map/all_to_all | solution.py:363
  81.1 0.0 copy-done.1
  81.1 8.5 %box_order.1 = bf16[8192,128]{1,0:T(8,128)(2,1)S(1)} custom-call(s32[1,8192]{1,0:T(1,128)S(1)} %copy-done.1, bf16[32,272,128]{2,1,0:T(8,128)(2,1)S(1)} %all_to_all.15.rows_ref.gain_ref), custom_call_target="tpu_custom_call" | custom-call | bytes 31457280 | tf_op jit(solution)/shard_map/box_order/pallas_call | solution.py:203
  89.7 20.4 %all_to_all.16.x_ref = bf16[32,256,128]{2,1,0:T(8,128)(2,1)S(1)} all-to-all(bf16[32,256,128]{2,1,0:T(8,128)(2,1)S(1)} %bitcast.8), channel_id=1, replica_groups=mesh['hi'=4,'lo'=32] {'lo'}, dimensions={0} | all-to-all | bytes 4194304 | tf_op jit(solution)/shard_map/all_to_all | solution.py:365
  110.0 3.0 %lower_levels.1 = bf16[32,2,64,256]{3,2,1,0:T(8,128)(2,1)S(1)} custom-call(s32[1]{0:T(128)S(6)} %select_n.4.own_ref, bf16[32,256,128]{2,1,0:T(8,128)(2,1)S(1)} %all_to_all.16.x_ref, bf16[15,128,128]{2,1,0:T(8,128)(2,1)S(1)} %bitcast.17, bf16[32,272,128]{2,1,0:T(8,128)(2,1)S(1)} %all_to_all.15.rows_ref.gain_ref), custom_call_target="tpu_custom_call" | custom-call | flops 10737418240 | bytes 4194304 | tf_op jit(solution)/shard_map/lower_levels/pallas_call | solution.py:269
  113.0 0.0 copy-start.2
  113.0 23.9 %all_to_all.17.x_ref = bf16[16,2,2,64,256]{4,3,2,1,0:T(8,128)(2,1)S(1)} all-to-all(bf16[16,2,2,64,256]{4,3,2,1,0:T(8,128)(2,1)S(1)} %bitcast.10), channel_id=1, replica_groups={{0,1,2,3,4,5,6,7,8,9,10,11,12,13,14,15},{16,17,18,19,20,21,22,23,24,25,..., dimensions={0} | all-to-all | bytes 4194304 | tf_op jit(solution)/shard_map/all_to_all | solution.py:368
  136.9 0.0 copy-done.2
  136.9 5.1 %target_map.1 = bf16[2,256,8192]{2,1,0:T(8,128)(2,1)} custom-call(bf16[16,2,2,64,256]{4,3,2,1,0:T(8,128)(2,1)S(1)} %all_to_all.17.x_ref, bf16[64,256]{1,0:T(8,128)(2,1)S(1)} %bitcast.11, f32[15,8192]{1,0:T(8,128)S(1)} %copy-done), custom_call_target="tpu_custom_call" | custom-call | flops 2147483648 | bytes 8388608 | tf_op jit(solution)/shard_map/target_map/pallas_call | solution.py:299
  (4 shorter events, 0.0 us)
Async XLA Ops:
  6.4 16.4 %copy-start = (f32[15,8192]{1,0:T(8,128)S(1)}, f32[15,8192]{1,0:T(8,128)}, u32[]{:S(2)}) copy-start(f32[15,8192]{1,0:T(8,128)} %gain_ref.1) | copy-start | bytes 1474564
  6.4 16.4 %copy-start.3 = (bf16[15,2,64,128]{3,2,1,0:T(8,128)(2,1)S(1)}, bf16[15,2,64,128]{3,2,1,0:T(8,128)(2,1)}, u32[]{:S(2)}) copy-start(bf16[15,2,64,128]{3,2,1,0:T(8,128)(2,1)} %param.8) | copy-start | bytes 1474564
  6.4 16.4 %copy-start.5 = (bf16[64,4096]{1,0:T(8,128)(2,1)S(1)}, bf16[64,4096]{1,0:T(8,128)(2,1)}, u32[]{:S(2)}) copy-start(bf16[64,4096]{1,0:T(8,128)(2,1)} %get-tuple-element.19.kept_in) | copy-start | bytes 1572868
  6.4 16.4 %collective-permute-start = (bf16[64,4096]{1,0:T(8,128)(2,1)}, bf16[64,4096]{1,0:T(8,128)(2,1)S(1)}, u32[]{:S(2)}, u32[]{:S(2)}) collective-permute-start(bf16[64,4096]{1,0:T(8,128)(2,1)} %get-tuple-element.20), channel_id=1, source_target_pairs={{0,64},{32,96},{64,0},{96,32},{1,65},{33,97},{65,1},{97,33},{2,66}... | collective-permute-start | bytes 1572872 | tf_op jit(solution)/shard_map/ppermute | solution.py:336
  17.3 16.7 %copy-start.4 = (bf16[64,4096]{1,0:T(8,128)(2,1)S(1)}, bf16[64,4096]{1,0:T(8,128)(2,1)}, u32[]{:S(2)}) copy-start(bf16[64,4096]{1,0:T(8,128)(2,1)} %get-tuple-element.23.kept_in) | copy-start | bytes 1572868
  17.3 16.7 %collective-permute-start.1 = (bf16[64,4096]{1,0:T(8,128)(2,1)}, bf16[64,4096]{1,0:T(8,128)(2,1)S(1)}, u32[]{:S(2)}, u32[]{:S(2)}) collective-permute-start(bf16[64,4096]{1,0:T(8,128)(2,1)} %get-tuple-element.24), channel_id=1, source_target_pairs={{0,64},{32,96},{64,0},{96,32},{1,65},{33,97},{65,1},{97,33},{2,66}... | collective-permute-start | bytes 1572872 | tf_op jit(solution)/shard_map/ppermute | solution.py:336
  35.0 18.6 %collective-permute-start.5 = (bf16[64,4096]{1,0:T(8,128)(2,1)S(1)}, bf16[64,4096]{1,0:T(8,128)(2,1)S(1)}, u32[]{:S(2)}, u32[]{:S(2)}) collective-permute-start(bf16[64,4096]{1,0:T(8,128)(2,1)S(1)} %get-tuple-element.30), channel_id=1, source_target_pairs={{0,32},{32,0},{64,96},{96,64},{1,33},{33,1},{65,97},{97,65},{2,34}... | collective-permute-start | bytes 1572872 | tf_op jit(solution)/shard_map/ppermute | solution.py:345
  36.3 17.3 %collective-permute-start.4 = (bf16[64,4096]{1,0:T(8,128)(2,1)S(1)}, bf16[64,4096]{1,0:T(8,128)(2,1)S(1)}, u32[]{:S(2)}, u32[]{:S(2)}) collective-permute-start(bf16[64,4096]{1,0:T(8,128)(2,1)S(1)} %get-tuple-element.29), channel_id=1, source_target_pairs={{0,32},{32,0},{64,96},{96,64},{1,33},{33,1},{65,97},{97,65},{2,34}... | collective-permute-start | bytes 1572872 | tf_op jit(solution)/shard_map/ppermute | solution.py:345
  36.4 8.2 %collective-permute-start.2 = (s32[1]{0:T(128)}, s32[1]{0:T(128)}, u32[]{:S(2)}, u32[]{:S(2)}) collective-permute-start(s32[1]{0:T(128)} %bitcast.1), channel_id=1, source_target_pairs={{32,98},{33,99},{34,96},{35,97},{36,102},{37,103},{38,100},{39,101... | collective-permute-start | bytes 20 | tf_op jit(solution)/shard_map/ppermute | solution.py:361
  44.5 8.3 %collective-permute-start.3 = (s32[1]{0:T(128)}, s32[1]{0:T(128)}, u32[]{:S(2)}, u32[]{:S(2)}) collective-permute-start(s32[1]{0:T(128)} %collective-permute-done.2), channel_id=1, source_target_pairs={{32,98},{33,99},{34,96},{35,97},{36,102},{37,103},{38,100},{39,101... | collective-permute-start | bytes 20 | tf_op jit(solution)/shard_map/ppermute | solution.py:361
  54.8 26.4 %copy-start.1 = (s32[1,8192]{1,0:T(1,128)S(1)}, s32[1,8192]{1,0:T(1,128)}, u32[]{:S(2)}) copy-start(s32[1,8192]{1,0:T(1,128)} %order_ref.1) | copy-start | bytes 98308
  113.0 23.9 %copy-start.2 = (bf16[256,64]{0,1:T(8,128)(2,1)S(1)}, bf16[256,64]{0,1:T(8,128)(2,1)}, u32[]{:S(2)}) copy-start(bf16[256,64]{0,1:T(8,128)(2,1)} %param.11) | copy-start | bytes 98308

commit v5 on v4

--- a/solution.py
+++ b/solution.py
@@ -13,8 +13,7 @@
 VMEM_LIMIT = 40 * 2**20
 FRONT_LIMIT = 56 * 2**20
 PARTS = 1
-TURN_STEPS = 2
-PARTNER = 66
+PARTNERS = 74, 66
 
 
 def dot(a, b):
@@ -356,10 +355,10 @@
             extra,
             rows,
         )
-    over_zx = [(d, d ^ PARTNER) for d in range(4 * n_lower) if d & n_lower]
-    for _ in range(TURN_STEPS):
-        turn = lax.ppermute(turn, ("hi", "lo"), over_zx)
-    own_half, rows = lax.optimization_barrier((jnp.where(owns[1:] == 0, own_half, turn), rows))
+    for partner in PARTNERS:
+        pairs = [(d, d ^ partner) for d in range(4 * n_lower) if d & n_lower]
+        turn = lax.ppermute(turn, ("hi", "lo"), pairs)
+    own_half, rows = lax.optimization_barrier((jnp.maximum(own_half, turn), rows))
     moved = lax.all_to_all(rows.reshape(n_lower, piece + extra, images * ranks), "lo", 0, 0)
     rows = gather_rows(target_order, moved)
     rows = lax.all_to_all(rows.reshape(n_lower, piece, images * ranks), "lo", 0, 0)

time: 142 us -> 141 us (level)
  blocking collectives: 70.6 us -> 68.7 us
    all_to_all x1, blocking collectives: 23.9 us -> 21.3 us  [body(): blocks = lax.all_to_all(blocks, 'lo', 0, 0, axis_index_groups=groups)]
where the time goes in v5:
time: 141 us
  blocking collectives  68.7 us (49%)
  Pallas kernels  32.5 us (23%)
  starting transfers between devices  22.2 us (16%)
  waiting for transfers between devices  16.9 us (12%)
    all_to_all x1, blocking collectives, body(): lax.all_to_all(rows.reshape(n_lower, piece + extra, images * ranks), 'lo'...  26.7 us
    all_to_all x1, blocking collectives, body(): blocks = lax.all_to_all(blocks, 'lo', 0, 0, axis_index_groups=groups)  21.3 us
    all_to_all x1, blocking collectives, body(): lax.all_to_all(rows.reshape(n_lower, piece, images * ranks), 'lo', 0, 0)  20.6 us
    ppermute x2, starting transfers between devices, body(): turn = lax.ppermute(turn, ('hi', 'lo'), pairs)  16.2 us
    ppermute x2, waiting for transfers between devices, body(): received[at] = lax.ppermute(sent, 'hi', [(i, i ^ 2) for i in range(4)])  15.5 us
    pallas_call x2, Pallas kernels, front(): pl.pallas_call(functools.partial(front_kernel, LOCAL_LEVELS), grid_spec=g...  12.7 us
    pallas_call x1, Pallas kernels, gather_rows(): pl.pallas_call(gather_kernel, in_specs=[pl.BlockSpec(memory_space=pltpu.S...  8.55 us
    pallas_call x1, Pallas kernels, to_targets(): pl.pallas_call(functools.partial(target_kernel, box_gain.shape[0] - 1), g...  5.07 us
  transfers between devices with their start and end apart: 6, of which 4 were waited for; matrix products, arithmetic and copies ran while one was open for 0% of the time, Pallas kernels for 5%

profile of v5, /device:TPU:1, one launch (start us, length us, event | category | flops | bytes accessed | tf_op | source)
XLA Modules:
  0.0 141.1 jit_solution(10424827242066433669)
XLA Ops:
  0.0 6.4 %source_map_and_local_levels.2 = (bf16[64,4096]{1,0:T(8,128)(2,1)}, bf16[64,4096]{1,0:T(8,128)(2,1)}) custom-call(s32[1]{0:T(128)} %bitcast.1.own_ref, bf16[2,256,8192]{2,1,0:T(8,128)(2,1)} %high_ref.3, bf16[2,256,8192]{2,1,0:T(8,128)(2,1)} %high_ref.3, bf16[64,256]{1,0:T(8,128)(2,1)} %map_ref.3, bf16[15,128,128]{2,1,0:T(8,128)(2,1)} %bitcast.12, ...), custom_call_target="tpu_custom_call" | custom-call | flops 10737418240 | bytes 4194304 | tf_op jit(solution)/shard_map/source_map_and_local_levels/pallas_call | solution.py:72
  6.4 4.5 %collective-permute-start = (bf16[64,4096]{1,0:T(8,128)(2,1)}, bf16[64,4096]{1,0:T(8,128)(2,1)S(1)}, u32[]{:S(2)}, u32[]{:S(2)}) collective-permute-start(bf16[64,4096]{1,0:T(8,128)(2,1)} %get-tuple-element.20), channel_id=1, source_target_pairs={{0,64},{32,96},{64,0},{96,32},{1,65},{33,97},{65,1},{97,33},{2,66}... | collective-permute-start | bytes 1572872 | tf_op jit(solution)/shard_map/ppermute | solution.py:335
  10.9 6.4 %source_map_and_local_levels.3 = (bf16[64,4096]{1,0:T(8,128)(2,1)}, bf16[64,4096]{1,0:T(8,128)(2,1)}) custom-call(s32[1]{0:T(128)} %bitcast.1.own_ref, bf16[2,256,8192]{2,1,0:T(8,128)(2,1)} %high_ref.3, bf16[2,256,8192]{2,1,0:T(8,128)(2,1)} %high_ref.3, bf16[64,256]{1,0:T(8,128)(2,1)} %map_ref.3, bf16[15,128,128]{2,1,0:T(8,128)(2,1)} %bitcast.13, ...), custom_call_target="tpu_custom_call" | custom-call | flops 10737418240 | bytes 4194304 | tf_op jit(solution)/shard_map/source_map_and_local_levels/pallas_call | solution.py:72
  17.3 0.1 collective-permute-start.1
  17.4 0.1 pad_add_fusion.own_ref
  17.5 5.3 %collective-permute-done.recv_in = bf16[64,4096]{1,0:T(8,128)(2,1)S(1)} collective-permute-done((bf16[64,4096]{1,0:T(8,128)(2,1)}, bf16[64,4096]{1,0:T(8,128)(2,1)S(1)}, u32[]{:S(2)}, u32[]{:S(2)}) %collective-permute-start) | collective-permute-done | bytes 524320 | tf_op jit(solution)/shard_map/ppermute | solution.py:335
  22.7 0.0 copy-done
  22.7 0.0 copy-done.3
  22.7 0.0 copy-done.5
  22.7 1.0 upper_level.2
  23.7 10.2 %collective-permute-done.1.recv_in = bf16[64,4096]{1,0:T(8,128)(2,1)S(1)} collective-permute-done((bf16[64,4096]{1,0:T(8,128)(2,1)}, bf16[64,4096]{1,0:T(8,128)(2,1)S(1)}, u32[]{:S(2)}, u32[]{:S(2)}) %collective-permute-start.1) | collective-permute-done | bytes 524320 | tf_op jit(solution)/shard_map/ppermute | solution.py:335
  34.0 0.0 copy-done.4
  34.0 1.0 upper_level.3
  35.0 1.3 collective-permute-start.5
  36.3 0.1 collective-permute-start.4
  36.4 9.0 %collective-permute-start.2 = (s32[1]{0:T(128)}, s32[1]{0:T(128)}, u32[]{:S(2)}, u32[]{:S(2)}) collective-permute-start(s32[1]{0:T(128)} %bitcast), channel_id=1, source_target_pairs={{32,106},{33,107},{34,104},{35,105},{36,110},{37,111},{38,108},{39... | collective-permute-start | bytes 20 | tf_op jit(solution)/shard_map/ppermute | solution.py:360
  45.4 0.2 collective-permute-done.2
  45.6 7.1 %collective-permute-start.3 = (s32[1]{0:T(128)}, s32[1]{0:T(128)}, u32[]{:S(2)}, u32[]{:S(2)}) collective-permute-start(s32[1]{0:T(128)} %collective-permute-done.2), channel_id=1, source_target_pairs={{32,98},{33,99},{34,96},{35,97},{36,102},{37,103},{38,100},{39,101... | collective-permute-start | bytes 20 | tf_op jit(solution)/shard_map/ppermute | solution.py:360
  52.7 1.2 collective-permute-done.3
  54.5 0.0 collective-permute-done.5.refs_3_
  54.5 0.0 collective-permute-done.4.refs_2_
  54.6 1.2 upper_level_to_rows.1
  55.8 0.0 copy-start.1
  55.8 26.7 %all_to_all.15.rows_ref.gain_ref = bf16[32,272,128]{2,1,0:T(8,128)(2,1)S(1)} all-to-all(bf16[32,272,128]{2,1,0:T(8,128)(2,1)S(1)} %bitcast.9), channel_id=1, replica_groups=mesh['hi'=4,'lo'=32] {'lo'}, dimensions={0} | all-to-all | bytes 4456448 | tf_op jit(solution)/shard_map/all_to_all | solution.py:362
  82.5 0.0 copy-done.1
  82.5 8.5 %box_order.1 = bf16[8192,128]{1,0:T(8,128)(2,1)S(1)} custom-call(s32[1,8192]{1,0:T(1,128)S(1)} %copy-done.1, bf16[32,272,128]{2,1,0:T(8,128)(2,1)S(1)} %all_to_all.15.rows_ref.gain_ref), custom_call_target="tpu_custom_call" | custom-call | bytes 31457280 | tf_op jit(solution)/shard_map/box_order/pallas_call | solution.py:202
  91.1 20.6 %all_to_all.16.x_ref = bf16[32,256,128]{2,1,0:T(8,128)(2,1)S(1)} all-to-all(bf16[32,256,128]{2,1,0:T(8,128)(2,1)S(1)} %bitcast.8), channel_id=1, replica_groups=mesh['hi'=4,'lo'=32] {'lo'}, dimensions={0} | all-to-all | bytes 4194304 | tf_op jit(solution)/shard_map/all_to_all | solution.py:364
  111.7 3.0 %lower_levels.1 = bf16[32,2,64,256]{3,2,1,0:T(8,128)(2,1)S(1)} custom-call(s32[1]{0:T(128)S(6)} %max.3.own_ref, bf16[32,256,128]{2,1,0:T(8,128)(2,1)S(1)} %all_to_all.16.x_ref, bf16[15,128,128]{2,1,0:T(8,128)(2,1)S(1)} %bitcast.17, bf16[32,272,128]{2,1,0:T(8,128)(2,1)S(1)} %all_to_all.15.rows_ref.gain_ref), custom_call_target="tpu_custom_call" | custom-call | flops 10737418240 | bytes 4194304 | tf_op jit(solution)/shard_map/lower_levels/pallas_call | solution.py:268
  114.7 0.0 copy-start.2
  114.7 21.3 %all_to_all.17.x_ref = bf16[16,2,2,64,256]{4,3,2,1,0:T(8,128)(2,1)S(1)} all-to-all(bf16[16,2,2,64,256]{4,3,2,1,0:T(8,128)(2,1)S(1)} %bitcast.10), channel_id=1, replica_groups={{0,1,2,3,4,5,6,7,8,9,10,11,12,13,14,15},{16,17,18,19,20,21,22,23,24,25,..., dimensions={0} | all-to-all | bytes 4194304 | tf_op jit(solution)/shard_map/all_to_all | solution.py:367
  136.0 0.0 copy-done.2
  136.0 5.1 %target_map.1 = bf16[2,256,8192]{2,1,0:T(8,128)(2,1)} custom-call(bf16[16,2,2,64,256]{4,3,2,1,0:T(8,128)(2,1)S(1)} %all_to_all.17.x_ref, bf16[64,256]{1,0:T(8,128)(2,1)S(1)} %bitcast.11, f32[15,8192]{1,0:T(8,128)S(1)} %copy-done), custom_call_target="tpu_custom_call" | custom-call | flops 2147483648 | bytes 8388608 | tf_op jit(solution)/shard_map/target_map/pallas_call | solution.py:298
  (4 shorter events, 0.0 us)
Async XLA Ops:
  6.4 16.4 %copy-start = (f32[15,8192]{1,0:T(8,128)S(1)}, f32[15,8192]{1,0:T(8,128)}, u32[]{:S(2)}) copy-start(f32[15,8192]{1,0:T(8,128)} %gain_ref.1) | copy-start | bytes 1474564
  6.4 16.4 %copy-start.3 = (bf16[15,2,64,128]{3,2,1,0:T(8,128)(2,1)S(1)}, bf16[15,2,64,128]{3,2,1,0:T(8,128)(2,1)}, u32[]{:S(2)}) copy-start(bf16[15,2,64,128]{3,2,1,0:T(8,128)(2,1)} %param.8) | copy-start | bytes 1474564
  6.4 16.4 %copy-start.5 = (bf16[64,4096]{1,0:T(8,128)(2,1)S(1)}, bf16[64,4096]{1,0:T(8,128)(2,1)}, u32[]{:S(2)}) copy-start(bf16[64,4096]{1,0:T(8,128)(2,1)} %get-tuple-element.19.kept_in) | copy-start | bytes 1572868
  6.4 16.4 %collective-permute-start = (bf16[64,4096]{1,0:T(8,128)(2,1)}, bf16[64,4096]{1,0:T(8,128)(2,1)S(1)}, u32[]{:S(2)}, u32[]{:S(2)}) collective-permute-start(bf16[64,4096]{1,0:T(8,128)(2,1)} %get-tuple-element.20), channel_id=1, source_target_pairs={{0,64},{32,96},{64,0},{96,32},{1,65},{33,97},{65,1},{97,33},{2,66}... | collective-permute-start | bytes 1572872 | tf_op jit(solution)/shard_map/ppermute | solution.py:335
  17.3 16.7 %copy-start.4 = (bf16[64,4096]{1,0:T(8,128)(2,1)S(1)}, bf16[64,4096]{1,0:T(8,128)(2,1)}, u32[]{:S(2)}) copy-start(bf16[64,4096]{1,0:T(8,128)(2,1)} %get-tuple-element.23.kept_in) | copy-start | bytes 1572868
  17.3 16.7 %collective-permute-start.1 = (bf16[64,4096]{1,0:T(8,128)(2,1)}, bf16[64,4096]{1,0:T(8,128)(2,1)S(1)}, u32[]{:S(2)}, u32[]{:S(2)}) collective-permute-start(bf16[64,4096]{1,0:T(8,128)(2,1)} %get-tuple-element.24), channel_id=1, source_target_pairs={{0,64},{32,96},{64,0},{96,32},{1,65},{33,97},{65,1},{97,33},{2,66}... | collective-permute-start | bytes 1572872 | tf_op jit(solution)/shard_map/ppermute | solution.py:335
  35.0 19.6 %collective-permute-start.5 = (bf16[64,4096]{1,0:T(8,128)(2,1)S(1)}, bf16[64,4096]{1,0:T(8,128)(2,1)S(1)}, u32[]{:S(2)}, u32[]{:S(2)}) collective-permute-start(bf16[64,4096]{1,0:T(8,128)(2,1)S(1)} %get-tuple-element.30), channel_id=1, source_target_pairs={{0,32},{32,0},{64,96},{96,64},{1,33},{33,1},{65,97},{97,65},{2,34}... | collective-permute-start | bytes 1572872 | tf_op jit(solution)/shard_map/ppermute | solution.py:344
  36.3 18.3 %collective-permute-start.4 = (bf16[64,4096]{1,0:T(8,128)(2,1)S(1)}, bf16[64,4096]{1,0:T(8,128)(2,1)S(1)}, u32[]{:S(2)}, u32[]{:S(2)}) collective-permute-start(bf16[64,4096]{1,0:T(8,128)(2,1)S(1)} %get-tuple-element.29), channel_id=1, source_target_pairs={{0,32},{32,0},{64,96},{96,64},{1,33},{33,1},{65,97},{97,65},{2,34}... | collective-permute-start | bytes 1572872 | tf_op jit(solution)/shard_map/ppermute | solution.py:344
  36.4 9.2 %collective-permute-start.2 = (s32[1]{0:T(128)}, s32[1]{0:T(128)}, u32[]{:S(2)}, u32[]{:S(2)}) collective-permute-start(s32[1]{0:T(128)} %bitcast), channel_id=1, source_target_pairs={{32,106},{33,107},{34,104},{35,105},{36,110},{37,111},{38,108},{39... | collective-permute-start | bytes 20 | tf_op jit(solution)/shard_map/ppermute | solution.py:360
  45.6 8.3 %collective-permute-start.3 = (s32[1]{0:T(128)}, s32[1]{0:T(128)}, u32[]{:S(2)}, u32[]{:S(2)}) collective-permute-start(s32[1]{0:T(128)} %collective-permute-done.2), channel_id=1, source_target_pairs={{32,98},{33,99},{34,96},{35,97},{36,102},{37,103},{38,100},{39,101... | collective-permute-start | bytes 20 | tf_op jit(solution)/shard_map/ppermute | solution.py:360
  55.8 26.7 %copy-start.1 = (s32[1,8192]{1,0:T(1,128)S(1)}, s32[1,8192]{1,0:T(1,128)}, u32[]{:S(2)}) copy-start(s32[1,8192]{1,0:T(1,128)} %order_ref.1) | copy-start | bytes 98308
  114.7 21.4 %copy-start.2 = (bf16[256,64]{0,1:T(8,128)(2,1)S(1)}, bf16[256,64]{0,1:T(8,128)(2,1)}, u32[]{:S(2)}) copy-start(bf16[256,64]{0,1:T(8,128)(2,1)} %param.11) | copy-start | bytes 98308

commit v6 on v5

--- a/solution.py
+++ b/solution.py
@@ -167,7 +167,7 @@
     )(owns, *kept, *received, matrices, box_gain, box_gain, *more)
 
 
-UNROLL = 128
+UNROLL = 512
 
 
 def gather_kernel(order_ref, rows_ref, out_ref, table, picked):
@@ -184,17 +184,11 @@
     def move(i, carry):
         base = pl.multiple_of(i * UNROLL, UNROLL)
         for k in range(UNROLL):
-            picked[pl.ds(base + k, 1), :] = table[pl.ds(order_ref[0, base + k], 1), :]
+            picked[k : k + 1, :] = table[pl.ds(order_ref[0, base + k], 1), :]
+        out_ref[pl.ds(base, UNROLL), :] = picked[...].astype(BF16)
         return carry
 
     lax.fori_loop(0, boxes // UNROLL, move, 0)
-
-    def narrow(i, carry):
-        at = pl.ds(pl.multiple_of(i * chunk, chunk), chunk)
-        out_ref[at, :] = picked[at, :].astype(BF16)
-        return carry
-
-    lax.fori_loop(0, boxes // chunk, narrow, 0)
 
 
 def gather_rows(order, rows):
@@ -207,7 +201,7 @@
         ],
         out_specs=pl.BlockSpec(memory_space=pltpu.VMEM),
         out_shape=jax.ShapeDtypeStruct((boxes, width), BF16),
-        scratch_shapes=[pltpu.VMEM((boxes, width), F32), pltpu.VMEM((boxes, width), F32)],
+        scratch_shapes=[pltpu.VMEM((boxes, width), F32), pltpu.VMEM((UNROLL, width), F32)],
         compiler_params=params(),
         cost_estimate=cost(0, 30 * 2**20),
         name="box_order",
@@ -365,7 +359,7 @@
     blocks = lower_levels(own_half, rows, matrices, moved, images, first_lower)
     blocks = blocks.reshape(halves, 2, images, ranks, piece)
     blocks = lax.all_to_all(blocks, "lo", 0, 0, axis_index_groups=groups)
-    return to_targets(blocks, target_map.T, box_gain, 8)
+    return to_targets(blocks, target_map.T, box_gain, 16)
 
 
 def solution(mesh):

time: 141 us -> 141 us (level)
  no operation moved by 1% of the time
where the time goes in v6:
time: 141 us
  blocking collectives  68.7 us (49%)
  Pallas kernels  32 us (23%)
  starting transfers between devices  22.2 us (16%)
  waiting for transfers between devices  16.9 us (12%)
    all_to_all x1, blocking collectives, body(): lax.all_to_all(rows.reshape(n_lower, piece + extra, images * ranks), 'lo'...  26.7 us
    all_to_all x1, blocking collectives, body(): blocks = lax.all_to_all(blocks, 'lo', 0, 0, axis_index_groups=groups)  21.3 us
    all_to_all x1, blocking collectives, body(): lax.all_to_all(rows.reshape(n_lower, piece, images * ranks), 'lo', 0, 0)  20.6 us
    ppermute x2, starting transfers between devices, body(): turn = lax.ppermute(turn, ('hi', 'lo'), pairs)  16.2 us
    ppermute x2, waiting for transfers between devices, body(): received[at] = lax.ppermute(sent, 'hi', [(i, i ^ 2) for i in range(4)])  15.5 us
    pallas_call x2, Pallas kernels, front(): pl.pallas_call(functools.partial(front_kernel, LOCAL_LEVELS), grid_spec=g...  12.7 us
    pallas_call x1, Pallas kernels, gather_rows(): pl.pallas_call(gather_kernel, in_specs=[pl.BlockSpec(memory_space=pltpu.S...  8.2 us
    pallas_call x1, Pallas kernels, to_targets(): pl.pallas_call(functools.partial(target_kernel, box_gain.shape[0] - 1), g...  4.88 us
  transfers between devices with their start and end apart: 6, of which 4 were waited for; matrix products, arithmetic and copies ran while one was open for 0% of the time, Pallas kernels for 5%

profile of v6, /device:TPU:1, one launch (start us, length us, event | category | flops | bytes accessed | tf_op | source)
XLA Modules:
  0.0 140.6 jit_solution(6558663564797718172)
XLA Ops:
  0.0 6.4 %source_map_and_local_levels.2 = (bf16[64,4096]{1,0:T(8,128)(2,1)}, bf16[64,4096]{1,0:T(8,128)(2,1)}) custom-call(s32[1]{0:T(128)} %bitcast.1.own_ref, bf16[2,256,8192]{2,1,0:T(8,128)(2,1)} %high_ref.3, bf16[2,256,8192]{2,1,0:T(8,128)(2,1)} %high_ref.3, bf16[64,256]{1,0:T(8,128)(2,1)} %map_ref.3, bf16[15,128,128]{2,1,0:T(8,128)(2,1)} %bitcast.12, ...), custom_call_target="tpu_custom_call" | custom-call | flops 10737418240 | bytes 4194304 | tf_op jit(solution)/shard_map/source_map_and_local_levels/pallas_call | solution.py:72
  6.4 4.5 %collective-permute-start = (bf16[64,4096]{1,0:T(8,128)(2,1)}, bf16[64,4096]{1,0:T(8,128)(2,1)S(1)}, u32[]{:S(2)}, u32[]{:S(2)}) collective-permute-start(bf16[64,4096]{1,0:T(8,128)(2,1)} %get-tuple-element.20), channel_id=1, source_target_pairs={{0,64},{32,96},{64,0},{96,32},{1,65},{33,97},{65,1},{97,33},{2,66}... | collective-permute-start | bytes 1572872 | tf_op jit(solution)/shard_map/ppermute | solution.py:329
  10.9 6.4 %source_map_and_local_levels.3 = (bf16[64,4096]{1,0:T(8,128)(2,1)}, bf16[64,4096]{1,0:T(8,128)(2,1)}) custom-call(s32[1]{0:T(128)} %bitcast.1.own_ref, bf16[2,256,8192]{2,1,0:T(8,128)(2,1)} %high_ref.3, bf16[2,256,8192]{2,1,0:T(8,128)(2,1)} %high_ref.3, bf16[64,256]{1,0:T(8,128)(2,1)} %map_ref.3, bf16[15,128,128]{2,1,0:T(8,128)(2,1)} %bitcast.13, ...), custom_call_target="tpu_custom_call" | custom-call | flops 10737418240 | bytes 4194304 | tf_op jit(solution)/shard_map/source_map_and_local_levels/pallas_call | solution.py:72
  17.3 0.1 collective-permute-start.1
  17.4 0.1 pad_add_fusion.own_ref
  17.5 5.3 %collective-permute-done.recv_in = bf16[64,4096]{1,0:T(8,128)(2,1)S(1)} collective-permute-done((bf16[64,4096]{1,0:T(8,128)(2,1)}, bf16[64,4096]{1,0:T(8,128)(2,1)S(1)}, u32[]{:S(2)}, u32[]{:S(2)}) %collective-permute-start) | collective-permute-done | bytes 524320 | tf_op jit(solution)/shard_map/ppermute | solution.py:329
  22.7 0.0 copy-done
  22.7 0.0 copy-done.3
  22.7 0.0 copy-done.5
  22.7 1.0 upper_level.2
  23.7 10.2 %collective-permute-done.1.recv_in = bf16[64,4096]{1,0:T(8,128)(2,1)S(1)} collective-permute-done((bf16[64,4096]{1,0:T(8,128)(2,1)}, bf16[64,4096]{1,0:T(8,128)(2,1)S(1)}, u32[]{:S(2)}, u32[]{:S(2)}) %collective-permute-start.1) | collective-permute-done | bytes 524320 | tf_op jit(solution)/shard_map/ppermute | solution.py:329
  34.0 0.0 copy-done.4
  34.0 1.0 upper_level.3
  35.0 1.3 collective-permute-start.5
  36.3 0.1 collective-permute-start.4
  36.4 9.0 %collective-permute-start.2 = (s32[1]{0:T(128)}, s32[1]{0:T(128)}, u32[]{:S(2)}, u32[]{:S(2)}) collective-permute-start(s32[1]{0:T(128)} %bitcast), channel_id=1, source_target_pairs={{32,106},{33,107},{34,104},{35,105},{36,110},{37,111},{38,108},{39... | collective-permute-start | bytes 20 | tf_op jit(solution)/shard_map/ppermute | solution.py:354
  45.4 0.2 collective-permute-done.2
  45.6 7.1 %collective-permute-start.3 = (s32[1]{0:T(128)}, s32[1]{0:T(128)}, u32[]{:S(2)}, u32[]{:S(2)}) collective-permute-start(s32[1]{0:T(128)} %collective-permute-done.2), channel_id=1, source_target_pairs={{32,98},{33,99},{34,96},{35,97},{36,102},{37,103},{38,100},{39,101... | collective-permute-start | bytes 20 | tf_op jit(solution)/shard_map/ppermute | solution.py:354
  52.7 1.2 collective-permute-done.3
  54.5 0.0 collective-permute-done.5.refs_3_
  54.5 0.0 collective-permute-done.4.refs_2_
  54.6 1.2 upper_level_to_rows.1
  55.8 0.0 copy-start.1
  55.8 26.7 %all_to_all.15.rows_ref.gain_ref = bf16[32,272,128]{2,1,0:T(8,128)(2,1)S(1)} all-to-all(bf16[32,272,128]{2,1,0:T(8,128)(2,1)S(1)} %bitcast.9), channel_id=1, replica_groups=mesh['hi'=4,'lo'=32] {'lo'}, dimensions={0} | all-to-all | bytes 4456448 | tf_op jit(solution)/shard_map/all_to_all | solution.py:356
  82.5 0.0 copy-done.1
  82.5 8.2 %box_order.1 = bf16[8192,128]{1,0:T(8,128)(2,1)S(1)} custom-call(s32[1,8192]{1,0:T(1,128)S(1)} %copy-done.1, bf16[32,272,128]{2,1,0:T(8,128)(2,1)S(1)} %all_to_all.15.rows_ref.gain_ref), custom_call_target="tpu_custom_call" | custom-call | bytes 31457280 | tf_op jit(solution)/shard_map/box_order/pallas_call | solution.py:196
  90.7 20.6 %all_to_all.16.x_ref = bf16[32,256,128]{2,1,0:T(8,128)(2,1)S(1)} all-to-all(bf16[32,256,128]{2,1,0:T(8,128)(2,1)S(1)} %bitcast.8), channel_id=1, replica_groups=mesh['hi'=4,'lo'=32] {'lo'}, dimensions={0} | all-to-all | bytes 4194304 | tf_op jit(solution)/shard_map/all_to_all | solution.py:358
  111.3 3.0 %lower_levels.1 = bf16[32,2,64,256]{3,2,1,0:T(8,128)(2,1)S(1)} custom-call(s32[1]{0:T(128)S(6)} %max.3.own_ref, bf16[32,256,128]{2,1,0:T(8,128)(2,1)S(1)} %all_to_all.16.x_ref, bf16[15,128,128]{2,1,0:T(8,128)(2,1)S(1)} %bitcast.17, bf16[32,272,128]{2,1,0:T(8,128)(2,1)S(1)} %all_to_all.15.rows_ref.gain_ref), custom_call_target="tpu_custom_call" | custom-call | flops 10737418240 | bytes 4194304 | tf_op jit(solution)/shard_map/lower_levels/pallas_call | solution.py:262
  114.3 0.0 copy-start.2
  114.3 21.3 %all_to_all.17.x_ref = bf16[16,2,2,64,256]{4,3,2,1,0:T(8,128)(2,1)S(1)} all-to-all(bf16[16,2,2,64,256]{4,3,2,1,0:T(8,128)(2,1)S(1)} %bitcast.10), channel_id=1, replica_groups={{0,1,2,3,4,5,6,7,8,9,10,11,12,13,14,15},{16,17,18,19,20,21,22,23,24,25,..., dimensions={0} | all-to-all | bytes 4194304 | tf_op jit(solution)/shard_map/all_to_all | solution.py:361
  135.7 0.0 copy-done.2
  135.7 4.9 %target_map.1 = bf16[2,256,8192]{2,1,0:T(8,128)(2,1)} custom-call(bf16[16,2,2,64,256]{4,3,2,1,0:T(8,128)(2,1)S(1)} %all_to_all.17.x_ref, bf16[64,256]{1,0:T(8,128)(2,1)S(1)} %bitcast.11, f32[15,8192]{1,0:T(8,128)S(1)} %copy-done), custom_call_target="tpu_custom_call" | custom-call | flops 2147483648 | bytes 8388608 | tf_op jit(solution)/shard_map/target_map/pallas_call | solution.py:292
  (4 shorter events, 0.0 us)
Async XLA Ops:
  6.4 16.4 %copy-start = (f32[15,8192]{1,0:T(8,128)S(1)}, f32[15,8192]{1,0:T(8,128)}, u32[]{:S(2)}) copy-start(f32[15,8192]{1,0:T(8,128)} %gain_ref.1) | copy-start | bytes 1474564
  6.4 16.4 %copy-start.3 = (bf16[15,2,64,128]{3,2,1,0:T(8,128)(2,1)S(1)}, bf16[15,2,64,128]{3,2,1,0:T(8,128)(2,1)}, u32[]{:S(2)}) copy-start(bf16[15,2,64,128]{3,2,1,0:T(8,128)(2,1)} %param.8) | copy-start | bytes 1474564
  6.4 16.4 %copy-start.5 = (bf16[64,4096]{1,0:T(8,128)(2,1)S(1)}, bf16[64,4096]{1,0:T(8,128)(2,1)}, u32[]{:S(2)}) copy-start(bf16[64,4096]{1,0:T(8,128)(2,1)} %get-tuple-element.19.kept_in) | copy-start | bytes 1572868
  6.4 16.4 %collective-permute-start = (bf16[64,4096]{1,0:T(8,128)(2,1)}, bf16[64,4096]{1,0:T(8,128)(2,1)S(1)}, u32[]{:S(2)}, u32[]{:S(2)}) collective-permute-start(bf16[64,4096]{1,0:T(8,128)(2,1)} %get-tuple-element.20), channel_id=1, source_target_pairs={{0,64},{32,96},{64,0},{96,32},{1,65},{33,97},{65,1},{97,33},{2,66}... | collective-permute-start | bytes 1572872 | tf_op jit(solution)/shard_map/ppermute | solution.py:329
  17.3 16.7 %copy-start.4 = (bf16[64,4096]{1,0:T(8,128)(2,1)S(1)}, bf16[64,4096]{1,0:T(8,128)(2,1)}, u32[]{:S(2)}) copy-start(bf16[64,4096]{1,0:T(8,128)(2,1)} %get-tuple-element.23.kept_in) | copy-start | bytes 1572868
  17.3 16.7 %collective-permute-start.1 = (bf16[64,4096]{1,0:T(8,128)(2,1)}, bf16[64,4096]{1,0:T(8,128)(2,1)S(1)}, u32[]{:S(2)}, u32[]{:S(2)}) collective-permute-start(bf16[64,4096]{1,0:T(8,128)(2,1)} %get-tuple-element.24), channel_id=1, source_target_pairs={{0,64},{32,96},{64,0},{96,32},{1,65},{33,97},{65,1},{97,33},{2,66}... | collective-permute-start | bytes 1572872 | tf_op jit(solution)/shard_map/ppermute | solution.py:329
  35.0 19.6 %collective-permute-start.5 = (bf16[64,4096]{1,0:T(8,128)(2,1)S(1)}, bf16[64,4096]{1,0:T(8,128)(2,1)S(1)}, u32[]{:S(2)}, u32[]{:S(2)}) collective-permute-start(bf16[64,4096]{1,0:T(8,128)(2,1)S(1)} %get-tuple-element.30), channel_id=1, source_target_pairs={{0,32},{32,0},{64,96},{96,64},{1,33},{33,1},{65,97},{97,65},{2,34}... | collective-permute-start | bytes 1572872 | tf_op jit(solution)/shard_map/ppermute | solution.py:338
  36.3 18.3 %collective-permute-start.4 = (bf16[64,4096]{1,0:T(8,128)(2,1)S(1)}, bf16[64,4096]{1,0:T(8,128)(2,1)S(1)}, u32[]{:S(2)}, u32[]{:S(2)}) collective-permute-start(bf16[64,4096]{1,0:T(8,128)(2,1)S(1)} %get-tuple-element.29), channel_id=1, source_target_pairs={{0,32},{32,0},{64,96},{96,64},{1,33},{33,1},{65,97},{97,65},{2,34}... | collective-permute-start | bytes 1572872 | tf_op jit(solution)/shard_map/ppermute | solution.py:338
  36.4 9.2 %collective-permute-start.2 = (s32[1]{0:T(128)}, s32[1]{0:T(128)}, u32[]{:S(2)}, u32[]{:S(2)}) collective-permute-start(s32[1]{0:T(128)} %bitcast), channel_id=1, source_target_pairs={{32,106},{33,107},{34,104},{35,105},{36,110},{37,111},{38,108},{39... | collective-permute-start | bytes 20 | tf_op jit(solution)/shard_map/ppermute | solution.py:354
  45.6 8.3 %collective-permute-start.3 = (s32[1]{0:T(128)}, s32[1]{0:T(128)}, u32[]{:S(2)}, u32[]{:S(2)}) collective-permute-start(s32[1]{0:T(128)} %collective-permute-done.2), channel_id=1, source_target_pairs={{32,98},{33,99},{34,96},{35,97},{36,102},{37,103},{38,100},{39,101... | collective-permute-start | bytes 20 | tf_op jit(solution)/shard_map/ppermute | solution.py:354
  55.8 26.7 %copy-start.1 = (s32[1,8192]{1,0:T(1,128)S(1)}, s32[1,8192]{1,0:T(1,128)}, u32[]{:S(2)}) copy-start(s32[1,8192]{1,0:T(1,128)} %order_ref.1) | copy-start | bytes 98308
  114.3 21.4 %copy-start.2 = (bf16[256,64]{0,1:T(8,128)(2,1)S(1)}, bf16[256,64]{0,1:T(8,128)(2,1)}, u32[]{:S(2)}) copy-start(bf16[256,64]{0,1:T(8,128)(2,1)} %param.11) | copy-start | bytes 98308

commit v7 on v6

--- a/solution.py
+++ b/solution.py
@@ -179,7 +179,7 @@
         table[pl.ds(pl.multiple_of(i * chunk, chunk), chunk), :] = rows_ref[i, :chunk, :].astype(F32)
         return carry
 
-    lax.fori_loop(0, pieces, widen, 0)
+    lax.fori_loop(0, pieces, widen, 0, unroll=4)
 
     def move(i, carry):
         base = pl.multiple_of(i * UNROLL, UNROLL)

time: 141 us -> 141 us (level)
  no operation moved by 1% of the time
where the time goes in v7:
time: 141 us; the launch traced here: 140 us
  blocking collectives  68.7 us (49%)
  Pallas kernels  31.9 us (23%)
  starting transfers between devices  22.2 us (16%)
  waiting for transfers between devices  16.9 us (12%)
    all_to_all x1, blocking collectives, body(): lax.all_to_all(rows.reshape(n_lower, piece + extra, images * ranks), 'lo'...  26.7 us
    all_to_all x1, blocking collectives, body(): blocks = lax.all_to_all(blocks, 'lo', 0, 0, axis_index_groups=groups)  21.3 us
    all_to_all x1, blocking collectives, body(): lax.all_to_all(rows.reshape(n_lower, piece, images * ranks), 'lo', 0, 0)  20.6 us
    ppermute x2, starting transfers between devices, body(): turn = lax.ppermute(turn, ('hi', 'lo'), pairs)  16.2 us
    ppermute x2, waiting for transfers between devices, body(): received[at] = lax.ppermute(sent, 'hi', [(i, i ^ 2) for i in range(4)])  15.5 us
    pallas_call x2, Pallas kernels, front(): pl.pallas_call(functools.partial(front_kernel, LOCAL_LEVELS), grid_spec=g...  12.7 us
    pallas_call x1, Pallas kernels, gather_rows(): pl.pallas_call(gather_kernel, in_specs=[pl.BlockSpec(memory_space=pltpu.S...  8.12 us
    pallas_call x1, Pallas kernels, to_targets(): pl.pallas_call(functools.partial(target_kernel, box_gain.shape[0] - 1), g...  4.88 us
  transfers between devices with their start and end apart: 6, of which 4 were waited for; matrix products, arithmetic and copies ran while one was open for 0% of the time, Pallas kernels for 5%

profile of v7, /device:TPU:1, one launch (start us, length us, event | category | flops | bytes accessed | tf_op | source)
XLA Modules:
  0.0 140.5 jit_solution(1850220168923675178)
XLA Ops:
  0.0 6.4 %source_map_and_local_levels.2 = (bf16[64,4096]{1,0:T(8,128)(2,1)}, bf16[64,4096]{1,0:T(8,128)(2,1)}) custom-call(s32[1]{0:T(128)} %bitcast.1.own_ref, bf16[2,256,8192]{2,1,0:T(8,128)(2,1)} %high_ref.3, bf16[2,256,8192]{2,1,0:T(8,128)(2,1)} %high_ref.3, bf16[64,256]{1,0:T(8,128)(2,1)} %map_ref.3, bf16[15,128,128]{2,1,0:T(8,128)(2,1)} %bitcast.12, ...), custom_call_target="tpu_custom_call" | custom-call | flops 10737418240 | bytes 4194304 | tf_op jit(solution)/shard_map/source_map_and_local_levels/pallas_call | solution.py:72
  6.4 4.5 %collective-permute-start = (bf16[64,4096]{1,0:T(8,128)(2,1)}, bf16[64,4096]{1,0:T(8,128)(2,1)S(1)}, u32[]{:S(2)}, u32[]{:S(2)}) collective-permute-start(bf16[64,4096]{1,0:T(8,128)(2,1)} %get-tuple-element.20), channel_id=1, source_target_pairs={{0,64},{32,96},{64,0},{96,32},{1,65},{33,97},{65,1},{97,33},{2,66}... | collective-permute-start | bytes 1572872 | tf_op jit(solution)/shard_map/ppermute | solution.py:329
  10.9 6.4 %source_map_and_local_levels.3 = (bf16[64,4096]{1,0:T(8,128)(2,1)}, bf16[64,4096]{1,0:T(8,128)(2,1)}) custom-call(s32[1]{0:T(128)} %bitcast.1.own_ref, bf16[2,256,8192]{2,1,0:T(8,128)(2,1)} %high_ref.3, bf16[2,256,8192]{2,1,0:T(8,128)(2,1)} %high_ref.3, bf16[64,256]{1,0:T(8,128)(2,1)} %map_ref.3, bf16[15,128,128]{2,1,0:T(8,128)(2,1)} %bitcast.13, ...), custom_call_target="tpu_custom_call" | custom-call | flops 10737418240 | bytes 4194304 | tf_op jit(solution)/shard_map/source_map_and_local_levels/pallas_call | solution.py:72
  17.3 0.1 collective-permute-start.1
  17.4 0.1 pad_add_fusion.own_ref
  17.5 5.3 %collective-permute-done.recv_in = bf16[64,4096]{1,0:T(8,128)(2,1)S(1)} collective-permute-done((bf16[64,4096]{1,0:T(8,128)(2,1)}, bf16[64,4096]{1,0:T(8,128)(2,1)S(1)}, u32[]{:S(2)}, u32[]{:S(2)}) %collective-permute-start) | collective-permute-done | bytes 524320 | tf_op jit(solution)/shard_map/ppermute | solution.py:329
  22.7 0.0 copy-done
  22.7 0.0 copy-done.3
  22.7 0.0 copy-done.5
  22.7 1.0 upper_level.2
  23.7 10.2 %collective-permute-done.1.recv_in = bf16[64,4096]{1,0:T(8,128)(2,1)S(1)} collective-permute-done((bf16[64,4096]{1,0:T(8,128)(2,1)}, bf16[64,4096]{1,0:T(8,128)(2,1)S(1)}, u32[]{:S(2)}, u32[]{:S(2)}) %collective-permute-start.1) | collective-permute-done | bytes 524320 | tf_op jit(solution)/shard_map/ppermute | solution.py:329
  34.0 0.0 copy-done.4
  34.0 1.0 upper_level.3
  35.0 1.3 collective-permute-start.5
  36.3 0.1 collective-permute-start.4
  36.4 9.0 %collective-permute-start.2 = (s32[1]{0:T(128)}, s32[1]{0:T(128)}, u32[]{:S(2)}, u32[]{:S(2)}) collective-permute-start(s32[1]{0:T(128)} %bitcast), channel_id=1, source_target_pairs={{32,106},{33,107},{34,104},{35,105},{36,110},{37,111},{38,108},{39... | collective-permute-start | bytes 20 | tf_op jit(solution)/shard_map/ppermute | solution.py:354
  45.4 0.2 collective-permute-done.2
  45.6 7.1 %collective-permute-start.3 = (s32[1]{0:T(128)}, s32[1]{0:T(128)}, u32[]{:S(2)}, u32[]{:S(2)}) collective-permute-start(s32[1]{0:T(128)} %collective-permute-done.2), channel_id=1, source_target_pairs={{32,98},{33,99},{34,96},{35,97},{36,102},{37,103},{38,100},{39,101... | collective-permute-start | bytes 20 | tf_op jit(solution)/shard_map/ppermute | solution.py:354
  52.7 1.2 collective-permute-done.3
  54.5 0.0 collective-permute-done.5.refs_3_
  54.5 0.0 collective-permute-done.4.refs_2_
  54.6 1.2 upper_level_to_rows.1
  55.8 0.0 copy-start.1
  55.8 26.7 %all_to_all.15.rows_ref.gain_ref = bf16[32,272,128]{2,1,0:T(8,128)(2,1)S(1)} all-to-all(bf16[32,272,128]{2,1,0:T(8,128)(2,1)S(1)} %bitcast.9), channel_id=1, replica_groups=mesh['hi'=4,'lo'=32] {'lo'}, dimensions={0} | all-to-all | bytes 4456448 | tf_op jit(solution)/shard_map/all_to_all | solution.py:356
  82.5 0.0 copy-done.1
  82.5 8.1 %box_order.1 = bf16[8192,128]{1,0:T(8,128)(2,1)S(1)} custom-call(s32[1,8192]{1,0:T(1,128)S(1)} %copy-done.1, bf16[32,272,128]{2,1,0:T(8,128)(2,1)S(1)} %all_to_all.15.rows_ref.gain_ref), custom_call_target="tpu_custom_call" | custom-call | bytes 31457280 | tf_op jit(solution)/shard_map/box_order/pallas_call | solution.py:196
  90.6 20.6 %all_to_all.16.x_ref = bf16[32,256,128]{2,1,0:T(8,128)(2,1)S(1)} all-to-all(bf16[32,256,128]{2,1,0:T(8,128)(2,1)S(1)} %bitcast.8), channel_id=1, replica_groups=mesh['hi'=4,'lo'=32] {'lo'}, dimensions={0} | all-to-all | bytes 4194304 | tf_op jit(solution)/shard_map/all_to_all | solution.py:358
  111.3 3.0 %lower_levels.1 = bf16[32,2,64,256]{3,2,1,0:T(8,128)(2,1)S(1)} custom-call(s32[1]{0:T(128)S(6)} %max.3.own_ref, bf16[32,256,128]{2,1,0:T(8,128)(2,1)S(1)} %all_to_all.16.x_ref, bf16[15,128,128]{2,1,0:T(8,128)(2,1)S(1)} %bitcast.17, bf16[32,272,128]{2,1,0:T(8,128)(2,1)S(1)} %all_to_all.15.rows_ref.gain_ref), custom_call_target="tpu_custom_call" | custom-call | flops 10737418240 | bytes 4194304 | tf_op jit(solution)/shard_map/lower_levels/pallas_call | solution.py:262
  114.2 0.0 copy-start.2
  114.3 21.3 %all_to_all.17.x_ref = bf16[16,2,2,64,256]{4,3,2,1,0:T(8,128)(2,1)S(1)} all-to-all(bf16[16,2,2,64,256]{4,3,2,1,0:T(8,128)(2,1)S(1)} %bitcast.10), channel_id=1, replica_groups={{0,1,2,3,4,5,6,7,8,9,10,11,12,13,14,15},{16,17,18,19,20,21,22,23,24,25,..., dimensions={0} | all-to-all | bytes 4194304 | tf_op jit(solution)/shard_map/all_to_all | solution.py:361
  135.6 0.0 copy-done.2
  135.6 4.9 %target_map.1 = bf16[2,256,8192]{2,1,0:T(8,128)(2,1)} custom-call(bf16[16,2,2,64,256]{4,3,2,1,0:T(8,128)(2,1)S(1)} %all_to_all.17.x_ref, bf16[64,256]{1,0:T(8,128)(2,1)S(1)} %bitcast.11, f32[15,8192]{1,0:T(8,128)S(1)} %copy-done), custom_call_target="tpu_custom_call" | custom-call | flops 2147483648 | bytes 8388608 | tf_op jit(solution)/shard_map/target_map/pallas_call | solution.py:292
  (4 shorter events, 0.0 us)
Async XLA Ops:
  6.4 16.4 %copy-start = (f32[15,8192]{1,0:T(8,128)S(1)}, f32[15,8192]{1,0:T(8,128)}, u32[]{:S(2)}) copy-start(f32[15,8192]{1,0:T(8,128)} %gain_ref.1) | copy-start | bytes 1474564
  6.4 16.4 %copy-start.3 = (bf16[15,2,64,128]{3,2,1,0:T(8,128)(2,1)S(1)}, bf16[15,2,64,128]{3,2,1,0:T(8,128)(2,1)}, u32[]{:S(2)}) copy-start(bf16[15,2,64,128]{3,2,1,0:T(8,128)(2,1)} %param.8) | copy-start | bytes 1474564
  6.4 16.4 %copy-start.5 = (bf16[64,4096]{1,0:T(8,128)(2,1)S(1)}, bf16[64,4096]{1,0:T(8,128)(2,1)}, u32[]{:S(2)}) copy-start(bf16[64,4096]{1,0:T(8,128)(2,1)} %get-tuple-element.19.kept_in) | copy-start | bytes 1572868
  6.4 16.4 %collective-permute-start = (bf16[64,4096]{1,0:T(8,128)(2,1)}, bf16[64,4096]{1,0:T(8,128)(2,1)S(1)}, u32[]{:S(2)}, u32[]{:S(2)}) collective-permute-start(bf16[64,4096]{1,0:T(8,128)(2,1)} %get-tuple-element.20), channel_id=1, source_target_pairs={{0,64},{32,96},{64,0},{96,32},{1,65},{33,97},{65,1},{97,33},{2,66}... | collective-permute-start | bytes 1572872 | tf_op jit(solution)/shard_map/ppermute | solution.py:329
  17.3 16.7 %copy-start.4 = (bf16[64,4096]{1,0:T(8,128)(2,1)S(1)}, bf16[64,4096]{1,0:T(8,128)(2,1)}, u32[]{:S(2)}) copy-start(bf16[64,4096]{1,0:T(8,128)(2,1)} %get-tuple-element.23.kept_in) | copy-start | bytes 1572868
  17.3 16.7 %collective-permute-start.1 = (bf16[64,4096]{1,0:T(8,128)(2,1)}, bf16[64,4096]{1,0:T(8,128)(2,1)S(1)}, u32[]{:S(2)}, u32[]{:S(2)}) collective-permute-start(bf16[64,4096]{1,0:T(8,128)(2,1)} %get-tuple-element.24), channel_id=1, source_target_pairs={{0,64},{32,96},{64,0},{96,32},{1,65},{33,97},{65,1},{97,33},{2,66}... | collective-permute-start | bytes 1572872 | tf_op jit(solution)/shard_map/ppermute | solution.py:329
  35.0 19.6 %collective-permute-start.5 = (bf16[64,4096]{1,0:T(8,128)(2,1)S(1)}, bf16[64,4096]{1,0:T(8,128)(2,1)S(1)}, u32[]{:S(2)}, u32[]{:S(2)}) collective-permute-start(bf16[64,4096]{1,0:T(8,128)(2,1)S(1)} %get-tuple-element.30), channel_id=1, source_target_pairs={{0,32},{32,0},{64,96},{96,64},{1,33},{33,1},{65,97},{97,65},{2,34}... | collective-permute-start | bytes 1572872 | tf_op jit(solution)/shard_map/ppermute | solution.py:338
  36.3 18.3 %collective-permute-start.4 = (bf16[64,4096]{1,0:T(8,128)(2,1)S(1)}, bf16[64,4096]{1,0:T(8,128)(2,1)S(1)}, u32[]{:S(2)}, u32[]{:S(2)}) collective-permute-start(bf16[64,4096]{1,0:T(8,128)(2,1)S(1)} %get-tuple-element.29), channel_id=1, source_target_pairs={{0,32},{32,0},{64,96},{96,64},{1,33},{33,1},{65,97},{97,65},{2,34}... | collective-permute-start | bytes 1572872 | tf_op jit(solution)/shard_map/ppermute | solution.py:338
  36.4 9.2 %collective-permute-start.2 = (s32[1]{0:T(128)}, s32[1]{0:T(128)}, u32[]{:S(2)}, u32[]{:S(2)}) collective-permute-start(s32[1]{0:T(128)} %bitcast), channel_id=1, source_target_pairs={{32,106},{33,107},{34,104},{35,105},{36,110},{37,111},{38,108},{39... | collective-permute-start | bytes 20 | tf_op jit(solution)/shard_map/ppermute | solution.py:354
  45.6 8.3 %collective-permute-start.3 = (s32[1]{0:T(128)}, s32[1]{0:T(128)}, u32[]{:S(2)}, u32[]{:S(2)}) collective-permute-start(s32[1]{0:T(128)} %collective-permute-done.2), channel_id=1, source_target_pairs={{32,98},{33,99},{34,96},{35,97},{36,102},{37,103},{38,100},{39,101... | collective-permute-start | bytes 20 | tf_op jit(solution)/shard_map/ppermute | solution.py:354
  55.8 26.7 %copy-start.1 = (s32[1,8192]{1,0:T(1,128)S(1)}, s32[1,8192]{1,0:T(1,128)}, u32[]{:S(2)}) copy-start(s32[1,8192]{1,0:T(1,128)} %order_ref.1) | copy-start | bytes 98308
  114.2 21.4 %copy-start.2 = (bf16[256,64]{0,1:T(8,128)(2,1)S(1)}, bf16[256,64]{0,1:T(8,128)(2,1)}, u32[]{:S(2)}) copy-start(bf16[256,64]{0,1:T(8,128)(2,1)} %param.11) | copy-start | bytes 98308
